TPU v7x, 32 devices: a whole 2x2x4 slice. The times are simulated.
32 devices in a mesh: seq: 4 (over y, x), zero: 8 (over z, core).
Axes of the slice: x: 2, y: 2, z: 4, core: 2. Of those that a mesh axis runs over, the one named last changes fastest.
Arguments:
- q_proj: bfloat16 [8, 1024, 2560], P('zero', 'seq'), as said below
- k_proj: bfloat16 [8, 1024, 2560], P('zero', 'seq'), as said below
- v_proj: bfloat16 [8, 1024, 2560], P('zero', 'seq'), may hold values from -6 to 6
- neighbours: int32 [8, 8, 4], P('zero'), may hold values from 0 to 7, as said below
- counts: int32 [8, 8], P('zero'), may hold values from 1 to 4
- w_out: bfloat16 [2560, 5120], P(('seq', 'zero')), may hold values from -0.125 to 0.125
- d_out: bfloat16 [8, 1024, 5120], P('zero', 'seq'), may hold values from -6 to 6
Outputs:
- out_y: bfloat16 [8, 1024, 5120], P('zero', 'seq')
- grad_q: bfloat16 [8, 1024, 2560], P('zero', 'seq')
- grad_k: bfloat16 [8, 1024, 2560], P('zero', 'seq')
- grad_v: bfloat16 [8, 1024, 2560], P('zero', 'seq')
- grad_w: float32 [2560, 5120], P(('seq', 'zero'))
Inputs may be any that keep to these rules, and one draw needn't show every extreme that they name: Entries of q_proj lie within -16 and 16. Entries of k_proj lie within -16 and 16. `neighbours`: for each clip and block the 4 entries are distinct block numbers of that clip, the first being the block itself.
All inputs are finite; a program needn't handle non-finite values.
Results may differ from a plain program's by a relative error of at most 0.018.
Values may be sent and summed in bfloat16 or wider, within the bound.
No kernel may reach another device: no remote copies, remote signals or barrier semaphores. Data moves between devices by JAX's collectives and lax.ppermute only.
A program may use at most 192 MiB of HBM per device.

v0:
```python
import functools
import math

import jax
import jax.numpy as jnp
from jax import lax
from jax.experimental import pallas as pl
from jax.experimental.pallas import tpu as pltpu
from jax.sharding import PartitionSpec as P

HD = 128
BLK = 128
MB = 1 << 20
BF = jnp.bfloat16
COST = pl.CostEstimate(flops=1024, bytes_accessed=1024, transcendentals=0)
LONG = pl.CostEstimate(flops=1024, bytes_accessed=1024, transcendentals=0)
F32 = jnp.float32


ANY = pl.BlockSpec(memory_space=pl.ANY)
SMEM = pl.BlockSpec(memory_space=pltpu.SMEM)


def params(mb):
    return pltpu.CompilerParams(vmem_limit_bytes=mb * MB)


def sds(shape, dtype=BF):
    return jax.ShapeDtypeStruct(shape, dtype)


def run_copies(copies):
    for c in copies:
        c.start()
    for c in copies:
        c.wait()


def staged(moves, *rest):
    held, sem_in, sem_out = rest[:-2], rest[-2], rest[-1]
    ins = [pltpu.make_async_copy(a, h, sem_in.at[i]) for i, ((a, _), h) in enumerate(zip(moves, held))]
    outs = [pltpu.make_async_copy(h, b, sem_out.at[i]) for i, ((_, b), h) in enumerate(zip(moves, held))]
    for c in ins:
        c.start()
    for c, o in zip(ins, outs):
        c.wait()
        o.start()
    for o in outs:
        o.wait()


def pack_kernel(q_ref, k_ref, v_ref, out_ref, *rest):
    n, _, _, width = out_ref.shape
    moves = [
        (src.at[0, :, pl.ds(g * width, width)], out_ref.at[g, t])
        for g in range(n)
        for t, src in enumerate((q_ref, k_ref, v_ref))
    ]
    staged(moves, *rest)


def pack(q, k, v, n):
    rows, cols = q.shape[1:]
    width = cols // n
    return pl.pallas_call(
        pack_kernel,
        out_shape=sds((n, 3, rows, width)),
        in_specs=[ANY, ANY, ANY],
        out_specs=ANY,
        scratch_shapes=[pltpu.VMEM((rows, width), BF)] * (3 * n)
        + [pltpu.SemaphoreType.DMA((3 * n,))] * 2,
        compiler_params=params(60),
        cost_estimate=COST,
        name="pack",
    )(q, k, v)


def unpack_kernel(n, width, cuts, me_ref, *rest):
    m = n * len(cuts)
    parts, outs = rest[:m], rest[m : m + 3]
    moves = []
    for i, part in enumerate(parts):
        col = pl.multiple_of((me_ref[0] ^ (i % n)) * width + cuts[i // n], 128)
        for t in range(3):
            moves.append((part.at[t], outs[t].at[0, :, pl.ds(col, part.shape[2])]))
    staged(moves, *rest[m + 3 :])


def unpack(me, chunks):
    n = len(chunks[0])
    cuts = [sum(c[0].shape[2] for c in chunks[:i]) for i in range(len(chunks))]
    width = sum(c[0].shape[2] for c in chunks)
    rows = chunks[0][0].shape[1]
    parts = [x for c in chunks for x in c]
    return pl.pallas_call(
        functools.partial(unpack_kernel, n, width, cuts),
        out_shape=[sds((1, rows, n * width))] * 3,
        in_specs=[SMEM] + [ANY] * len(parts),
        out_specs=[ANY] * 3,
        scratch_shapes=[pltpu.VMEM(x.shape[1:], BF) for x in parts for _ in range(3)]
        + [pltpu.SemaphoreType.DMA((3 * len(parts),))] * 2,
        compiler_params=params(60),
        cost_estimate=LONG,
        name="unpack",
    )(me, *parts)


def join_kernel(width, low_ref, *rest):
    m = (len(rest) - 3) // 2
    parts, out = rest[:m], rest[m]
    moves, col = [], 0
    for i, part in enumerate(parts):
        if i == m // 2:
            col = 0
        side = low_ref[0] if i < m // 2 else 1 - low_ref[0]
        start = pl.multiple_of(side * width + col, 128)
        col += part.shape[1]
        moves.append((part, out.at[0, :, pl.ds(start, part.shape[1])]))
    staged(moves, *rest[m + 1 :])


def join(low, own, pair):
    parts = own + pair
    rows = parts[0].shape[0]
    width = sum(x.shape[1] for x in own)
    return pl.pallas_call(
        functools.partial(join_kernel, width),
        out_shape=sds((1, rows, 2 * width)),
        in_specs=[SMEM] + [ANY] * len(parts),
        out_specs=ANY,
        scratch_shapes=[pltpu.VMEM(x.shape, BF) for x in parts]
        + [pltpu.SemaphoreType.DMA((len(parts),))] * 2,
        compiler_params=params(60),
        cost_estimate=LONG,
        name="join",
    )(low, *parts)


def place(block, me, per):
    return pl.multiple_of((((block // per) ^ me) * per + block % per) * BLK, BLK)


NT = (((1,), (1,)), ((), ()))
TN = (((0,), (0,)), ((), ()))


def dot(a, b, dims=(((1,), (0,)), ((), ()))):
    return lax.dot_general(a, b, dims, preferred_element_type=F32)


def soft_of(scores, axis):
    expo = jnp.exp(scores - jnp.max(scores, axis=axis, keepdims=True))
    return expo * (1.0 / jnp.sum(expo, axis=axis, keepdims=True))


def for_blocks(blocks, slots, nbr_ref, cnt_ref, body):
    def block(b, _):
        for count in range(1, slots + 1):

            @pl.when(cnt_ref[0, b] == count)
            def _():
                body(b, [nbr_ref[0, b, j] for j in range(count)])

        return 0

    lax.fori_loop(0, blocks, block, 0)


def gather(held, t, keys, per, out):
    for j, e in enumerate(keys):
        rows = pl.ds(pl.multiple_of(e % per * BLK, BLK), BLK)
        out[j * BLK : (j + 1) * BLK] = held[e // per, t, rows]


def fwd_kernel(heads, slots, scale, me_ref, nbr_ref, cnt_ref, held, attn_ref, swap_ref, ks, vs):
    me = me_ref[0]
    n, per = held.shape[0], held.shape[2] // BLK

    def body(b, keys):
        here, there = place(b, me, per), place(b, me ^ 1, per)
        rows = pl.ds(pl.multiple_of(b % per * BLK, BLK), BLK)
        gather(held, 1, keys, per, ks)
        gather(held, 2, keys, per, vs)
        used = slice(0, len(keys) * BLK)
        cols = [slice(h * HD, (h + 1) * HD) for h in range(heads)]
        scores = [dot(held[b // per, 0, rows, c], ks[used, c], NT) * scale for c in cols]
        probs = [soft_of(x, 1).astype(BF) for x in scores]
        for c, p in zip(cols, probs):
            out = dot(p, vs[used, c]).astype(BF)
            attn_ref[pl.ds(here, BLK), c] = out
            swap_ref[pl.ds(there, BLK), c] = out

    for_blocks(n * per, slots, nbr_ref, cnt_ref, body)


def attend(me, nbr, cnt, got, scale):
    n, _, rows, width = got.shape
    vm = pl.BlockSpec(memory_space=pltpu.VMEM)
    return pl.pallas_call(
        functools.partial(fwd_kernel, width // HD, nbr.shape[2], scale),
        out_shape=[sds((n * rows, width))] * 2,
        in_specs=[SMEM] * 3 + [vm],
        out_specs=[vm, vm],
        scratch_shapes=[pltpu.VMEM((nbr.shape[2] * BLK, width), BF)] * 2,
        compiler_params=params(60),
        cost_estimate=COST,
        name="attend",
    )(me, nbr, cnt, got)


def bwd_kernel(begin, slots, scale, me_ref, nbr_ref, cnt_ref, got_ref, *rest):
    d_refs, outs, (held, terms, dq, dk, dv, ks, vs, sem, d_sem) = rest[:4], rest[4:-9], rest[-9:]
    me = me_ref[0]
    n, _, rows, some = held.shape
    per = rows // BLK
    cols = pl.ds(begin, some)
    copies = [pltpu.make_async_copy(got_ref.at[:, :, :, cols], held, sem)]
    for i, ref in enumerate(d_refs):
        part = pl.ds(i % 2 * ref.shape[0], ref.shape[0])
        copies.append(
            pltpu.make_async_copy(ref.at[:, cols], terms.at[i // 2, part], d_sem.at[i])
        )
    for c in copies:
        c.start()
    dk[...] = jnp.zeros_like(dk)
    dv[...] = jnp.zeros_like(dv)
    for c in copies:
        c.wait()

    def body(b, keys):
        here = pl.ds(place(b, me, per), BLK)
        rows_b = pl.ds(pl.multiple_of(b % per * BLK, BLK), BLK)
        gather(held, 1, keys, per, ks)
        gather(held, 2, keys, per, vs)
        used = slice(0, len(keys) * BLK)
        heads = [slice(h * HD, (h + 1) * HD) for h in range(some // HD)]
        qs = [held[b // per, 0, rows_b, c] for c in heads]
        ds = [
            (terms[0, here, c].astype(F32) + terms[1, here, c].astype(F32)).astype(BF)
            for c in heads
        ]
        softs = [soft_of(dot(ks[used, c], q, NT) * scale, 0) for c, q in zip(heads, qs)]
        dps = [dot(vs[used, c], d, NT) for c, d in zip(heads, ds)]
        dss = [
            (s * (p - jnp.sum(s * p, axis=0, keepdims=True))).astype(BF)
            for s, p in zip(softs, dps)
        ]
        for c, q, d, s, x in zip(heads, qs, ds, softs, dss):
            dq[b // per, rows_b, c] = (dot(x, ks[used, c], TN) * scale).astype(BF)
            to_v, to_k = dot(s.astype(BF), d), dot(x, q)
            for j, e in enumerate(keys):
                rows_e = pl.ds(pl.multiple_of(e * BLK, BLK), BLK)
                dv[rows_e, c] += to_v[j * BLK : (j + 1) * BLK]
                dk[rows_e, c] += to_k[j * BLK : (j + 1) * BLK]

    for_blocks(n * per, slots, nbr_ref, cnt_ref, body)
    for r, out in enumerate(outs):
        g = me ^ r
        rows_g = pl.ds(pl.multiple_of(g * rows, BLK), rows)
        out[0] = dq[g]
        out[1] = (dk[rows_g] * scale).astype(BF)
        out[2] = dv[rows_g].astype(BF)


def attend_back(me, nbr, cnt, got, terms, begin, end, scale):
    n, _, rows, _ = got.shape
    some = end - begin
    vm = pl.BlockSpec(memory_space=pltpu.VMEM)
    return pl.pallas_call(
        functools.partial(bwd_kernel, begin, nbr.shape[2], scale),
        out_shape=[sds((3, rows, some))] * n,
        in_specs=[SMEM] * 3 + [ANY] * 5,
        out_specs=[vm] * n,
        scratch_shapes=[
            pltpu.VMEM((n, 3, rows, some), BF),
            pltpu.VMEM((2, n * rows, some), BF),
            pltpu.VMEM((n, rows, some), BF),
            pltpu.VMEM((n * rows, some), F32),
            pltpu.VMEM((n * rows, some), F32),
            pltpu.VMEM((nbr.shape[2] * BLK, some), BF),
            pltpu.VMEM((nbr.shape[2] * BLK, some), BF),
            pltpu.SemaphoreType.DMA,
            pltpu.SemaphoreType.DMA((4,)),
        ],
        compiler_params=params(60),
        cost_estimate=COST,
        name="attend_back",
    )(me, nbr, cnt, got, *terms)


def project_kernel(a_ref, b_ref, wa_ref, wb_ref, *rest):
    y = dot(a_ref[...], wa_ref[...]) + dot(b_ref[...], wb_ref[...])
    if len(rest) == 1:
        rest[0][...] = y.astype(BF)
        return
    far_ref, own_ref, pair_ref = rest
    y = (y + far_ref[...].astype(F32)).astype(BF)
    rows = own_ref.shape[0]
    own_ref[...] = y[:rows]
    pair_ref[...] = y[rows:]


def project(a, b, wa, wb, part, parts, far=None, tile=640):
    rows, depth = a.shape
    rows //= 2
    cols = wa.shape[1] // parts
    skip = part * (cols // tile)
    near = far is not None
    left = pl.BlockSpec((rows, depth), lambda j: (0 if near else 1, 0))
    right = pl.BlockSpec((depth, tile), lambda j: (0, skip + j))
    out = rows // 2 if near else rows
    return pl.pallas_call(
        project_kernel,
        grid=(cols // tile,),
        out_shape=[sds((out, cols))] * (2 if near else 1),
        in_specs=[left, left, right, right]
        + [pl.BlockSpec((rows, tile), lambda j: (0, j))] * int(near),
        out_specs=[pl.BlockSpec((out, tile), lambda j: (0, j))] * (2 if near else 1),
        compiler_params=params(60),
        cost_estimate=LONG if near else COST,
        name="project",
    )(a, b, wa, wb, *([far] if near else []))


def project_back_kernel(n, m, order, *refs):
    d_refs, w_refs, o_refs = refs[:n], refs[n : n + m], refs[n + m : n + 2 * m]
    held_d, held_w, sem = refs[n + 2 * m :]
    rows = d_refs[0].shape[0]
    copies = [
        pltpu.make_async_copy(d, held_d.at[pl.ds(i * rows, rows)], sem.at[i])
        for i, d in enumerate(d_refs)
    ] + [pltpu.make_async_copy(w, held_w.at[i], sem.at[n + i]) for i, w in enumerate(w_refs)]
    for c in copies:
        c.start()
    for c in copies[: n + 1]:
        c.wait()
    for i in range(m):
        if i:
            copies[n + i].wait()
        out = dot(held_d[...], held_w[i], NT).astype(BF)
        for r in range(n):
            there = r ^ 1 if order[i] else r
            o_refs[i][there * rows : (there + 1) * rows] = out[r * rows : (r + 1) * rows]


def project_back(ds, ws, order):
    n, m = len(ds), len(ws)
    rows, cols = ds[0].shape
    width = ws[0].shape[0]
    vm = pl.BlockSpec(memory_space=pltpu.VMEM)
    return pl.pallas_call(
        functools.partial(project_back_kernel, n, m, order),
        out_shape=[sds((n * rows, width))] * m,
        in_specs=[ANY] * (n + m),
        out_specs=[vm] * m,
        scratch_shapes=[
            pltpu.VMEM((n * rows, cols), BF),
            pltpu.VMEM((m, width, cols), BF),
            pltpu.SemaphoreType.DMA((n + m,)),
        ],
        compiler_params=params(60),
        cost_estimate=COST,
        name="project_back",
    )(*ds, *ws)


def weight_kernel(n, a_ref, b_ref, *refs):
    ds, o_ref, at, bt, d = refs[:n], refs[n], refs[n + 1], refs[n + 2], refs[n + 3]
    rows = ds[0].shape[0]

    @pl.when(pl.program_id(0) == 0)
    def _():
        at[...] = a_ref[...].T
        bt[...] = b_ref[...].T

    for r, piece in enumerate(ds):
        d[r * rows : (r + 1) * rows] = piece[...]
    for i, t in enumerate((at, bt)):
        out = dot(t[...], d[...]).astype(BF)
        o_ref[:, i] = out.reshape(o_ref.shape[0], *o_ref.shape[2:])


def weight_grad(a, b, ds, owners, tile=512):
    n = len(ds)
    tokens, width = a.shape
    rows, cols = ds[0].shape
    some = width // owners
    apart = owners if some % 16 == 0 else 1
    whole = pl.BlockSpec((tokens, width), lambda j: (0, 0))
    out = pl.pallas_call(
        functools.partial(weight_kernel, n),
        grid=(cols // tile,),
        out_shape=sds((apart, 2, width // apart, cols)),
        in_specs=[whole, whole] + [pl.BlockSpec((rows, tile), lambda j: (0, j))] * n,
        out_specs=pl.BlockSpec((apart, 2, width // apart, tile), lambda j: (0, 0, 0, j)),
        scratch_shapes=[pltpu.VMEM((width, tokens), BF)] * 2 + [pltpu.VMEM((tokens, tile), BF)],
        compiler_params=params(60),
        cost_estimate=COST,
        name="weight_grad",
    )(a, b, *ds)
    if apart == 1:
        out = out.reshape(2, owners, some, cols).swapaxes(0, 1)
    return out.reshape(2 * width, cols)


def on_device(n, owners, q_proj, k_proj, v_proj, neighbours, counts, w_out, d_out):
    scale = 1.0 / math.sqrt(HD)
    seq = lax.axis_index("seq")
    me = seq.astype(jnp.int32)[None]
    half = d_out.shape[2] // 2
    low = seq & 1

    def to(x, r):
        return lax.ppermute(x, "seq", [(i, i ^ r) for i in range(n)])

    def mine(x):
        return lax.dynamic_slice_in_dim(x, low * half, half, 1)

    def theirs(x):
        return lax.dynamic_slice_in_dim(x, (1 - low) * half, half, 1)

    def after(x, *others):
        return lax.optimization_barrier((x, *others))[0]

    def exchange(x):
        return lax.all_to_all(x, "seq", split_axis=0, concat_axis=0, tiled=True)

    sent = pack(q_proj, k_proj, v_proj, n)
    got = exchange(sent)

    w_a = lax.all_gather(mine(w_out), "zero", axis=0, tiled=True)
    w_pair = after(to(theirs(after(w_out, sent)), 1), w_a, got)
    w_b = lax.all_gather(w_pair, "zero", axis=0, tiled=True)

    d_local = after(d_out, sent)[0]
    d0 = mine(d_local)
    d1 = to(theirs(d_local), 1)
    d2 = to(d0, 2)

    attn, swapped = attend(me, neighbours, counts, got, scale)
    attn_pair = to(swapped, 1)
    d3 = to(after(d1, attn), 2)

    sent_0, own_0 = project_back([d0, d1], [w_b, w_a], (1, 0))
    (sent_1,) = project_back([after(d2, sent_0), d3], [w_b], (1,))
    pair_0, pair_1 = to(sent_0, 1), to(sent_1, 1)

    attn_pair = after(attn_pair, sent_1)
    pieces = 2
    y_far = [project(attn, attn_pair, w_a, w_b, i, pieces)[0] for i in range(pieces)]
    after_far = after(attn_pair, *y_far)
    y_far = [to(y, 2) for y in y_far]

    (own_1,) = project_back([after(d2, after_far), d3], [w_a], (0,))

    gw = weight_grad(attn, after(after_far, own_1), [d0, d1, d2, d3], owners)

    terms = [own_0, after(own_1, gw), pair_0, pair_1]
    grads = attend_back(me, neighbours, counts, got, terms, 0, attn.shape[1], scale)
    back = [grads[0]] + [to(x, r) for r, x in enumerate(grads[1:], 1)]

    attn = after(attn, grads[0])
    ys = [project(attn, attn_pair, w_a, w_b, i, pieces, far) for i, far in enumerate(y_far)]
    y_own, y_pair = [y[0] for y in ys], [to(y[1], 1) for y in ys]
    out_y = join(low.astype(jnp.int32)[None], y_own, y_pair)
    grad_q, grad_k, grad_v = unpack(me, [back])

    gw = lax.psum_scatter(after(gw, y_far[0], pair_0, pair_1), "zero", scatter_dimension=0, tiled=True)
    gw = after(gw, grads[0])
    rows = gw.shape[0] // 2
    gw_own, gw_pair = gw[:rows], to(gw[rows:], 1)
    grad_w = jnp.where(
        low == 0,
        jnp.concatenate([gw_own, gw_pair], axis=1),
        jnp.concatenate([gw_pair, gw_own], axis=1),
    ).astype(F32)
    return (out_y, grad_q, grad_k, grad_v, grad_w)


def solution(mesh):
    return jax.shard_map(
        functools.partial(on_device, mesh.shape["seq"], mesh.shape["zero"]),
        mesh=mesh,
        in_specs=(
            P("zero", "seq", None),
            P("zero", "seq", None),
            P("zero", "seq", None),
            P("zero", None, None),
            P("zero", None),
            P(("seq", "zero"), None),
            P("zero", "seq", None),
        ),
        out_specs=(
            P("zero", "seq", None),
            P("zero", "seq", None),
            P("zero", "seq", None),
            P("zero", "seq", None),
            P(("seq", "zero"), None),
        ),
        check_vma=False,
    )
```

profile of v0, /device:TPU:0, one launch (start us, length us, event | category | flops | bytes accessed | tf_op | source)
XLA Modules:
  0.0 281.9 jit_solution(3064767755869615640)
XLA Ops:
  9.1 3.6 %pack.1 = bf16[4,3,256,640]{3,2,1,0:T(8,128)(2,1)} custom-call(bf16[1,256,2560]{2,1,0:T(8,128)(2,1)} %q_ref.1, bf16[1,256,2560]{2,1,0:T(8,128)(2,1)} %k_ref.1, bf16[1,256,2560]{2,1,0:T(8,128)(2,1)} %v_ref.1), custom_call_target="tpu_custom_call" | custom-call | flops 1024 | bytes 1024 | tf_op jit(solution)/shard_map/pack/pallas_call | solution.py:65
  12.7 5.2 %all-to-all-start = ((bf16[4,3,256,640]{3,2,1,0:T(8,128)(2,1)}), bf16[4,3,256,640]{3,2,1,0:T(8,128)(2,1)}, u32[]{:S(2)}, u32[]{:S(2)}) async-start(bf16[4,3,256,640]{3,2,1,0:T(8,128)(2,1)} %pack.1), calls=%async_computation | async-start | bytes 7864320 | tf_op jit(solution)/shard_map/all_to_all | solution.py:426
  17.9 2.8 collective-permute-start.1
  20.7 51.7 %collective-permute-done.1 = bf16[80,2560]{1,0:T(8,128)(2,1)S(1)} collective-permute-done((bf16[80,2560]{1,0:T(8,128)(2,1)S(1)}, bf16[80,2560]{1,0:T(8,128)(2,1)S(1)}, u32[]{:S(2)}, u32[]{:S(2)}) %collective-permute-start.1) | collective-permute-done | bytes 409632 | tf_op jit(solution)/shard_map/ppermute | solution.py:414
  73.1 1.9 dynamic-slice_bitcast_fusion
  75.1 1.9 collective-permute-start.2
  77.7 9.4 %attend.1 = (bf16[1024,640]{1,0:T(8,128)(2,1)}, bf16[1024,640]{1,0:T(8,128)(2,1)}) custom-call(s32[1]{0:T(128)} %bitcast.1.me_ref, s32[1,8,4]{2,1,0:T(8,128)} %copy.12.nbr_ref, s32[1,8]{1,0:T(1,128)} %cnt_ref.3, bf16[4,3,256,640]{3,2,1,0:T(8,128)(2,1)} %all-to-all-done.held.got_ref), custom_call_target="tpu_custom_call" | custom-call | flops 1024 | bytes 1024 | tf_op jit(solution)/shard_map/attend/pallas_call | solution.py:199
  87.2 18.0 %collective-permute-done.refs_1_ = bf16[256,2560]{1,0:T(8,128)(2,1)} collective-permute-done((bf16[256,2560]{1,0:T(8,128)(2,1)S(1)}, bf16[256,2560]{1,0:T(8,128)(2,1)}, u32[]{:S(2)}, u32[]{:S(2)}) %collective-permute-start) | collective-permute-done | bytes 1310752 | tf_op jit(solution)/shard_map/ppermute | solution.py:414
  105.2 1.5 collective-permute-start.4
  107.1 6.0 %all-gather.5.cloned.1.call-done.refs_2_.wb_ref = bf16[640,2560]{1,0:T(8,128)(2,1)} async-done(((bf16[80,2560]{1,0:T(8,128)(2,1)}), bf16[640,2560]{1,0:T(8,128)(2,1)}) %all-gather.5.cloned.1.call-update) | async-done | bytes 3276816 | tf_op jit(solution)/shard_map/all_gather | solution.py:433
  113.1 9.4 %project_back.3 = (bf16[512,640]{1,0:T(8,128)(2,1)}, bf16[512,640]{1,0:T(8,128)(2,1)}) custom-call(bf16[256,2560]{1,0:T(8,128)(2,1)} %copy-done.3, bf16[256,2560]{1,0:T(8,128)(2,1)} %collective-permute-done.refs_1_, bf16[640,2560]{1,0:T(8,128)(2,1)} %all-gather.5.cloned.1.call-done.refs_2_.wb_ref, ...), custom_call_target="tpu_custom_call" | custom-call | flops 1024 | bytes 1024 | tf_op jit(solution)/shard_map/project_back/pallas_call | solution.py:351
  122.5 12.0 %collective-permute-done.4.refs_1_.refs_3_ = bf16[256,2560]{1,0:T(8,128)(2,1)} collective-permute-done((bf16[256,2560]{1,0:T(8,128)(2,1)}, bf16[256,2560]{1,0:T(8,128)(2,1)}, u32[]{:S(2)}, u32[]{:S(2)}) %collective-permute-start.4) | collective-permute-done | bytes 1310752 | tf_op jit(solution)/shard_map/ppermute | solution.py:414
  134.5 5.8 %project_back.4 = bf16[512,640]{1,0:T(8,128)(2,1)} custom-call(bf16[256,2560]{1,0:T(8,128)(2,1)} %collective-permute-done.2.refs_0_.refs_2_, bf16[256,2560]{1,0:T(8,128)(2,1)} %collective-permute-done.4.refs_1_.refs_3_, bf16[640,2560]{1,0:T(8,128)(2,1)} %all-gather.5.cloned.1.call-done.refs_2_.wb_ref), custom_call_target="tpu_custom_call" | custom-call | flops 1024 | bytes 1024 | tf_op jit(solution)/shard_map/project_back/pallas_call | solution.py:351
  141.4 5.3 %project.4 = bf16[512,1280]{1,0:T(8,128)(2,1)} custom-call(bf16[1024,640]{1,0:T(8,128)(2,1)} %get-tuple-element.48.a_ref, bf16[1024,640]{1,0:T(8,128)(2,1)} %copy-done.2, bf16[640,2560]{1,0:T(8,128)(2,1)} %all-gather.3.cloned.1.call-done.refs_3_.wa_ref.refs_2_, bf16[640,2560]{1,0:T(8,128)(2,1)} %all-gather.5.cloned.1.call-done.refs_2_.wb_ref), custom_call_target="tpu_custom_call" | custom-call | flops 1024 | bytes 1024 | tf_op jit(solution)/shard_map/project/pallas_call | solution.py:312
  146.7 1.5 collective-permute-start.7
  148.7 1.5 collective-permute-start.6
  150.2 5.3 %project.5 = bf16[512,1280]{1,0:T(8,128)(2,1)} custom-call(bf16[1024,640]{1,0:T(8,128)(2,1)} %get-tuple-element.48.a_ref, bf16[1024,640]{1,0:T(8,128)(2,1)} %copy-done.2, bf16[640,2560]{1,0:T(8,128)(2,1)} %all-gather.3.cloned.1.call-done.refs_3_.wa_ref.refs_2_, bf16[640,2560]{1,0:T(8,128)(2,1)} %all-gather.5.cloned.1.call-done.refs_2_.wb_ref), custom_call_target="tpu_custom_call" | custom-call | flops 1024 | bytes 1024 | tf_op jit(solution)/shard_map/project/pallas_call | solution.py:312
  155.5 5.8 %project_back.5.rest_1_ = bf16[512,640]{1,0:T(8,128)(2,1)} custom-call(bf16[256,2560]{1,0:T(8,128)(2,1)} %collective-permute-done.2.refs_0_.refs_2_, bf16[256,2560]{1,0:T(8,128)(2,1)} %collective-permute-done.4.refs_1_.refs_3_, bf16[640,2560]{1,0:T(8,128)(2,1)} %all-gather.3.cloned.1.call-done.refs_3_.wa_ref.refs_2_), custom_call_target="tpu_custom_call" | custom-call | flops 1024 | bytes 1024 | tf_op jit(solution)/shard_map/project_back/pallas_call | solution.py:351
  161.4 12.0 %weight_grad.1 = bf16[8,2,80,2560]{3,2,1,0:T(8,128)(2,1)} custom-call(bf16[1024,640]{1,0:T(8,128)(2,1)} %get-tuple-element.48.a_ref, bf16[1024,640]{1,0:T(8,128)(2,1)} %copy-done.2, bf16[256,2560]{1,0:T(8,128)(2,1)} %copy-done.3, bf16[256,2560]{1,0:T(8,128)(2,1)} %collective-permute-done.refs_1_, bf16[256,2560]{1,0:T(8,128)(2,1)} %collective-permute-done.2.refs_0_.refs_2_, ...), custom_call_target="tpu_custom_call" | custom-call | flops 1024 | bytes 1024 | tf_op jit(solution)/shard_map/weight_grad/pallas_call | solution.py:390
  173.4 2.9 %collective-permute-done.6.rest_3_ = bf16[512,640]{1,0:T(8,128)(2,1)S(1)} collective-permute-done((bf16[512,640]{1,0:T(8,128)(2,1)S(1)}, bf16[512,640]{1,0:T(8,128)(2,1)S(1)}, u32[]{:S(2)}, u32[]{:S(2)}) %collective-permute-start.6) | collective-permute-done | bytes 655392 | tf_op jit(solution)/shard_map/ppermute | solution.py:414
  179.5 15.0 %attend_back.1 = (bf16[3,256,640]{2,1,0:T(8,128)(2,1)}, bf16[3,256,640]{2,1,0:T(8,128)(2,1)}, bf16[3,256,640]{2,1,0:T(8,128)(2,1)}, bf16[3,256,640]{2,1,0:T(8,128)(2,1)}) custom-call(s32[1]{0:T(128)} %bitcast.1.me_ref, s32[1,8,4]{2,1,0:T(8,128)} %copy.12.nbr_ref, s32[1,8]{1,0:T(1,128)} %cnt_ref.3, bf16[4,3,256,640]{3,2,1,0:T(8,128)(2,1)} %all-to-all-done.held.got_ref, ...), custom_call_target="tpu_custom_call" | custom-call | flops 1024 | bytes 1024 | tf_op jit(solution)/shard_map/attend_back/pallas_call | solution.py:269
  195.9 2.1 collective-permute-start.13
  198.0 5.8 %project.6 = (bf16[256,1280]{1,0:T(8,128)(2,1)}, bf16[256,1280]{1,0:T(8,128)(2,1)}) custom-call(bf16[1024,640]{1,0:T(8,128)(2,1)} %get-tuple-element.48.a_ref, bf16[1024,640]{1,0:T(8,128)(2,1)} %copy-done.2, bf16[640,2560]{1,0:T(8,128)(2,1)} %all-gather.3.cloned.1.call-done.refs_3_.wa_ref.refs_2_, ...), custom_call_target="tpu_custom_call" | custom-call | flops 1024 | bytes 1024 | tf_op jit(solution)/shard_map/project/pallas_call | solution.py:312
  204.2 6.5 %collective-permute-done.8.rest_0_ = bf16[512,1280]{1,0:T(8,128)(2,1)} collective-permute-done((bf16[512,1280]{1,0:T(8,128)(2,1)S(1)}, bf16[512,1280]{1,0:T(8,128)(2,1)}, u32[]{:S(2)}, u32[]{:S(2)}) %collective-permute-start.8) | collective-permute-done | bytes 1310752 | tf_op jit(solution)/shard_map/ppermute | solution.py:414
  210.7 6.1 %project.7 = (bf16[256,1280]{1,0:T(8,128)(2,1)}, bf16[256,1280]{1,0:T(8,128)(2,1)}) custom-call(bf16[1024,640]{1,0:T(8,128)(2,1)} %get-tuple-element.48.a_ref, bf16[1024,640]{1,0:T(8,128)(2,1)} %copy-done.2, bf16[640,2560]{1,0:T(8,128)(2,1)} %all-gather.3.cloned.1.call-done.refs_3_.wa_ref.refs_2_, ...), custom_call_target="tpu_custom_call" | custom-call | flops 1024 | bytes 1024 | tf_op jit(solution)/shard_map/project/pallas_call | solution.py:312
  217.3 31.6 %reduce-scatter.2.cloned.1.call-done = bf16[160,2560]{1,0:T(8,128)(2,1)} async-done(((bf16[1280,2560]{1,0:T(8,128)(2,1)}), bf16[160,2560]{1,0:T(8,128)(2,1)}) %reduce-scatter.2.cloned.1.call-update) | async-done | bytes 819216 | tf_op jit(solution)/shard_map/reduce_scatter | solution.py:468
  248.9 1.2 fusion.1
  250.1 1.5 collective-permute-start.14
  251.6 3.5 %unpack.1 = (bf16[1,256,2560]{2,1,0:T(8,128)(2,1)}, bf16[1,256,2560]{2,1,0:T(8,128)(2,1)}, bf16[1,256,2560]{2,1,0:T(8,128)(2,1)}) custom-call(s32[1]{0:T(128)} %bitcast.1.me_ref, bf16[3,256,640]{2,1,0:T(8,128)(2,1)} %get-tuple-element.47.rest_0_, bf16[3,256,640]{2,1,0:T(8,128)(2,1)} %copy-done.6, bf16[3,256,640]{2,1,0:T(8,128)(2,1)} %collective-permute-done.12.rest_2_, ...), custom_call_target="tpu_custom_call" | custom-call | flops 1024 | bytes 1024 | tf_op jit(solution)/shard_map/unpack/pallas_call | solution.py:95
  255.1 13.2 %collective-permute-done.10.rest_3_ = bf16[256,1280]{1,0:T(8,128)(2,1)S(1)} collective-permute-done((bf16[256,1280]{1,0:T(8,128)(2,1)}, bf16[256,1280]{1,0:T(8,128)(2,1)S(1)}, u32[]{:S(2)}, u32[]{:S(2)}) %collective-permute-start.10) | collective-permute-done | bytes 655392 | tf_op jit(solution)/shard_map/ppermute | solution.py:414
  269.2 2.7 join.1
  272.8 2.5 fusion
  (54 shorter events, 12.9 us)
Async XLA Ops:
  7.2 1.2 copy-start
  7.2 65.1 %all-gather.3.cloned.1.call-start = ((), (), s32[]{:S(2)}) async-start(), calls=%async_computation.2 | async-start | bytes 3686400 | tf_op jit(solution)/shard_map/all_gather | solution.py:431
  12.7 59.6 %all-to-all-start = ((bf16[4,3,256,640]{3,2,1,0:T(8,128)(2,1)}), bf16[4,3,256,640]{3,2,1,0:T(8,128)(2,1)}, u32[]{:S(2)}, u32[]{:S(2)}) async-start(bf16[4,3,256,640]{3,2,1,0:T(8,128)(2,1)} %pack.1), calls=%async_computation | async-start | bytes 7864320 | tf_op jit(solution)/shard_map/all_to_all | solution.py:426
  17.9 95.2 %all-gather.5.cloned.1.call-start = ((), (), s32[]{:S(2)}) async-start(), calls=%async_computation.3 | async-start | bytes 3686400 | tf_op jit(solution)/shard_map/all_gather | solution.py:433
  17.9 54.4 %collective-permute-start.1 = (bf16[80,2560]{1,0:T(8,128)(2,1)S(1)}, bf16[80,2560]{1,0:T(8,128)(2,1)S(1)}, u32[]{:S(2)}, u32[]{:S(2)}) collective-permute-start(bf16[80,2560]{1,0:T(8,128)(2,1)S(1)} %constant_dynamic-slice_fusion.1), channel_id=1, source_target_pairs={{0,8},{8,0},{16,24},{24,16},{1,9},{9,1},{17,25},{25,17},{2,10},{10... | collective-permute-start | bytes 1228808 | tf_op jit(solution)/shard_map/ppermute | solution.py:414
  72.3 0.8 copy-start.11
  73.1 4.0 %copy-start.12 = (s32[1,8,4]{1,2,0:T(4,128)S(1)}, s32[1,8,4]{1,2,0:T(4,128)}, u32[]{:S(2)}) copy-start(s32[1,8,4]{1,2,0:T(4,128)} %param.10) | copy-start | bytes 388
  73.1 175.8 %reduce-scatter.2.cloned.1.call-start = ((), (), s32[]{:S(2)}) async-start(), calls=%async_computation.4 | async-start | bytes 7372800 | tf_op jit(solution)/shard_map/reduce_scatter | solution.py:468
  75.0 12.1 %copy-start.3 = (bf16[256,2560]{1,0:T(8,128)(2,1)}, bf16[256,2560]{1,0:T(8,128)(2,1)S(1)}, u32[]{:S(2)}) copy-start(bf16[256,2560]{1,0:T(8,128)(2,1)S(1)} %get-tuple-element.62.refs_0_) | copy-start | bytes 3932164
  75.1 30.1 %collective-permute-start = (bf16[256,2560]{1,0:T(8,128)(2,1)S(1)}, bf16[256,2560]{1,0:T(8,128)(2,1)}, u32[]{:S(2)}, u32[]{:S(2)}) collective-permute-start(bf16[256,2560]{1,0:T(8,128)(2,1)S(1)} %get-tuple-element.61), channel_id=1, source_target_pairs={{0,8},{8,0},{16,24},{24,16},{1,9},{9,1},{17,25},{25,17},{2,10},{10... | collective-permute-start | bytes 3932168 | tf_op jit(solution)/shard_map/ppermute | solution.py:414
  75.1 47.4 %collective-permute-start.2 = (bf16[256,2560]{1,0:T(8,128)(2,1)S(1)}, bf16[256,2560]{1,0:T(8,128)(2,1)}, u32[]{:S(2)}, u32[]{:S(2)}) collective-permute-start(bf16[256,2560]{1,0:T(8,128)(2,1)S(1)} %get-tuple-element.62.refs_0_), channel_id=1, source_target_pairs={{0,16},{8,24},{16,0},{24,8},{1,17},{9,25},{17,1},{25,9},{2,18},{10... | collective-permute-start | bytes 3932168 | tf_op jit(solution)/shard_map/ppermute | solution.py:414
  105.2 29.4 %collective-permute-start.4 = (bf16[256,2560]{1,0:T(8,128)(2,1)}, bf16[256,2560]{1,0:T(8,128)(2,1)}, u32[]{:S(2)}, u32[]{:S(2)}) collective-permute-start(bf16[256,2560]{1,0:T(8,128)(2,1)} %collective-permute-done.refs_1_), channel_id=1, source_target_pairs={{0,16},{8,24},{16,0},{24,8},{1,17},{9,25},{17,1},{25,9},{2,18},{10... | collective-permute-start | bytes 3932168 | tf_op jit(solution)/shard_map/ppermute | solution.py:414
  106.6 33.7 %collective-permute-start.3 = (bf16[1024,640]{1,0:T(8,128)(2,1)}, bf16[1024,640]{1,0:T(8,128)(2,1)S(1)}, u32[]{:S(2)}, u32[]{:S(2)}) collective-permute-start(bf16[1024,640]{1,0:T(8,128)(2,1)} %get-tuple-element.38), channel_id=1, source_target_pairs={{0,8},{8,0},{16,24},{24,16},{1,9},{9,1},{17,25},{25,17},{2,10},{10... | collective-permute-start | bytes 3932168 | tf_op jit(solution)/shard_map/ppermute | solution.py:414
  140.4 8.3 %copy-start.9 = (bf16[512,640]{1,0:T(8,128)(2,1)S(1)}, bf16[512,640]{1,0:T(8,128)(2,1)}, u32[]{:S(2)}) copy-start(bf16[512,640]{1,0:T(8,128)(2,1)} %project_back.4) | copy-start | bytes 1966084
  140.4 1.1 copy-start.2
  146.7 29.5 %collective-permute-start.7 = (bf16[512,1280]{1,0:T(8,128)(2,1)}, bf16[512,1280]{1,0:T(8,128)(2,1)S(1)}, u32[]{:S(2)}, u32[]{:S(2)}) collective-permute-start(bf16[512,1280]{1,0:T(8,128)(2,1)} %project.4), channel_id=1, source_target_pairs={{0,16},{8,24},{16,0},{24,8},{1,17},{9,25},{17,1},{25,9},{2,18},{10... | collective-permute-start | bytes 3932168 | tf_op jit(solution)/shard_map/ppermute | solution.py:414
  148.2 25.2 %collective-permute-start.5 = (bf16[512,640]{1,0:T(8,128)(2,1)}, bf16[512,640]{1,0:T(8,128)(2,1)S(1)}, u32[]{:S(2)}, u32[]{:S(2)}) collective-permute-start(bf16[512,640]{1,0:T(8,128)(2,1)} %get-tuple-element.39), channel_id=1, source_target_pairs={{0,8},{8,0},{16,24},{24,16},{1,9},{9,1},{17,25},{25,17},{2,10},{10... | collective-permute-start | bytes 1966088 | tf_op jit(solution)/shard_map/ppermute | solution.py:414
  148.7 27.5 %collective-permute-start.6 = (bf16[512,640]{1,0:T(8,128)(2,1)S(1)}, bf16[512,640]{1,0:T(8,128)(2,1)S(1)}, u32[]{:S(2)}, u32[]{:S(2)}) collective-permute-start(bf16[512,640]{1,0:T(8,128)(2,1)S(1)} %copy-done.9), channel_id=1, source_target_pairs={{0,8},{8,0},{16,24},{24,16},{1,9},{9,1},{17,25},{25,17},{2,10},{10... | collective-permute-start | bytes 1966088 | tf_op jit(solution)/shard_map/ppermute | solution.py:414
  173.4 3.8 %copy-start.7 = (bf16[512,640]{1,0:T(8,128)(2,1)}, bf16[512,640]{1,0:T(8,128)(2,1)S(1)}, u32[]{:S(2)}) copy-start(bf16[512,640]{1,0:T(8,128)(2,1)S(1)} %collective-permute-done.5.rest_2_) | copy-start | bytes 1966084
  176.3 0.8 copy-start.8
  177.1 1.1 copy-start.4
  177.1 1.8 copy-start.5
  178.9 31.8 %collective-permute-start.8 = (bf16[512,1280]{1,0:T(8,128)(2,1)S(1)}, bf16[512,1280]{1,0:T(8,128)(2,1)}, u32[]{:S(2)}, u32[]{:S(2)}) collective-permute-start(bf16[512,1280]{1,0:T(8,128)(2,1)S(1)} %copy-done.5), channel_id=1, source_target_pairs={{0,16},{8,24},{16,0},{24,8},{1,17},{9,25},{17,1},{25,9},{2,18},{10... | collective-permute-start | bytes 3932168 | tf_op jit(solution)/shard_map/ppermute | solution.py:414
  194.4 55.6 %collective-permute-start.11 = (bf16[3,256,640]{2,1,0:T(8,128)(2,1)}, bf16[3,256,640]{2,1,0:T(8,128)(2,1)S(1)}, u32[]{:S(2)}, u32[]{:S(2)}) collective-permute-start(bf16[3,256,640]{2,1,0:T(8,128)(2,1)} %get-tuple-element.53), channel_id=1, source_target_pairs={{0,8},{8,0},{16,24},{24,16},{1,9},{9,1},{17,25},{25,17},{2,10},{10... | collective-permute-start | bytes 2949128 | tf_op jit(solution)/shard_map/ppermute | solution.py:414
  194.8 56.8 %collective-permute-start.12 = (bf16[3,256,640]{2,1,0:T(8,128)(2,1)}, bf16[3,256,640]{2,1,0:T(8,128)(2,1)}, u32[]{:S(2)}, u32[]{:S(2)}) collective-permute-start(bf16[3,256,640]{2,1,0:T(8,128)(2,1)} %get-tuple-element.54), channel_id=1, source_target_pairs={{0,16},{8,24},{16,0},{24,8},{1,17},{9,25},{17,1},{25,9},{2,18},{10... | collective-permute-start | bytes 2949128 | tf_op jit(solution)/shard_map/ppermute | solution.py:414
  195.9 55.7 %collective-permute-start.13 = (bf16[3,256,640]{2,1,0:T(8,128)(2,1)}, bf16[3,256,640]{2,1,0:T(8,128)(2,1)}, u32[]{:S(2)}, u32[]{:S(2)}) collective-permute-start(bf16[3,256,640]{2,1,0:T(8,128)(2,1)} %get-tuple-element.55), channel_id=1, source_target_pairs={{0,24},{8,16},{16,8},{24,0},{1,25},{9,17},{17,9},{25,1},{2,26},{10... | collective-permute-start | bytes 2949128 | tf_op jit(solution)/shard_map/ppermute | solution.py:414
  203.8 51.3 %collective-permute-start.9 = (bf16[256,1280]{1,0:T(8,128)(2,1)}, bf16[256,1280]{1,0:T(8,128)(2,1)}, u32[]{:S(2)}, u32[]{:S(2)}) collective-permute-start(bf16[256,1280]{1,0:T(8,128)(2,1)} %get-tuple-element.51), channel_id=1, source_target_pairs={{0,8},{8,0},{16,24},{24,16},{1,9},{9,1},{17,25},{25,17},{2,10},{10... | collective-permute-start | bytes 1966088 | tf_op jit(solution)/shard_map/ppermute | solution.py:414
  216.8 51.5 %collective-permute-start.10 = (bf16[256,1280]{1,0:T(8,128)(2,1)}, bf16[256,1280]{1,0:T(8,128)(2,1)S(1)}, u32[]{:S(2)}, u32[]{:S(2)}) collective-permute-start(bf16[256,1280]{1,0:T(8,128)(2,1)} %get-tuple-element.52), channel_id=1, source_target_pairs={{0,8},{8,0},{16,24},{24,16},{1,9},{9,1},{17,25},{25,17},{2,10},{10... | collective-permute-start | bytes 1966088 | tf_op jit(solution)/shard_map/ppermute | solution.py:414
  250.1 1.6 copy-start.6
  250.1 22.8 %collective-permute-start.14 = (bf16[80,2560]{1,0:T(8,128)(2,1)S(1)}, bf16[80,2560]{1,0:T(8,128)(2,1)}, u32[]{:S(2)}, u32[]{:S(2)}) collective-permute-start(bf16[80,2560]{1,0:T(8,128)(2,1)S(1)} %get-tuple-element.64), channel_id=1, source_target_pairs={{0,8},{8,0},{16,24},{24,16},{1,9},{9,1},{17,25},{25,17},{2,10},{10... | collective-permute-start | bytes 1228808 | tf_op jit(solution)/shard_map/ppermute | solution.py:414
  268.3 0.8 copy-start.10
  269.2 6.1 %copy-start.1 = (bf16[80,5120]{1,0:T(8,128)(2,1)S(1)}, bf16[80,5120]{1,0:T(8,128)(2,1)}, u32[]{:S(2)}) copy-start(bf16[80,5120]{1,0:T(8,128)(2,1)} %param.12) | copy-start | bytes 2457604
Sparse Core Ops, SparseCore 0:
  10.2 42.0 all-gather.2
  73.2 39.8 all-gather.4
  177.2 71.5 reduce-scatter.1
where the time goes:
time: 283 us; the launch traced here: 282 us
  waiting for transfers between devices  143 us (51%)
  Pallas kernels  89.7 us (32%)
  starting transfers between devices  22 us (8%)
  between operations  13.9 us (5%)
  local copies, waits for them, and re-layouts  10.9 us (4%)
    ppermute x15, waiting for transfers between devices, to(): return lax.ppermute(x, 'seq', [(i, i ^ r) for i in range(n)])  105 us
    reduce_scatter x1, waiting for transfers between devices, on_device(): lax.psum_scatter(after(gw, y_far[0], pair_0, pair_1), 'zero', scatter_dim...  31.6 us
    pallas_call x4, Pallas kernels, project(): pl.pallas_call(project_kernel, grid=(cols // tile,), out_shape=[sds((out,...  22.6 us
    pallas_call x3, Pallas kernels, project_back(): pl.pallas_call(functools.partial(project_back_kernel, n, m, order), out_s...  21 us
    ppermute x15, starting transfers between devices, to(): return lax.ppermute(x, 'seq', [(i, i ^ r) for i in range(n)])  16.7 us
    pallas_call x1, Pallas kernels, attend_back(): pl.pallas_call(functools.partial(bwd_kernel, begin, nbr.shape[2], scale),...  15 us
    pallas_call x1, Pallas kernels, weight_grad(): pl.pallas_call(functools.partial(weight_kernel, n), grid=(cols // tile,),...  12 us
    pallas_call x1, Pallas kernels, attend(): pl.pallas_call(functools.partial(fwd_kernel, width // HD, nbr.shape[2], s...  9.43 us
  transfers between devices with their start and end apart: 19, of which 9 were waited for; matrix products, arithmetic and copies ran while one was open for 1% of the time, Pallas kernels for 30%

commit v1 on v0

--- a/solution.py
+++ b/solution.py
@@ -172,7 +172,7 @@
         out[j * BLK : (j + 1) * BLK] = held[e // per, t, rows]
 
 
-def fwd_kernel(heads, slots, scale, me_ref, nbr_ref, cnt_ref, held, attn_ref, swap_ref, ks, vs):
+def fwd_kernel(heads, slots, scale, me_ref, nbr_ref, cnt_ref, held, attn_ref, swap_ref, t_ref, ks, vs):
     me = me_ref[0]
     n, per = held.shape[0], held.shape[2] // BLK
 
@@ -191,6 +191,7 @@
             swap_ref[pl.ds(there, BLK), c] = out
 
     for_blocks(n * per, slots, nbr_ref, cnt_ref, body)
+    t_ref[...] = attn_ref[...].T
 
 
 def attend(me, nbr, cnt, got, scale):
@@ -198,9 +199,9 @@
     vm = pl.BlockSpec(memory_space=pltpu.VMEM)
     return pl.pallas_call(
         functools.partial(fwd_kernel, width // HD, nbr.shape[2], scale),
-        out_shape=[sds((n * rows, width))] * 2,
+        out_shape=[sds((n * rows, width))] * 2 + [sds((width, n * rows))],
         in_specs=[SMEM] * 3 + [vm],
-        out_specs=[vm, vm],
+        out_specs=[vm] * 3,
         scratch_shapes=[pltpu.VMEM((nbr.shape[2] * BLK, width), BF)] * 2,
         compiler_params=params(60),
         cost_estimate=COST,
@@ -215,10 +216,19 @@
     per = rows // BLK
     cols = pl.ds(begin, some)
     copies = [pltpu.make_async_copy(got_ref.at[:, :, :, cols], held, sem)]
-    for i, ref in enumerate(d_refs):
-        part = pl.ds(i % 2 * ref.shape[0], ref.shape[0])
+    own_0, own_1, pair_0, pair_1 = d_refs
+    for i, (ref, begin, end, t, start) in enumerate(
+        (
+            (own_0, 0, 3, 0, 0),
+            (own_1, 0, 1, 0, 3),
+            (pair_0, 0, 2, 1, 0),
+            (pair_0, 2, 3, 1, 3),
+            (pair_1, 0, 1, 1, 2),
+        )
+    ):
+        part, there = pl.ds(begin * rows, (end - begin) * rows), pl.ds(start * rows, (end - begin) * rows)
         copies.append(
-            pltpu.make_async_copy(ref.at[:, cols], terms.at[i // 2, part], d_sem.at[i])
+            pltpu.make_async_copy(ref.at[part, cols], terms.at[t, there], d_sem.at[i])
         )
     for c in copies:
         c.start()
@@ -280,7 +290,7 @@
             pltpu.VMEM((nbr.shape[2] * BLK, some), BF),
             pltpu.VMEM((nbr.shape[2] * BLK, some), BF),
             pltpu.SemaphoreType.DMA,
-            pltpu.SemaphoreType.DMA((4,)),
+            pltpu.SemaphoreType.DMA((5,)),
         ],
         compiler_params=params(60),
         cost_estimate=COST,
@@ -300,11 +310,11 @@
     pair_ref[...] = y[rows:]
 
 
-def project(a, b, wa, wb, part, parts, far=None, tile=640):
+def project(a, b, wa, wb, begin, end, far=None, tile=512):
     rows, depth = a.shape
     rows //= 2
-    cols = wa.shape[1] // parts
-    skip = part * (cols // tile)
+    cols = end - begin
+    skip = begin // tile
     near = far is not None
     left = pl.BlockSpec((rows, depth), lambda j: (0 if near else 1, 0))
     right = pl.BlockSpec((depth, tile), lambda j: (0, skip + j))
@@ -339,7 +349,7 @@
             copies[n + i].wait()
         out = dot(held_d[...], held_w[i], NT).astype(BF)
         for r in range(n):
-            there = r ^ 1 if order[i] else r
+            there = order[i][r]
             o_refs[i][there * rows : (there + 1) * rows] = out[r * rows : (r + 1) * rows]
 
 
@@ -364,13 +374,12 @@
     )(*ds, *ws)
 
 
-def weight_kernel(n, a_ref, b_ref, *refs):
-    ds, o_ref, at, bt, d = refs[:n], refs[n], refs[n + 1], refs[n + 2], refs[n + 3]
+def weight_kernel(n, at, b_ref, *refs):
+    ds, o_ref, bt, d = refs[:n], refs[n], refs[n + 1], refs[n + 2]
     rows = ds[0].shape[0]
 
     @pl.when(pl.program_id(0) == 0)
     def _():
-        at[...] = a_ref[...].T
         bt[...] = b_ref[...].T
 
     for r, piece in enumerate(ds):
@@ -380,24 +389,27 @@
         o_ref[:, i] = out.reshape(o_ref.shape[0], *o_ref.shape[2:])
 
 
-def weight_grad(a, b, ds, owners, tile=512):
+def weight_grad(at, b, ds, owners, tile=512):
     n = len(ds)
-    tokens, width = a.shape
+    tokens, width = b.shape
     rows, cols = ds[0].shape
     some = width // owners
     apart = owners if some % 16 == 0 else 1
-    whole = pl.BlockSpec((tokens, width), lambda j: (0, 0))
     out = pl.pallas_call(
         functools.partial(weight_kernel, n),
         grid=(cols // tile,),
         out_shape=sds((apart, 2, width // apart, cols)),
-        in_specs=[whole, whole] + [pl.BlockSpec((rows, tile), lambda j: (0, j))] * n,
+        in_specs=[
+            pl.BlockSpec((width, tokens), lambda j: (0, 0)),
+            pl.BlockSpec((tokens, width), lambda j: (0, 0)),
+        ]
+        + [pl.BlockSpec((rows, tile), lambda j: (0, j))] * n,
         out_specs=pl.BlockSpec((apart, 2, width // apart, tile), lambda j: (0, 0, 0, j)),
-        scratch_shapes=[pltpu.VMEM((width, tokens), BF)] * 2 + [pltpu.VMEM((tokens, tile), BF)],
+        scratch_shapes=[pltpu.VMEM((width, tokens), BF), pltpu.VMEM((tokens, tile), BF)],
         compiler_params=params(60),
         cost_estimate=COST,
         name="weight_grad",
-    )(a, b, *ds)
+    )(at, b, *ds)
     if apart == 1:
         out = out.reshape(2, owners, some, cols).swapaxes(0, 1)
     return out.reshape(2 * width, cols)
@@ -425,43 +437,54 @@
     def exchange(x):
         return lax.all_to_all(x, "seq", split_axis=0, concat_axis=0, tiled=True)
 
+    def exchange(x):
+        return lax.all_to_all(x, "seq", split_axis=0, concat_axis=0, tiled=True)
+
     sent = pack(q_proj, k_proj, v_proj, n)
     got = exchange(sent)
 
+    w_out = after(w_out, sent)
     w_a = lax.all_gather(mine(w_out), "zero", axis=0, tiled=True)
-    w_pair = after(to(theirs(after(w_out, sent)), 1), w_a, got)
+    d_local = after(d_out, sent)[0]
+    d0, d_theirs = mine(d_local), theirs(d_local)
+
+    w_pair = after(to(theirs(after(w_out, d0, d_theirs)), 1), w_a, got)
     w_b = lax.all_gather(w_pair, "zero", axis=0, tiled=True)
 
-    d_local = after(d_out, sent)[0]
-    d0 = mine(d_local)
-    d1 = to(theirs(d_local), 1)
+    d1 = to(d_theirs, 1)
     d2 = to(d0, 2)
 
-    attn, swapped = attend(me, neighbours, counts, got, scale)
+    attn, swapped, attn_t = attend(me, neighbours, counts, got, scale)
     attn_pair = to(swapped, 1)
     d3 = to(after(d1, attn), 2)
 
-    sent_0, own_0 = project_back([d0, d1], [w_b, w_a], (1, 0))
-    (sent_1,) = project_back([after(d2, sent_0), d3], [w_b], (1,))
-    pair_0, pair_1 = to(sent_0, 1), to(sent_1, 1)
-
-    attn_pair = after(attn_pair, sent_1)
-    pieces = 2
-    y_far = [project(attn, attn_pair, w_a, w_b, i, pieces)[0] for i in range(pieces)]
-    after_far = after(attn_pair, *y_far)
-    y_far = [to(y, 2) for y in y_far]
-
-    (own_1,) = project_back([after(d2, after_far), d3], [w_a], (0,))
-
-    gw = weight_grad(attn, after(after_far, own_1), [d0, d1, d2, d3], owners)
+    (own_0,) = project_back([d0, d1, d2], [w_a], ((0, 1, 2),))
+    (sent_0,) = project_back([d0, after(d1, own_0), d2], [w_b], ((1, 0, 2),))
+    pair_0 = to(sent_0, 1)
+    attn_pair = after(attn_pair, sent_0)
+
+    near_cut = half * 2 // 5
+    ranges = [(0, near_cut), (near_cut, half)]
+    far_0 = project(attn, attn_pair, w_a, w_b, *ranges[0])[0]
+    (sent_1,) = project_back([after(d3, far_0)], [w_b], ((0,),))
+    pair_1 = to(sent_1, 1)
+    far_1 = project(attn, after(attn_pair, sent_1), w_a, w_b, *ranges[1])[0]
+    after_far = after(attn_pair, far_1)
+    y_far = [to(far_0, 2), to(far_1, 2)]
+    (own_1,) = project_back([after(d3, after_far)], [w_a], ((0,),))
+
+    gw = weight_grad(attn_t, after(after_far, own_1), [d0, d1, d2, d3], owners)
 
     terms = [own_0, after(own_1, gw), pair_0, pair_1]
     grads = attend_back(me, neighbours, counts, got, terms, 0, attn.shape[1], scale)
     back = [grads[0]] + [to(x, r) for r, x in enumerate(grads[1:], 1)]
 
-    attn = after(attn, grads[0])
-    ys = [project(attn, attn_pair, w_a, w_b, i, pieces, far) for i, far in enumerate(y_far)]
-    y_own, y_pair = [y[0] for y in ys], [to(y[1], 1) for y in ys]
+    ys, y_pair, last = [], [], gw
+    for c, far in zip(ranges, y_far):
+        ys.append(project(after(attn, last), attn_pair, w_a, w_b, *c, far))
+        y_pair.append(to(ys[-1][1], 1))
+        last = y_pair[-1]
+    y_own = [y[0] for y in ys]
     out_y = join(low.astype(jnp.int32)[None], y_own, y_pair)
     grad_q, grad_k, grad_v = unpack(me, [back])
 

time: 283 us -> 268 us (0.947)
  waiting for transfers between devices: 143 us -> 125 us
    ppermute x15, waiting for transfers between devices: 105 us -> 99.3 us  [to(): return lax.ppermute(x, 'seq', [(i, i ^ r) for i in range(n)])]
    all_gather x1, waiting for transfers between devices: 5.97 us -> 0.02 us  [on_device(): w_b = lax.all_gather(w_pair, 'zero', axis=0, tiled=True)]
    reduce_scatter x1, waiting for transfers between devices: 31.6 us -> 25.8 us  [on_device(): lax.psum_scatter(after(gw, y_far[0], pair_0, pair_1), 'zero', scatter_dim...]
    pallas_call x3 -> x4, Pallas kernels: 21 us -> 23.3 us  [project_back(): pl.pallas_call(functools.partial(project_back_kernel, n, m, order), out_s...]
    unnamed x27 -> x25, local copies, waits for them, and re-layouts: 7.01 us -> 5.93 us
  transfers between devices with their start and end apart: 19 -> 19, of which waited for: 9 -> 9; matrix products, arithmetic and copies ran while one was open for 1% -> 2% of each run, Pallas kernels for 30% -> 33%
where the time goes in v1:
time: 268 us; the launch traced here: 266 us
  waiting for transfers between devices  125 us (47%)
  Pallas kernels  91.6 us (34%)
  starting transfers between devices  23.4 us (9%)
  between operations  13.9 us (5%)
  local copies, waits for them, and re-layouts  10.9 us (4%)
    ppermute x15, waiting for transfers between devices, to(): return lax.ppermute(x, 'seq', [(i, i ^ r) for i in range(n)])  99.3 us
    reduce_scatter x1, waiting for transfers between devices, on_device(): lax.psum_scatter(after(gw, y_far[0], pair_0, pair_1), 'zero', scatter_dim...  25.8 us
    pallas_call x4, Pallas kernels, project_back(): pl.pallas_call(functools.partial(project_back_kernel, n, m, order), out_s...  23.3 us
    pallas_call x4, Pallas kernels, project(): pl.pallas_call(project_kernel, grid=(cols // tile,), out_shape=[sds((out,...  21.6 us
    ppermute x15, starting transfers between devices, to(): return lax.ppermute(x, 'seq', [(i, i ^ r) for i in range(n)])  18.1 us
    pallas_call x1, Pallas kernels, attend_back(): pl.pallas_call(functools.partial(bwd_kernel, begin, nbr.shape[2], scale),...  15.1 us
    pallas_call x1, Pallas kernels, weight_grad(): pl.pallas_call(functools.partial(weight_kernel, n), grid=(cols // tile,),...  11.7 us
    pallas_call x1, Pallas kernels, attend(): pl.pallas_call(functools.partial(fwd_kernel, width // HD, nbr.shape[2], s...  10.1 us
  transfers between devices with their start and end apart: 19, of which 9 were waited for; matrix products, arithmetic and copies ran while one was open for 2% of the time, Pallas kernels for 33%

profile of v1, /device:TPU:0, one launch (start us, length us, event | category | flops | bytes accessed | tf_op | source)
XLA Modules:
  0.0 266.4 jit_solution(13291340132685360682)
XLA Ops:
  7.2 3.6 %pack.1 = bf16[4,3,256,640]{3,2,1,0:T(8,128)(2,1)} custom-call(bf16[1,256,2560]{2,1,0:T(8,128)(2,1)} %q_ref.1, bf16[1,256,2560]{2,1,0:T(8,128)(2,1)} %k_ref.1, bf16[1,256,2560]{2,1,0:T(8,128)(2,1)} %v_ref.1), custom_call_target="tpu_custom_call" | custom-call | flops 1024 | bytes 1024 | tf_op jit(solution)/shard_map/pack/pallas_call | solution.py:65
  11.7 5.2 %all-to-all-start = ((bf16[4,3,256,640]{3,2,1,0:T(8,128)(2,1)}), bf16[4,3,256,640]{3,2,1,0:T(8,128)(2,1)}, u32[]{:S(2)}, u32[]{:S(2)}) async-start(bf16[4,3,256,640]{3,2,1,0:T(8,128)(2,1)} %pack.1), calls=%async_computation | async-start | bytes 7864320 | tf_op jit(solution)/shard_map/all_to_all | solution.py:441
  16.9 2.9 %dynamic-slice_bitcast_fusion = (bf16[256,2560]{1,0:T(8,128)(2,1)}, bf16[256,2560]{1,0:T(8,128)(2,1)S(1)}) fusion(bf16[1,256,5120]{2,1,0:T(8,128)(2,1)} %param.13, s32[]{:T(128)S(6)} %select_n.17, s32[]{:T(128)S(6)} %select_n.16), kind=kLoop, calls=%fused_computation | loop fusion | bytes 5242888 | tf_op jit(solution)/shard_map/dynamic_slice | solution.py:432
  19.9 2.7 %collective-permute-start.3 = (bf16[80,2560]{1,0:T(8,128)(2,1)S(1)}, bf16[80,2560]{1,0:T(8,128)(2,1)S(1)}, u32[]{:S(2)}, u32[]{:S(2)}) collective-permute-start(bf16[80,2560]{1,0:T(8,128)(2,1)S(1)} %constant_dynamic-slice_fusion), channel_id=1, source_target_pairs={{0,8},{8,0},{16,24},{24,16},{1,9},{9,1},{17,25},{25,17},{2,10},{10... | collective-permute-start | bytes 1228808 | tf_op jit(solution)/shard_map/ppermute | solution.py:426
  22.6 48.7 %collective-permute-done.3 = bf16[80,2560]{1,0:T(8,128)(2,1)S(1)} collective-permute-done((bf16[80,2560]{1,0:T(8,128)(2,1)S(1)}, bf16[80,2560]{1,0:T(8,128)(2,1)S(1)}, u32[]{:S(2)}, u32[]{:S(2)}) %collective-permute-start.3) | collective-permute-done | bytes 409632 | tf_op jit(solution)/shard_map/ppermute | solution.py:426
  72.2 1.9 collective-permute-start.2
  74.8 10.1 %attend.1 = (bf16[1024,640]{1,0:T(8,128)(2,1)}, bf16[1024,640]{1,0:T(8,128)(2,1)}, bf16[640,1024]{1,0:T(8,128)(2,1)}) custom-call(s32[1]{0:T(128)} %bitcast.1.me_ref, s32[1,8,4]{2,1,0:T(8,128)} %copy.12.nbr_ref, s32[1,8]{1,0:T(1,128)} %cnt_ref.3, bf16[4,3,256,640]{3,2,1,0:T(8,128)(2,1)} %all-to-all-done.held.got_ref), custom_call_target="tpu_custom_call" | custom-call | flops 1024 | bytes 1024 | tf_op jit(solution)/shard_map/attend/pallas_call | solution.py:200
  85.0 1.5 collective-permute-start
  86.5 17.7 %collective-permute-done.1.refs_1_ = bf16[256,2560]{1,0:T(8,128)(2,1)} collective-permute-done((bf16[256,2560]{1,0:T(8,128)(2,1)}, bf16[256,2560]{1,0:T(8,128)(2,1)}, u32[]{:S(2)}, u32[]{:S(2)}) %collective-permute-start.1) | collective-permute-done | bytes 1310752 | tf_op jit(solution)/shard_map/ppermute | solution.py:426
  104.2 1.5 collective-permute-start.4
  105.7 7.4 %project_back.4.rest_0_ = bf16[768,640]{1,0:T(8,128)(2,1)} custom-call(bf16[256,2560]{1,0:T(8,128)(2,1)} %copy-done.3, bf16[256,2560]{1,0:T(8,128)(2,1)} %collective-permute-done.1.refs_1_, bf16[256,2560]{1,0:T(8,128)(2,1)} %collective-permute-done.2.refs_2_, bf16[640,2560]{1,0:T(8,128)(2,1)} %all-gather.3.cloned.1.call-done.refs_3_.wa_ref.refs_1_), custom_call_target="tpu_custom_call" | custom-call | flops 1024 | bytes 1024 | tf_op jit(solution)/shard_map/project_back/pallas_call | solution.py:361
  113.2 7.3 %project_back.5 = bf16[768,640]{1,0:T(8,128)(2,1)} custom-call(bf16[256,2560]{1,0:T(8,128)(2,1)} %copy-done.3, bf16[256,2560]{1,0:T(8,128)(2,1)} %collective-permute-done.1.refs_1_, bf16[256,2560]{1,0:T(8,128)(2,1)} %collective-permute-done.2.refs_2_, bf16[640,2560]{1,0:T(8,128)(2,1)} %all-gather.5.cloned.1.call-done.refs_3_.wb_ref.refs_1_), custom_call_target="tpu_custom_call" | custom-call | flops 1024 | bytes 1024 | tf_op jit(solution)/shard_map/project_back/pallas_call | solution.py:361
  120.5 10.0 %collective-permute-done.b_ref = bf16[1024,640]{1,0:T(8,128)(2,1)S(1)} collective-permute-done((bf16[1024,640]{1,0:T(8,128)(2,1)}, bf16[1024,640]{1,0:T(8,128)(2,1)S(1)}, u32[]{:S(2)}, u32[]{:S(2)}) %collective-permute-start) | collective-permute-done | bytes 1310752 | tf_op jit(solution)/shard_map/ppermute | solution.py:426
  131.5 4.5 %project.4 = bf16[512,1024]{1,0:T(8,128)(2,1)} custom-call(bf16[1024,640]{1,0:T(8,128)(2,1)} %get-tuple-element.54.a_ref, bf16[1024,640]{1,0:T(8,128)(2,1)} %copy-done.2, bf16[640,2560]{1,0:T(8,128)(2,1)} %all-gather.3.cloned.1.call-done.refs_3_.wa_ref.refs_1_, bf16[640,2560]{1,0:T(8,128)(2,1)} %all-gather.5.cloned.1.call-done.refs_3_.wb_ref.refs_1_), custom_call_target="tpu_custom_call" | custom-call | flops 1024 | bytes 1024 | tf_op jit(solution)/shard_map/project/pallas_call | solution.py:322
  136.1 1.5 collective-permute-start.5
  138.0 4.3 %project_back.6 = bf16[256,640]{1,0:T(8,128)(2,1)} custom-call(bf16[256,2560]{1,0:T(8,128)(2,1)} %collective-permute-done.4.refs_0_.refs_3_, bf16[640,2560]{1,0:T(8,128)(2,1)} %all-gather.5.cloned.1.call-done.refs_3_.wb_ref.refs_1_), custom_call_target="tpu_custom_call" | custom-call | flops 1024 | bytes 1024 | tf_op jit(solution)/shard_map/project_back/pallas_call | solution.py:361
  142.4 1.6 collective-permute-start.10
  144.0 5.9 %project.5 = bf16[512,1536]{1,0:T(8,128)(2,1)} custom-call(bf16[1024,640]{1,0:T(8,128)(2,1)} %get-tuple-element.54.a_ref, bf16[1024,640]{1,0:T(8,128)(2,1)} %copy-done.2, bf16[640,2560]{1,0:T(8,128)(2,1)} %all-gather.3.cloned.1.call-done.refs_3_.wa_ref.refs_1_, bf16[640,2560]{1,0:T(8,128)(2,1)} %all-gather.5.cloned.1.call-done.refs_3_.wb_ref.refs_1_), custom_call_target="tpu_custom_call" | custom-call | flops 1024 | bytes 1024 | tf_op jit(solution)/shard_map/project/pallas_call | solution.py:322
  149.9 4.3 %project_back.7.rest_1_ = bf16[256,640]{1,0:T(8,128)(2,1)} custom-call(bf16[256,2560]{1,0:T(8,128)(2,1)} %collective-permute-done.4.refs_0_.refs_3_, bf16[640,2560]{1,0:T(8,128)(2,1)} %all-gather.3.cloned.1.call-done.refs_3_.wa_ref.refs_1_), custom_call_target="tpu_custom_call" | custom-call | flops 1024 | bytes 1024 | tf_op jit(solution)/shard_map/project_back/pallas_call | solution.py:361
  154.2 11.7 %weight_grad.1 = bf16[8,2,80,2560]{3,2,1,0:T(8,128)(2,1)} custom-call(bf16[640,1024]{1,0:T(8,128)(2,1)} %get-tuple-element.37.at, bf16[1024,640]{1,0:T(8,128)(2,1)} %copy-done.2, bf16[256,2560]{1,0:T(8,128)(2,1)} %copy-done.3, bf16[256,2560]{1,0:T(8,128)(2,1)} %collective-permute-done.1.refs_1_, bf16[256,2560]{1,0:T(8,128)(2,1)} %collective-permute-done.2.refs_2_, ...), custom_call_target="tpu_custom_call" | custom-call | flops 1024 | bytes 1024 | tf_op jit(solution)/shard_map/weight_grad/pallas_call | solution.py:398
  169.7 4.8 %project.6 = (bf16[256,1024]{1,0:T(8,128)(2,1)}, bf16[256,1024]{1,0:T(8,128)(2,1)}) custom-call(bf16[1024,640]{1,0:T(8,128)(2,1)} %get-tuple-element.54.a_ref, bf16[1024,640]{1,0:T(8,128)(2,1)} %copy-done.2, bf16[640,2560]{1,0:T(8,128)(2,1)} %all-gather.3.cloned.1.call-done.refs_3_.wa_ref.refs_1_, ...), custom_call_target="tpu_custom_call" | custom-call | flops 1024 | bytes 1024 | tf_op jit(solution)/shard_map/project/pallas_call | solution.py:322
  175.1 15.1 %attend_back.1 = (bf16[3,256,640]{2,1,0:T(8,128)(2,1)}, bf16[3,256,640]{2,1,0:T(8,128)(2,1)}, bf16[3,256,640]{2,1,0:T(8,128)(2,1)}, bf16[3,256,640]{2,1,0:T(8,128)(2,1)}) custom-call(s32[1]{0:T(128)} %bitcast.1.me_ref, s32[1,8,4]{2,1,0:T(8,128)} %copy.12.nbr_ref, s32[1,8]{1,0:T(1,128)} %cnt_ref.3, bf16[4,3,256,640]{3,2,1,0:T(8,128)(2,1)} %all-to-all-done.held.got_ref, ...), custom_call_target="tpu_custom_call" | custom-call | flops 1024 | bytes 1024 | tf_op jit(solution)/shard_map/attend_back/pallas_call | solution.py:279
  190.2 1.5 collective-permute-start.11
  193.7 12.9 %collective-permute-done.7.rest_0_ = bf16[512,1536]{1,0:T(8,128)(2,1)} collective-permute-done((bf16[512,1536]{1,0:T(8,128)(2,1)S(1)}, bf16[512,1536]{1,0:T(8,128)(2,1)}, u32[]{:S(2)}, u32[]{:S(2)}) %collective-permute-start.7) | collective-permute-done | bytes 1572896 | tf_op jit(solution)/shard_map/ppermute | solution.py:426
  206.6 6.3 %project.7 = (bf16[256,1536]{1,0:T(8,128)(2,1)}, bf16[256,1536]{1,0:T(8,128)(2,1)}) custom-call(bf16[1024,640]{1,0:T(8,128)(2,1)} %get-tuple-element.54.a_ref, bf16[1024,640]{1,0:T(8,128)(2,1)} %copy-done.2, bf16[640,2560]{1,0:T(8,128)(2,1)} %all-gather.3.cloned.1.call-done.refs_3_.wa_ref.refs_1_, ...), custom_call_target="tpu_custom_call" | custom-call | flops 1024 | bytes 1024 | tf_op jit(solution)/shard_map/project/pallas_call | solution.py:322
  213.6 25.8 %reduce-scatter.2.cloned.1.call-done = bf16[160,2560]{1,0:T(8,128)(2,1)} async-done(((bf16[1280,2560]{1,0:T(8,128)(2,1)}), bf16[160,2560]{1,0:T(8,128)(2,1)}) %reduce-scatter.2.cloned.1.call-update) | async-done | bytes 819216 | tf_op jit(solution)/shard_map/reduce_scatter | solution.py:491
  240.6 1.5 collective-permute-start.14
  242.1 2.9 %collective-permute-done.12.rest_2_ = bf16[3,256,640]{2,1,0:T(8,128)(2,1)} collective-permute-done((bf16[3,256,640]{2,1,0:T(8,128)(2,1)}, bf16[3,256,640]{2,1,0:T(8,128)(2,1)}, u32[]{:S(2)}, u32[]{:S(2)}) %collective-permute-start.12) | collective-permute-done | bytes 983072 | tf_op jit(solution)/shard_map/ppermute | solution.py:426
  245.0 3.5 %unpack.1 = (bf16[1,256,2560]{2,1,0:T(8,128)(2,1)}, bf16[1,256,2560]{2,1,0:T(8,128)(2,1)}, bf16[1,256,2560]{2,1,0:T(8,128)(2,1)}) custom-call(s32[1]{0:T(128)} %bitcast.1.me_ref, bf16[3,256,640]{2,1,0:T(8,128)(2,1)} %get-tuple-element.58.rest_0_, bf16[3,256,640]{2,1,0:T(8,128)(2,1)} %collective-permute-done.11.rest_1_, ...), custom_call_target="tpu_custom_call" | custom-call | flops 1024 | bytes 1024 | tf_op jit(solution)/shard_map/unpack/pallas_call | solution.py:95
  248.5 4.7 %collective-permute-done.8.rest_3_ = bf16[256,1536]{1,0:T(8,128)(2,1)S(1)} collective-permute-done((bf16[256,1536]{1,0:T(8,128)(2,1)}, bf16[256,1536]{1,0:T(8,128)(2,1)S(1)}, u32[]{:S(2)}, u32[]{:S(2)}) %collective-permute-start.8) | collective-permute-done | bytes 786464 | tf_op jit(solution)/shard_map/ppermute | solution.py:426
  254.0 2.7 %join.1 = bf16[1,256,5120]{2,1,0:T(8,128)(2,1)} custom-call(s32[1]{0:T(128)} %bitcast.low_ref, bf16[256,1024]{1,0:T(8,128)(2,1)} %get-tuple-element.52.rest_0_, bf16[256,1536]{1,0:T(8,128)(2,1)} %get-tuple-element.55.rest_1_, bf16[256,1024]{1,0:T(8,128)(2,1)} %copy-done.8, bf16[256,1536]{1,0:T(8,128)(2,1)} %copy-done.7), custom_call_target="tpu_custom_call" | custom-call | flops 1024 | bytes 1024 | tf_op jit(solution)/shard_map/join/pallas_call | solution.py:126
  256.7 1.8 collective-permute-done.14
  (53 shorter events, 14.5 us)
Async XLA Ops:
  7.2 3.7 %copy-start = (bf16[80,5120]{1,0:T(8,128)(2,1)S(1)}, bf16[80,5120]{1,0:T(8,128)(2,1)}, u32[]{:S(2)}) copy-start(bf16[80,5120]{1,0:T(8,128)(2,1)} %param.12) | copy-start | bytes 2457604
  7.2 64.1 %all-gather.3.cloned.1.call-start = ((), (), s32[]{:S(2)}) async-start(), calls=%async_computation.2 | async-start | bytes 3686400 | tf_op jit(solution)/shard_map/all_gather | solution.py:447
  11.7 59.6 %all-to-all-start = ((bf16[4,3,256,640]{3,2,1,0:T(8,128)(2,1)}), bf16[4,3,256,640]{3,2,1,0:T(8,128)(2,1)}, u32[]{:S(2)}, u32[]{:S(2)}) async-start(bf16[4,3,256,640]{3,2,1,0:T(8,128)(2,1)} %pack.1), calls=%async_computation | async-start | bytes 7864320 | tf_op jit(solution)/shard_map/all_to_all | solution.py:441
  16.9 96.3 %all-gather.5.cloned.1.call-start = ((), (), s32[]{:S(2)}) async-start(), calls=%async_computation.3 | async-start | bytes 3686400 | tf_op jit(solution)/shard_map/all_gather | solution.py:452
  16.9 57.3 %copy-start.11 = (s32[1,8,4]{1,2,0:T(4,128)S(1)}, s32[1,8,4]{1,2,0:T(4,128)}, u32[]{:S(2)}) copy-start(s32[1,8,4]{1,2,0:T(4,128)} %param.10) | copy-start | bytes 388
  19.8 65.1 %copy-start.3 = (bf16[256,2560]{1,0:T(8,128)(2,1)}, bf16[256,2560]{1,0:T(8,128)(2,1)S(1)}, u32[]{:S(2)}) copy-start(bf16[256,2560]{1,0:T(8,128)(2,1)S(1)} %get-tuple-element.68.refs_0_) | copy-start | bytes 3932164
  19.9 51.4 %collective-permute-start.3 = (bf16[80,2560]{1,0:T(8,128)(2,1)S(1)}, bf16[80,2560]{1,0:T(8,128)(2,1)S(1)}, u32[]{:S(2)}, u32[]{:S(2)}) collective-permute-start(bf16[80,2560]{1,0:T(8,128)(2,1)S(1)} %constant_dynamic-slice_fusion), channel_id=1, source_target_pairs={{0,8},{8,0},{16,24},{24,16},{1,9},{9,1},{17,25},{25,17},{2,10},{10... | collective-permute-start | bytes 1228808 | tf_op jit(solution)/shard_map/ppermute | solution.py:426
  71.3 0.8 copy-start.9
  72.1 167.3 %reduce-scatter.2.cloned.1.call-start = ((), (), s32[]{:S(2)}) async-start(), calls=%async_computation.4 | async-start | bytes 7372800 | tf_op jit(solution)/shard_map/reduce_scatter | solution.py:491
  72.1 32.1 %collective-permute-start.1 = (bf16[256,2560]{1,0:T(8,128)(2,1)}, bf16[256,2560]{1,0:T(8,128)(2,1)}, u32[]{:S(2)}, u32[]{:S(2)}) collective-permute-start(bf16[256,2560]{1,0:T(8,128)(2,1)} %get-tuple-element.67), channel_id=1, source_target_pairs={{0,8},{8,0},{16,24},{24,16},{1,9},{9,1},{17,25},{25,17},{2,10},{10... | collective-permute-start | bytes 3932168 | tf_op jit(solution)/shard_map/ppermute | solution.py:426
  72.2 33.5 %collective-permute-start.2 = (bf16[256,2560]{1,0:T(8,128)(2,1)S(1)}, bf16[256,2560]{1,0:T(8,128)(2,1)}, u32[]{:S(2)}, u32[]{:S(2)}) collective-permute-start(bf16[256,2560]{1,0:T(8,128)(2,1)S(1)} %get-tuple-element.68.refs_0_), channel_id=1, source_target_pairs={{0,16},{8,24},{16,0},{24,8},{1,17},{9,25},{17,1},{25,9},{2,18},{10... | collective-permute-start | bytes 3932168 | tf_op jit(solution)/shard_map/ppermute | solution.py:426
  85.0 45.5 %collective-permute-start = (bf16[1024,640]{1,0:T(8,128)(2,1)}, bf16[1024,640]{1,0:T(8,128)(2,1)S(1)}, u32[]{:S(2)}, u32[]{:S(2)}) collective-permute-start(bf16[1024,640]{1,0:T(8,128)(2,1)} %get-tuple-element.38), channel_id=1, source_target_pairs={{0,8},{8,0},{16,24},{24,16},{1,9},{9,1},{17,25},{25,17},{2,10},{10... | collective-permute-start | bytes 3932168 | tf_op jit(solution)/shard_map/ppermute | solution.py:426
  104.2 33.8 %collective-permute-start.4 = (bf16[256,2560]{1,0:T(8,128)(2,1)}, bf16[256,2560]{1,0:T(8,128)(2,1)}, u32[]{:S(2)}, u32[]{:S(2)}) collective-permute-start(bf16[256,2560]{1,0:T(8,128)(2,1)} %collective-permute-done.1.refs_1_), channel_id=1, source_target_pairs={{0,16},{8,24},{16,0},{24,8},{1,17},{9,25},{17,1},{25,9},{2,18},{10... | collective-permute-start | bytes 3932168 | tf_op jit(solution)/shard_map/ppermute | solution.py:426
  130.5 1.1 copy-start.2
  136.1 30.6 %collective-permute-start.5 = (bf16[512,1024]{1,0:T(8,128)(2,1)}, bf16[512,1024]{1,0:T(8,128)(2,1)S(1)}, u32[]{:S(2)}, u32[]{:S(2)}) collective-permute-start(bf16[512,1024]{1,0:T(8,128)(2,1)} %project.4), channel_id=1, source_target_pairs={{0,16},{8,24},{16,0},{24,8},{1,17},{9,25},{17,1},{25,9},{2,18},{10... | collective-permute-start | bytes 3145736 | tf_op jit(solution)/shard_map/ppermute | solution.py:426
  137.5 29.1 %collective-permute-start.9 = (bf16[768,640]{1,0:T(8,128)(2,1)}, bf16[768,640]{1,0:T(8,128)(2,1)S(1)}, u32[]{:S(2)}, u32[]{:S(2)}) collective-permute-start(bf16[768,640]{1,0:T(8,128)(2,1)} %project_back.5), channel_id=1, source_target_pairs={{0,8},{8,0},{16,24},{24,16},{1,9},{9,1},{17,25},{25,17},{2,10},{10... | collective-permute-start | bytes 2949128 | tf_op jit(solution)/shard_map/ppermute | solution.py:426
  142.4 24.2 %collective-permute-start.10 = (bf16[256,640]{1,0:T(8,128)(2,1)}, bf16[256,640]{1,0:T(8,128)(2,1)S(1)}, u32[]{:S(2)}, u32[]{:S(2)}) collective-permute-start(bf16[256,640]{1,0:T(8,128)(2,1)} %project_back.6), channel_id=1, source_target_pairs={{0,8},{8,0},{16,24},{24,16},{1,9},{9,1},{17,25},{25,17},{2,10},{10... | collective-permute-start | bytes 983048 | tf_op jit(solution)/shard_map/ppermute | solution.py:426
  166.6 0.8 copy-start.10
  166.6 1.0 copy-start.6
  167.4 1.0 copy-start.5
  167.7 1.5 copy-start.4
  169.2 37.4 %collective-permute-start.7 = (bf16[512,1536]{1,0:T(8,128)(2,1)S(1)}, bf16[512,1536]{1,0:T(8,128)(2,1)}, u32[]{:S(2)}, u32[]{:S(2)}) collective-permute-start(bf16[512,1536]{1,0:T(8,128)(2,1)S(1)} %copy-done.4), channel_id=1, source_target_pairs={{0,16},{8,24},{16,0},{24,8},{1,17},{9,25},{17,1},{25,9},{2,18},{10... | collective-permute-start | bytes 4718600 | tf_op jit(solution)/shard_map/ppermute | solution.py:426
  174.5 19.2 %collective-permute-start.6 = (bf16[256,1024]{1,0:T(8,128)(2,1)}, bf16[256,1024]{1,0:T(8,128)(2,1)S(1)}, u32[]{:S(2)}, u32[]{:S(2)}) collective-permute-start(bf16[256,1024]{1,0:T(8,128)(2,1)} %get-tuple-element.53), channel_id=1, source_target_pairs={{0,8},{8,0},{16,24},{24,16},{1,9},{9,1},{17,25},{25,17},{2,10},{10... | collective-permute-start | bytes 1572872 | tf_op jit(solution)/shard_map/ppermute | solution.py:426
  190.2 51.9 %collective-permute-start.11 = (bf16[3,256,640]{2,1,0:T(8,128)(2,1)}, bf16[3,256,640]{2,1,0:T(8,128)(2,1)}, u32[]{:S(2)}, u32[]{:S(2)}) collective-permute-start(bf16[3,256,640]{2,1,0:T(8,128)(2,1)} %get-tuple-element.59), channel_id=1, source_target_pairs={{0,8},{8,0},{16,24},{24,16},{1,9},{9,1},{17,25},{25,17},{2,10},{10... | collective-permute-start | bytes 2949128 | tf_op jit(solution)/shard_map/ppermute | solution.py:426
  191.7 53.3 %collective-permute-start.12 = (bf16[3,256,640]{2,1,0:T(8,128)(2,1)}, bf16[3,256,640]{2,1,0:T(8,128)(2,1)}, u32[]{:S(2)}, u32[]{:S(2)}) collective-permute-start(bf16[3,256,640]{2,1,0:T(8,128)(2,1)} %get-tuple-element.60), channel_id=1, source_target_pairs={{0,16},{8,24},{16,0},{24,8},{1,17},{9,25},{17,1},{25,9},{2,18},{10... | collective-permute-start | bytes 2949128 | tf_op jit(solution)/shard_map/ppermute | solution.py:426
  193.2 51.8 %collective-permute-start.13 = (bf16[3,256,640]{2,1,0:T(8,128)(2,1)}, bf16[3,256,640]{2,1,0:T(8,128)(2,1)}, u32[]{:S(2)}, u32[]{:S(2)}) collective-permute-start(bf16[3,256,640]{2,1,0:T(8,128)(2,1)} %get-tuple-element.61), channel_id=1, source_target_pairs={{0,24},{8,16},{16,8},{24,0},{1,25},{9,17},{17,9},{25,1},{2,26},{10... | collective-permute-start | bytes 2949128 | tf_op jit(solution)/shard_map/ppermute | solution.py:426
  193.7 19.2 %copy-start.8 = (bf16[256,1024]{1,0:T(8,128)(2,1)}, bf16[256,1024]{1,0:T(8,128)(2,1)S(1)}, u32[]{:S(2)}) copy-start(bf16[256,1024]{1,0:T(8,128)(2,1)S(1)} %collective-permute-done.6.rest_2_) | copy-start | bytes 1572868
  213.0 40.1 %collective-permute-start.8 = (bf16[256,1536]{1,0:T(8,128)(2,1)}, bf16[256,1536]{1,0:T(8,128)(2,1)S(1)}, u32[]{:S(2)}, u32[]{:S(2)}) collective-permute-start(bf16[256,1536]{1,0:T(8,128)(2,1)} %get-tuple-element.56), channel_id=1, source_target_pairs={{0,8},{8,0},{16,24},{24,16},{1,9},{9,1},{17,25},{25,17},{2,10},{10... | collective-permute-start | bytes 2359304 | tf_op jit(solution)/shard_map/ppermute | solution.py:426
  240.6 17.9 %collective-permute-start.14 = (bf16[80,2560]{1,0:T(8,128)(2,1)S(1)}, bf16[80,2560]{1,0:T(8,128)(2,1)S(1)}, u32[]{:S(2)}, u32[]{:S(2)}) collective-permute-start(bf16[80,2560]{1,0:T(8,128)(2,1)S(1)} %get-tuple-element.70), channel_id=1, source_target_pairs={{0,8},{8,0},{16,24},{24,16},{1,9},{9,1},{17,25},{25,17},{2,10},{10... | collective-permute-start | bytes 1228808 | tf_op jit(solution)/shard_map/ppermute | solution.py:426
  253.1 0.9 copy-start.7
  254.0 5.9 %copy-start.1 = (bf16[80,5120]{1,0:T(8,128)(2,1)S(1)}, bf16[80,5120]{1,0:T(8,128)(2,1)}, u32[]{:S(2)}) copy-start(bf16[80,5120]{1,0:T(8,128)(2,1)} %param.12) | copy-start | bytes 2457604
Sparse Core Ops, SparseCore 0:
  11.8 42.0 all-gather.2
  72.2 39.8 all-gather.4
  167.8 71.5 reduce-scatter.1

commit v2 on v1

--- a/solution.py
+++ b/solution.py
@@ -69,7 +69,7 @@
         out_specs=ANY,
         scratch_shapes=[pltpu.VMEM((rows, width), BF)] * (3 * n)
         + [pltpu.SemaphoreType.DMA((3 * n,))] * 2,
-        compiler_params=params(60),
+        compiler_params=params(64),
         cost_estimate=COST,
         name="pack",
     )(q, k, v)
@@ -99,7 +99,7 @@
         out_specs=[ANY] * 3,
         scratch_shapes=[pltpu.VMEM(x.shape[1:], BF) for x in parts for _ in range(3)]
         + [pltpu.SemaphoreType.DMA((3 * len(parts),))] * 2,
-        compiler_params=params(60),
+        compiler_params=params(64),
         cost_estimate=LONG,
         name="unpack",
     )(me, *parts)
@@ -130,7 +130,7 @@
         out_specs=ANY,
         scratch_shapes=[pltpu.VMEM(x.shape, BF) for x in parts]
         + [pltpu.SemaphoreType.DMA((len(parts),))] * 2,
-        compiler_params=params(60),
+        compiler_params=params(64),
         cost_estimate=LONG,
         name="join",
     )(low, *parts)
@@ -203,7 +203,7 @@
         in_specs=[SMEM] * 3 + [vm],
         out_specs=[vm] * 3,
         scratch_shapes=[pltpu.VMEM((nbr.shape[2] * BLK, width), BF)] * 2,
-        compiler_params=params(60),
+        compiler_params=params(64),
         cost_estimate=COST,
         name="attend",
     )(me, nbr, cnt, got)
@@ -292,44 +292,69 @@
             pltpu.SemaphoreType.DMA,
             pltpu.SemaphoreType.DMA((5,)),
         ],
-        compiler_params=params(60),
+        compiler_params=params(64),
         cost_estimate=COST,
         name="attend_back",
     )(me, nbr, cnt, got, *terms)
 
 
-def project_kernel(a_ref, b_ref, wa_ref, wb_ref, *rest):
-    y = dot(a_ref[...], wa_ref[...]) + dot(b_ref[...], wb_ref[...])
+def project_own_kernel(a_ref, w_ref, o_ref):
+    o_ref[...] = dot(a_ref[...], w_ref[...])
+
+
+def project_own(a, w, tile=512):
+    rows, depth = a.shape
+    cols = w.shape[1]
+    return pl.pallas_call(
+        project_own_kernel,
+        grid=(cols // tile,),
+        out_shape=sds((rows, cols), F32),
+        in_specs=[
+            pl.BlockSpec((rows, depth), lambda j: (0, 0)),
+            pl.BlockSpec((depth, tile), lambda j: (0, j)),
+        ],
+        out_specs=pl.BlockSpec((rows, tile), lambda j: (0, j)),
+        compiler_params=params(64),
+        cost_estimate=COST,
+        name="project_own",
+    )(a, w)
+
+
+def project_kernel(own_ref, b_ref, w_ref, *rest):
+    y = own_ref[...] + dot(b_ref[...], w_ref[...])
     if len(rest) == 1:
         rest[0][...] = y.astype(BF)
         return
-    far_ref, own_ref, pair_ref = rest
+    far_ref, own_out, pair_out = rest
     y = (y + far_ref[...].astype(F32)).astype(BF)
-    rows = own_ref.shape[0]
-    own_ref[...] = y[:rows]
-    pair_ref[...] = y[rows:]
-
-
-def project(a, b, wa, wb, begin, end, far=None, tile=512):
-    rows, depth = a.shape
+    rows = own_out.shape[0]
+    own_out[...] = y[:rows]
+    pair_out[...] = y[rows:]
+
+
+def project(own, b, w, begin, end, far=None, tile=512):
+    rows, depth = b.shape
     rows //= 2
     cols = end - begin
     skip = begin // tile
     near = far is not None
-    left = pl.BlockSpec((rows, depth), lambda j: (0 if near else 1, 0))
-    right = pl.BlockSpec((depth, tile), lambda j: (0, skip + j))
+    half = 0 if near else 1
     out = rows // 2 if near else rows
     return pl.pallas_call(
         project_kernel,
         grid=(cols // tile,),
         out_shape=[sds((out, cols))] * (2 if near else 1),
-        in_specs=[left, left, right, right]
+        in_specs=[
+            pl.BlockSpec((rows, tile), lambda j: (half, skip + j)),
+            pl.BlockSpec((rows, depth), lambda j: (half, 0)),
+            pl.BlockSpec((depth, tile), lambda j: (0, skip + j)),
+        ]
         + [pl.BlockSpec((rows, tile), lambda j: (0, j))] * int(near),
         out_specs=[pl.BlockSpec((out, tile), lambda j: (0, j))] * (2 if near else 1),
-        compiler_params=params(60),
+        compiler_params=params(64),
         cost_estimate=LONG if near else COST,
         name="project",
-    )(a, b, wa, wb, *([far] if near else []))
+    )(own, b, w, *([far] if near else []))
 
 
 def project_back_kernel(n, m, order, *refs):
@@ -368,13 +393,39 @@
             pltpu.VMEM((m, width, cols), BF),
             pltpu.SemaphoreType.DMA((n + m,)),
         ],
-        compiler_params=params(60),
+        compiler_params=params(64),
         cost_estimate=COST,
         name="project_back",
     )(*ds, *ws)
 
 
-def weight_kernel(n, at, b_ref, *refs):
+def weight_own_kernel(n, at, *refs):
+    ds, o_ref, d = refs[:n], refs[n], refs[n + 1]
+    rows = ds[0].shape[0]
+    for r, piece in enumerate(ds):
+        d[r * rows : (r + 1) * rows] = piece[...]
+    o_ref[...] = dot(at[...], d[...])
+
+
+def weight_own(at, ds, tile=512):
+    n = len(ds)
+    width = at.shape[0]
+    rows, cols = ds[0].shape
+    return pl.pallas_call(
+        functools.partial(weight_own_kernel, n),
+        grid=(cols // tile,),
+        out_shape=sds((width, cols), F32),
+        in_specs=[pl.BlockSpec((width, n * rows), lambda j: (0, 0))]
+        + [pl.BlockSpec((rows, tile), lambda j: (0, j))] * n,
+        out_specs=pl.BlockSpec((width, tile), lambda j: (0, j)),
+        scratch_shapes=[pltpu.VMEM((n * rows, tile), BF)],
+        compiler_params=params(64),
+        cost_estimate=COST,
+        name="weight_own",
+    )(at, *ds)
+
+
+def weight_kernel(n, done_ref, at, b_ref, *refs):
     ds, o_ref, bt, d = refs[:n], refs[n], refs[n + 1], refs[n + 2]
     rows = ds[0].shape[0]
 
@@ -384,12 +435,12 @@
 
     for r, piece in enumerate(ds):
         d[r * rows : (r + 1) * rows] = piece[...]
-    for i, t in enumerate((at, bt)):
-        out = dot(t[...], d[...]).astype(BF)
-        o_ref[:, i] = out.reshape(o_ref.shape[0], *o_ref.shape[2:])
-
-
-def weight_grad(at, b, ds, owners, tile=512):
+    own = done_ref[...] + dot(at[...], ds[n - 1][...])
+    for i, out in enumerate((own, dot(bt[...], d[...]))):
+        o_ref[:, i] = out.astype(BF).reshape(o_ref.shape[0], *o_ref.shape[2:])
+
+
+def weight_grad(done, at, b, ds, owners, tile=512):
     n = len(ds)
     tokens, width = b.shape
     rows, cols = ds[0].shape
@@ -400,16 +451,17 @@
         grid=(cols // tile,),
         out_shape=sds((apart, 2, width // apart, cols)),
         in_specs=[
-            pl.BlockSpec((width, tokens), lambda j: (0, 0)),
+            pl.BlockSpec((width, tile), lambda j: (0, j)),
+            pl.BlockSpec((width, rows), lambda j: (0, n - 1)),
             pl.BlockSpec((tokens, width), lambda j: (0, 0)),
         ]
         + [pl.BlockSpec((rows, tile), lambda j: (0, j))] * n,
         out_specs=pl.BlockSpec((apart, 2, width // apart, tile), lambda j: (0, 0, 0, j)),
         scratch_shapes=[pltpu.VMEM((width, tokens), BF), pltpu.VMEM((tokens, tile), BF)],
-        compiler_params=params(60),
+        compiler_params=params(64),
         cost_estimate=COST,
         name="weight_grad",
-    )(at, b, *ds)
+    )(done, at, b, *ds)
     if apart == 1:
         out = out.reshape(2, owners, some, cols).swapaxes(0, 1)
     return out.reshape(2 * width, cols)
@@ -456,24 +508,26 @@
 
     attn, swapped, attn_t = attend(me, neighbours, counts, got, scale)
     attn_pair = to(swapped, 1)
-    d3 = to(after(d1, attn), 2)
+    y_own = project_own(after(attn, swapped), w_a)
+    d3 = to(after(d1, y_own), 2)
 
     (own_0,) = project_back([d0, d1, d2], [w_a], ((0, 1, 2),))
     (sent_0,) = project_back([d0, after(d1, own_0), d2], [w_b], ((1, 0, 2),))
     pair_0 = to(sent_0, 1)
-    attn_pair = after(attn_pair, sent_0)
+    gw_own = weight_own(after(attn_t, sent_0), [d0, d1, d2])
+    attn_pair = after(attn_pair, gw_own)
 
     near_cut = half * 2 // 5
     ranges = [(0, near_cut), (near_cut, half)]
-    far_0 = project(attn, attn_pair, w_a, w_b, *ranges[0])[0]
+    far_0 = project(y_own, attn_pair, w_b, *ranges[0])[0]
     (sent_1,) = project_back([after(d3, far_0)], [w_b], ((0,),))
     pair_1 = to(sent_1, 1)
-    far_1 = project(attn, after(attn_pair, sent_1), w_a, w_b, *ranges[1])[0]
+    far_1 = project(y_own, after(attn_pair, sent_1), w_b, *ranges[1])[0]
     after_far = after(attn_pair, far_1)
     y_far = [to(far_0, 2), to(far_1, 2)]
     (own_1,) = project_back([after(d3, after_far)], [w_a], ((0,),))
 
-    gw = weight_grad(attn_t, after(after_far, own_1), [d0, d1, d2, d3], owners)
+    gw = weight_grad(gw_own, attn_t, after(after_far, own_1), [d0, d1, d2, d3], owners)
 
     terms = [own_0, after(own_1, gw), pair_0, pair_1]
     grads = attend_back(me, neighbours, counts, got, terms, 0, attn.shape[1], scale)
@@ -481,11 +535,10 @@
 
     ys, y_pair, last = [], [], gw
     for c, far in zip(ranges, y_far):
-        ys.append(project(after(attn, last), attn_pair, w_a, w_b, *c, far))
+        ys.append(project(y_own, after(attn_pair, last), w_b, *c, far))
         y_pair.append(to(ys[-1][1], 1))
         last = y_pair[-1]
-    y_own = [y[0] for y in ys]
-    out_y = join(low.astype(jnp.int32)[None], y_own, y_pair)
+    out_y = join(low.astype(jnp.int32)[None], [y[0] for y in ys], y_pair)
     grad_q, grad_k, grad_v = unpack(me, [back])
 
     gw = lax.psum_scatter(after(gw, y_far[0], pair_0, pair_1), "zero", scatter_dimension=0, tiled=True)

time: 268 us -> 264 us (0.985)
  waiting for transfers between devices: 125 us -> 108 us
  Pallas kernels: 91.6 us -> 107 us
  local copies, waits for them, and re-layouts: 10.9 us -> 7.03 us
    pallas_call x0 -> x2, Pallas kernels: none -> 17.2 us  [the longest x1 9.19 us: project_own(): pl.pallas_call(project_own_kernel, grid=(cols // tile,), out_shape=sds((r...]
    ppermute x15, waiting for transfers between devices: 99.3 us -> 83.4 us  [to(): return lax.ppermute(x, 'seq', [(i, i ^ r) for i in range(n)])]
    unnamed x25 -> x9, local copies, waits for them, and re-layouts: 5.93 us -> 1.44 us
    pallas_call x4, Pallas kernels: 21.6 us -> 18.7 us  [project(): pl.pallas_call(project_kernel, grid=(cols // tile,), out_shape=[sds((out,...]
  transfers between devices with their start and end apart: 19 -> 19, of which waited for: 9 -> 9; matrix products, arithmetic and copies ran while one was open for 2% -> 2% of each run, Pallas kernels for 33% -> 40%
where the time goes in v2:
time: 264 us; the launch traced here: 262 us
  waiting for transfers between devices  108 us (41%)
  Pallas kernels  107 us (41%)
  starting transfers between devices  23 us (9%)
  between operations  13.9 us (5%)
  local copies, waits for them, and re-layouts  7.03 us (3%)
  other arithmetic  2.73 us (1%)
    ppermute x15, waiting for transfers between devices, to(): return lax.ppermute(x, 'seq', [(i, i ^ r) for i in range(n)])  83.4 us
    reduce_scatter x1, waiting for transfers between devices, on_device(): lax.psum_scatter(after(gw, y_far[0], pair_0, pair_1), 'zero', scatter_dim...  24.7 us
    pallas_call x4, Pallas kernels, project_back(): pl.pallas_call(functools.partial(project_back_kernel, n, m, order), out_s...  23.3 us
    pallas_call x4, Pallas kernels, project(): pl.pallas_call(project_kernel, grid=(cols // tile,), out_shape=[sds((out,...  18.7 us
    ppermute x15, starting transfers between devices, to(): return lax.ppermute(x, 'seq', [(i, i ^ r) for i in range(n)])  17.5 us
    pallas_call x1, Pallas kernels, attend_back(): pl.pallas_call(functools.partial(bwd_kernel, begin, nbr.shape[2], scale),...  16.1 us
    pallas_call x1, Pallas kernels, weight_grad(): pl.pallas_call(functools.partial(weight_kernel, n), grid=(cols // tile,),...  11.7 us
    pallas_call x1, Pallas kernels, attend(): pl.pallas_call(functools.partial(fwd_kernel, width // HD, nbr.shape[2], s...  10.6 us
  transfers between devices with their start and end apart: 19, of which 9 were waited for; matrix products, arithmetic and copies ran while one was open for 2% of the time, Pallas kernels for 40%

profile of v2, /device:TPU:0, one launch (start us, length us, event | category | flops | bytes accessed | tf_op | source)
XLA Modules:
  0.0 262.1 jit_solution(2157038691972004630)
XLA Ops:
  7.2 3.6 %pack.1 = bf16[4,3,256,640]{3,2,1,0:T(8,128)(2,1)} custom-call(bf16[1,256,2560]{2,1,0:T(8,128)(2,1)} %q_ref.1, bf16[1,256,2560]{2,1,0:T(8,128)(2,1)} %k_ref.1, bf16[1,256,2560]{2,1,0:T(8,128)(2,1)} %v_ref.1), custom_call_target="tpu_custom_call" | custom-call | flops 1024 | bytes 1024 | tf_op jit(solution)/shard_map/pack/pallas_call | solution.py:65
  10.8 1.8 constant_dynamic-slice_fusion.1
  12.6 5.4 %all-to-all-start = ((bf16[4,3,256,640]{3,2,1,0:T(8,128)(2,1)}), bf16[4,3,256,640]{3,2,1,0:T(8,128)(2,1)}, u32[]{:S(2)}, u32[]{:S(2)}) async-start(bf16[4,3,256,640]{3,2,1,0:T(8,128)(2,1)} %pack.1), calls=%async_computation | async-start | bytes 7864320 | tf_op jit(solution)/shard_map/all_to_all | solution.py:493
  18.1 1.7 dynamic-slice_bitcast_fusion
  19.8 2.8 %collective-permute-start.3 = (bf16[80,2560]{1,0:T(8,128)(2,1)S(1)}, bf16[80,2560]{1,0:T(8,128)(2,1)S(1)}, u32[]{:S(2)}, u32[]{:S(2)}) collective-permute-start(bf16[80,2560]{1,0:T(8,128)(2,1)S(1)} %constant_dynamic-slice_fusion), channel_id=1, source_target_pairs={{0,8},{8,0},{16,24},{24,16},{1,9},{9,1},{17,25},{25,17},{2,10},{10... | collective-permute-start | bytes 1228808 | tf_op jit(solution)/shard_map/ppermute | solution.py:478
  22.5 50.0 %collective-permute-done.3 = bf16[80,2560]{1,0:T(8,128)(2,1)S(1)} collective-permute-done((bf16[80,2560]{1,0:T(8,128)(2,1)S(1)}, bf16[80,2560]{1,0:T(8,128)(2,1)S(1)}, u32[]{:S(2)}, u32[]{:S(2)}) %collective-permute-start.3) | collective-permute-done | bytes 409632 | tf_op jit(solution)/shard_map/ppermute | solution.py:478
  73.4 1.9 collective-permute-start.2
  76.0 10.6 %attend.1 = (bf16[1024,640]{1,0:T(8,128)(2,1)}, bf16[1024,640]{1,0:T(8,128)(2,1)}, bf16[640,1024]{1,0:T(8,128)(2,1)}) custom-call(s32[1]{0:T(128)} %bitcast.1.me_ref, s32[1,8,4]{2,1,0:T(8,128)} %copy.12.nbr_ref, s32[1,8]{1,0:T(1,128)} %cnt_ref.3, bf16[4,3,256,640]{3,2,1,0:T(8,128)(2,1)} %all-to-all-done.held.got_ref), custom_call_target="tpu_custom_call" | custom-call | flops 1024 | bytes 1024 | tf_op jit(solution)/shard_map/attend/pallas_call | solution.py:200
  88.1 9.2 %project_own.1.own_ref = f32[1024,2560]{1,0:T(8,128)} custom-call(bf16[1024,640]{1,0:T(8,128)(2,1)} %get-tuple-element.40.a_ref, bf16[640,2560]{1,0:T(8,128)(2,1)} %all-gather.3.cloned.1.call-done.w_ref.refs_3_.refs_1_), custom_call_target="tpu_custom_call" | custom-call | flops 1024 | bytes 1024 | tf_op jit(solution)/shard_map/project_own/pallas_call | solution.py:308
  97.3 8.1 %collective-permute-done.1.refs_1_ = bf16[256,2560]{1,0:T(8,128)(2,1)} collective-permute-done((bf16[256,2560]{1,0:T(8,128)(2,1)}, bf16[256,2560]{1,0:T(8,128)(2,1)}, u32[]{:S(2)}, u32[]{:S(2)}) %collective-permute-start.1) | collective-permute-done | bytes 1310752 | tf_op jit(solution)/shard_map/ppermute | solution.py:478
  106.9 7.4 %project_back.4.rest_0_ = bf16[768,640]{1,0:T(8,128)(2,1)} custom-call(bf16[256,2560]{1,0:T(8,128)(2,1)} %get-tuple-element.72.refs_0_, bf16[256,2560]{1,0:T(8,128)(2,1)} %collective-permute-done.1.refs_1_, bf16[256,2560]{1,0:T(8,128)(2,1)} %collective-permute-done.2.refs_2_, bf16[640,2560]{1,0:T(8,128)(2,1)} %all-gather.3.cloned.1.call-done.w_ref.refs_3_.refs_1_), custom_call_target="tpu_custom_call" | custom-call | flops 1024 | bytes 1024 | tf_op jit(solution)/shard_map/project_back/pallas_call | solution.py:386
  114.3 7.4 %project_back.5 = bf16[768,640]{1,0:T(8,128)(2,1)} custom-call(bf16[256,2560]{1,0:T(8,128)(2,1)} %get-tuple-element.72.refs_0_, bf16[256,2560]{1,0:T(8,128)(2,1)} %collective-permute-done.1.refs_1_, bf16[256,2560]{1,0:T(8,128)(2,1)} %collective-permute-done.2.refs_2_, bf16[640,2560]{1,0:T(8,128)(2,1)} %all-gather.5.cloned.1.call-done.refs_3_.w_ref.refs_1_), custom_call_target="tpu_custom_call" | custom-call | flops 1024 | bytes 1024 | tf_op jit(solution)/shard_map/project_back/pallas_call | solution.py:386
  121.7 8.0 %weight_own.1.done_ref = f32[640,2560]{1,0:T(8,128)} custom-call(bf16[640,1024]{1,0:T(8,128)(2,1)} %get-tuple-element.47.at, bf16[256,2560]{1,0:T(8,128)(2,1)} %get-tuple-element.72.refs_0_, bf16[256,2560]{1,0:T(8,128)(2,1)} %collective-permute-done.1.refs_1_, bf16[256,2560]{1,0:T(8,128)(2,1)} %collective-permute-done.2.refs_2_), custom_call_target="tpu_custom_call" | custom-call | flops 1024 | bytes 1024 | tf_op jit(solution)/shard_map/weight_own/pallas_call | solution.py:414
  129.7 2.1 collective-permute-done.b_ref
  131.8 3.6 %project.4 = bf16[512,1024]{1,0:T(8,128)(2,1)} custom-call(f32[1024,2560]{1,0:T(8,128)} %project_own.1.own_ref, bf16[1024,640]{1,0:T(8,128)(2,1)} %collective-permute-done.b_ref, bf16[640,2560]{1,0:T(8,128)(2,1)} %all-gather.5.cloned.1.call-done.refs_3_.w_ref.refs_1_), custom_call_target="tpu_custom_call" | custom-call | flops 1024 | bytes 1024 | tf_op jit(solution)/shard_map/project/pallas_call | solution.py:343
  137.3 4.3 %project_back.6 = bf16[256,640]{1,0:T(8,128)(2,1)} custom-call(bf16[256,2560]{1,0:T(8,128)(2,1)} %collective-permute-done.4.refs_0_.refs_3_, bf16[640,2560]{1,0:T(8,128)(2,1)} %all-gather.5.cloned.1.call-done.refs_3_.w_ref.refs_1_), custom_call_target="tpu_custom_call" | custom-call | flops 1024 | bytes 1024 | tf_op jit(solution)/shard_map/project_back/pallas_call | solution.py:386
  141.6 1.6 collective-permute-start.10
  143.2 5.4 %project.5 = bf16[512,1536]{1,0:T(8,128)(2,1)} custom-call(f32[1024,2560]{1,0:T(8,128)} %project_own.1.own_ref, bf16[1024,640]{1,0:T(8,128)(2,1)} %collective-permute-done.b_ref, bf16[640,2560]{1,0:T(8,128)(2,1)} %all-gather.5.cloned.1.call-done.refs_3_.w_ref.refs_1_), custom_call_target="tpu_custom_call" | custom-call | flops 1024 | bytes 1024 | tf_op jit(solution)/shard_map/project/pallas_call | solution.py:343
  148.5 4.3 %project_back.7.rest_1_ = bf16[256,640]{1,0:T(8,128)(2,1)} custom-call(bf16[256,2560]{1,0:T(8,128)(2,1)} %collective-permute-done.4.refs_0_.refs_3_, bf16[640,2560]{1,0:T(8,128)(2,1)} %all-gather.3.cloned.1.call-done.w_ref.refs_3_.refs_1_), custom_call_target="tpu_custom_call" | custom-call | flops 1024 | bytes 1024 | tf_op jit(solution)/shard_map/project_back/pallas_call | solution.py:386
  152.8 11.7 %weight_grad.1 = bf16[8,2,80,2560]{3,2,1,0:T(8,128)(2,1)} custom-call(f32[640,2560]{1,0:T(8,128)} %weight_own.1.done_ref, bf16[640,1024]{1,0:T(8,128)(2,1)} %get-tuple-element.47.at, bf16[1024,640]{1,0:T(8,128)(2,1)} %collective-permute-done.b_ref, bf16[256,2560]{1,0:T(8,128)(2,1)} %get-tuple-element.72.refs_0_, ...), custom_call_target="tpu_custom_call" | custom-call | flops 1024 | bytes 1024 | tf_op jit(solution)/shard_map/weight_grad/pallas_call | solution.py:449
  166.5 3.9 %project.6 = (bf16[256,1024]{1,0:T(8,128)(2,1)}, bf16[256,1024]{1,0:T(8,128)(2,1)}) custom-call(f32[1024,2560]{1,0:T(8,128)} %project_own.1.own_ref, bf16[1024,640]{1,0:T(8,128)(2,1)} %collective-permute-done.b_ref, bf16[640,2560]{1,0:T(8,128)(2,1)} %all-gather.5.cloned.1.call-done.refs_3_.w_ref.refs_1_, bf16[512,1024]{1,0:T(8,128)(2,1)} %collective-permute-done.5.rest_0_), custom_call_target="tpu_custom_call" | custom-call | flops 1024 | bytes 1024 | tf_op jit(solution)/shard_map/project/pallas_call | solution.py:343
  171.1 16.1 %attend_back.1 = (bf16[3,256,640]{2,1,0:T(8,128)(2,1)}, bf16[3,256,640]{2,1,0:T(8,128)(2,1)}, bf16[3,256,640]{2,1,0:T(8,128)(2,1)}, bf16[3,256,640]{2,1,0:T(8,128)(2,1)}) custom-call(s32[1]{0:T(128)} %bitcast.1.me_ref, s32[1,8,4]{2,1,0:T(8,128)} %copy.12.nbr_ref, s32[1,8]{1,0:T(1,128)} %cnt_ref.3, bf16[4,3,256,640]{3,2,1,0:T(8,128)(2,1)} %all-to-all-done.held.got_ref, ...), custom_call_target="tpu_custom_call" | custom-call | flops 1024 | bytes 1024 | tf_op jit(solution)/shard_map/attend_back/pallas_call | solution.py:279
  187.2 1.6 collective-permute-start.11
  190.7 16.4 %collective-permute-done.7.rest_0_ = bf16[512,1536]{1,0:T(8,128)(2,1)} collective-permute-done((bf16[512,1536]{1,0:T(8,128)(2,1)}, bf16[512,1536]{1,0:T(8,128)(2,1)}, u32[]{:S(2)}, u32[]{:S(2)}) %collective-permute-start.7) | collective-permute-done | bytes 1572896 | tf_op jit(solution)/shard_map/ppermute | solution.py:478
  207.2 5.8 %project.7 = (bf16[256,1536]{1,0:T(8,128)(2,1)}, bf16[256,1536]{1,0:T(8,128)(2,1)}) custom-call(f32[1024,2560]{1,0:T(8,128)} %project_own.1.own_ref, bf16[1024,640]{1,0:T(8,128)(2,1)} %collective-permute-done.b_ref, bf16[640,2560]{1,0:T(8,128)(2,1)} %all-gather.5.cloned.1.call-done.refs_3_.w_ref.refs_1_, bf16[512,1536]{1,0:T(8,128)(2,1)} %collective-permute-done.7.rest_0_), custom_call_target="tpu_custom_call" | custom-call | flops 1024 | bytes 1024 | tf_op jit(solution)/shard_map/project/pallas_call | solution.py:343
  212.9 24.7 %reduce-scatter.2.cloned.1.call-done = bf16[160,2560]{1,0:T(8,128)(2,1)} async-done(((bf16[1280,2560]{1,0:T(8,128)(2,1)}), bf16[160,2560]{1,0:T(8,128)(2,1)}) %reduce-scatter.2.cloned.1.call-update) | async-done | bytes 819216 | tf_op jit(solution)/shard_map/reduce_scatter | solution.py:544
  237.6 2.1 fusion.1
  241.9 3.5 %unpack.1 = (bf16[1,256,2560]{2,1,0:T(8,128)(2,1)}, bf16[1,256,2560]{2,1,0:T(8,128)(2,1)}, bf16[1,256,2560]{2,1,0:T(8,128)(2,1)}) custom-call(s32[1]{0:T(128)} %bitcast.1.me_ref, bf16[3,256,640]{2,1,0:T(8,128)(2,1)} %get-tuple-element.62.rest_0_, bf16[3,256,640]{2,1,0:T(8,128)(2,1)} %collective-permute-done.11.rest_1_, ...), custom_call_target="tpu_custom_call" | custom-call | flops 1024 | bytes 1024 | tf_op jit(solution)/shard_map/unpack/pallas_call | solution.py:95
  245.3 2.4 collective-permute-done.8.rest_3_
  247.7 2.7 %join.1 = bf16[1,256,5120]{2,1,0:T(8,128)(2,1)} custom-call(s32[1]{0:T(128)} %bitcast.low_ref, bf16[256,1024]{1,0:T(8,128)(2,1)} %get-tuple-element.56.rest_0_, bf16[256,1536]{1,0:T(8,128)(2,1)} %get-tuple-element.59.rest_1_, bf16[256,1024]{1,0:T(8,128)(2,1)} %collective-permute-done.6.rest_2_, bf16[256,1536]{1,0:T(8,128)(2,1)} %collective-permute-done.8.rest_3_), custom_call_target="tpu_custom_call" | custom-call | flops 1024 | bytes 1024 | tf_op jit(solution)/shard_map/join/pallas_call | solution.py:126
  250.4 2.4 collective-permute-done.14
  252.8 2.7 %fusion = f32[80,5120]{1,0:T(8,128)} fusion(bf16[80,2560]{1,0:T(8,128)(2,1)} %collective-permute-done.14, bf16[80,2560]{1,0:T(8,128)(2,1)} %get-tuple-element.73, pred[]{:T(512)S(6)} %eq.3), kind=kLoop, calls=%fused_computation.3 | loop fusion | flops 4096000 | bytes 2457601 | tf_op jit(solution)/shard_map/convert_element_type | solution.py:552
  (39 shorter events, 13.3 us)
Async XLA Ops:
  7.2 65.3 %all-gather.3.cloned.1.call-start = ((), (), s32[]{:S(2)}) async-start(), calls=%async_computation.2 | async-start | bytes 3686400 | tf_op jit(solution)/shard_map/all_gather | solution.py:499
  12.6 5.5 %copy-start = (bf16[1,256,5120]{2,1,0:T(8,128)(2,1)S(1)}, bf16[1,256,5120]{2,1,0:T(8,128)(2,1)}, u32[]{:S(2)}) copy-start(bf16[1,256,5120]{2,1,0:T(8,128)(2,1)} %param.13) | copy-start | bytes 7864324
  12.6 59.9 %all-to-all-start = ((bf16[4,3,256,640]{3,2,1,0:T(8,128)(2,1)}), bf16[4,3,256,640]{3,2,1,0:T(8,128)(2,1)}, u32[]{:S(2)}, u32[]{:S(2)}) async-start(bf16[4,3,256,640]{3,2,1,0:T(8,128)(2,1)} %pack.1), calls=%async_computation | async-start | bytes 7864320 | tf_op jit(solution)/shard_map/all_to_all | solution.py:493
  18.0 96.2 %all-gather.5.cloned.1.call-start = ((), (), s32[]{:S(2)}) async-start(), calls=%async_computation.3 | async-start | bytes 3686400 | tf_op jit(solution)/shard_map/all_gather | solution.py:504
  18.1 1.7 copy-start.1
  18.1 57.3 %copy-start.3 = (s32[1,8,4]{1,2,0:T(4,128)S(1)}, s32[1,8,4]{1,2,0:T(4,128)}, u32[]{:S(2)}) copy-start(s32[1,8,4]{1,2,0:T(4,128)} %param.10) | copy-start | bytes 388
  19.8 52.7 %collective-permute-start.3 = (bf16[80,2560]{1,0:T(8,128)(2,1)S(1)}, bf16[80,2560]{1,0:T(8,128)(2,1)S(1)}, u32[]{:S(2)}, u32[]{:S(2)}) collective-permute-start(bf16[80,2560]{1,0:T(8,128)(2,1)S(1)} %constant_dynamic-slice_fusion), channel_id=1, source_target_pairs={{0,8},{8,0},{16,24},{24,16},{1,9},{9,1},{17,25},{25,17},{2,10},{10... | collective-permute-start | bytes 1228808 | tf_op jit(solution)/shard_map/ppermute | solution.py:478
  72.5 0.8 copy-start.2
  73.3 164.4 %reduce-scatter.2.cloned.1.call-start = ((), (), s32[]{:S(2)}) async-start(), calls=%async_computation.4 | async-start | bytes 7372800 | tf_op jit(solution)/shard_map/reduce_scatter | solution.py:544
  73.3 32.1 %collective-permute-start.1 = (bf16[256,2560]{1,0:T(8,128)(2,1)}, bf16[256,2560]{1,0:T(8,128)(2,1)}, u32[]{:S(2)}, u32[]{:S(2)}) collective-permute-start(bf16[256,2560]{1,0:T(8,128)(2,1)} %get-tuple-element.71), channel_id=1, source_target_pairs={{0,8},{8,0},{16,24},{24,16},{1,9},{9,1},{17,25},{25,17},{2,10},{10... | collective-permute-start | bytes 3932168 | tf_op jit(solution)/shard_map/ppermute | solution.py:478
  73.4 33.5 %collective-permute-start.2 = (bf16[256,2560]{1,0:T(8,128)(2,1)}, bf16[256,2560]{1,0:T(8,128)(2,1)}, u32[]{:S(2)}, u32[]{:S(2)}) collective-permute-start(bf16[256,2560]{1,0:T(8,128)(2,1)} %get-tuple-element.72.refs_0_), channel_id=1, source_target_pairs={{0,16},{8,24},{16,0},{24,8},{1,17},{9,25},{17,1},{25,9},{2,18},{10... | collective-permute-start | bytes 3932168 | tf_op jit(solution)/shard_map/ppermute | solution.py:478
  86.6 45.2 %collective-permute-start = (bf16[1024,640]{1,0:T(8,128)(2,1)}, bf16[1024,640]{1,0:T(8,128)(2,1)}, u32[]{:S(2)}, u32[]{:S(2)}) collective-permute-start(bf16[1024,640]{1,0:T(8,128)(2,1)} %get-tuple-element.39), channel_id=1, source_target_pairs={{0,8},{8,0},{16,24},{24,16},{1,9},{9,1},{17,25},{25,17},{2,10},{10... | collective-permute-start | bytes 3932168 | tf_op jit(solution)/shard_map/ppermute | solution.py:478
  105.4 31.9 %collective-permute-start.4 = (bf16[256,2560]{1,0:T(8,128)(2,1)}, bf16[256,2560]{1,0:T(8,128)(2,1)}, u32[]{:S(2)}, u32[]{:S(2)}) collective-permute-start(bf16[256,2560]{1,0:T(8,128)(2,1)} %collective-permute-done.1.refs_1_), channel_id=1, source_target_pairs={{0,16},{8,24},{16,0},{24,8},{1,17},{9,25},{17,1},{25,9},{2,18},{10... | collective-permute-start | bytes 3932168 | tf_op jit(solution)/shard_map/ppermute | solution.py:478
  135.3 30.5 %collective-permute-start.5 = (bf16[512,1024]{1,0:T(8,128)(2,1)}, bf16[512,1024]{1,0:T(8,128)(2,1)}, u32[]{:S(2)}, u32[]{:S(2)}) collective-permute-start(bf16[512,1024]{1,0:T(8,128)(2,1)} %project.4), channel_id=1, source_target_pairs={{0,16},{8,24},{16,0},{24,8},{1,17},{9,25},{17,1},{25,9},{2,18},{10... | collective-permute-start | bytes 3145736 | tf_op jit(solution)/shard_map/ppermute | solution.py:478
  136.8 29.1 %collective-permute-start.9 = (bf16[768,640]{1,0:T(8,128)(2,1)}, bf16[768,640]{1,0:T(8,128)(2,1)}, u32[]{:S(2)}, u32[]{:S(2)}) collective-permute-start(bf16[768,640]{1,0:T(8,128)(2,1)} %project_back.5), channel_id=1, source_target_pairs={{0,8},{8,0},{16,24},{24,16},{1,9},{9,1},{17,25},{25,17},{2,10},{10... | collective-permute-start | bytes 2949128 | tf_op jit(solution)/shard_map/ppermute | solution.py:478
  141.6 24.3 %collective-permute-start.10 = (bf16[256,640]{1,0:T(8,128)(2,1)}, bf16[256,640]{1,0:T(8,128)(2,1)}, u32[]{:S(2)}, u32[]{:S(2)}) collective-permute-start(bf16[256,640]{1,0:T(8,128)(2,1)} %project_back.6), channel_id=1, source_target_pairs={{0,8},{8,0},{16,24},{24,16},{1,9},{9,1},{17,25},{25,17},{2,10},{10... | collective-permute-start | bytes 983048 | tf_op jit(solution)/shard_map/ppermute | solution.py:478
  165.9 41.3 %collective-permute-start.7 = (bf16[512,1536]{1,0:T(8,128)(2,1)}, bf16[512,1536]{1,0:T(8,128)(2,1)}, u32[]{:S(2)}, u32[]{:S(2)}) collective-permute-start(bf16[512,1536]{1,0:T(8,128)(2,1)} %project.5), channel_id=1, source_target_pairs={{0,16},{8,24},{16,0},{24,8},{1,17},{9,25},{17,1},{25,9},{2,18},{10... | collective-permute-start | bytes 4718600 | tf_op jit(solution)/shard_map/ppermute | solution.py:478
  170.5 20.3 %collective-permute-start.6 = (bf16[256,1024]{1,0:T(8,128)(2,1)}, bf16[256,1024]{1,0:T(8,128)(2,1)}, u32[]{:S(2)}, u32[]{:S(2)}) collective-permute-start(bf16[256,1024]{1,0:T(8,128)(2,1)} %get-tuple-element.57), channel_id=1, source_target_pairs={{0,8},{8,0},{16,24},{24,16},{1,9},{9,1},{17,25},{25,17},{2,10},{10... | collective-permute-start | bytes 1572872 | tf_op jit(solution)/shard_map/ppermute | solution.py:478
  187.2 54.0 %collective-permute-start.11 = (bf16[3,256,640]{2,1,0:T(8,128)(2,1)}, bf16[3,256,640]{2,1,0:T(8,128)(2,1)}, u32[]{:S(2)}, u32[]{:S(2)}) collective-permute-start(bf16[3,256,640]{2,1,0:T(8,128)(2,1)} %get-tuple-element.63), channel_id=1, source_target_pairs={{0,8},{8,0},{16,24},{24,16},{1,9},{9,1},{17,25},{25,17},{2,10},{10... | collective-permute-start | bytes 2949128 | tf_op jit(solution)/shard_map/ppermute | solution.py:478
  188.8 53.1 %collective-permute-start.12 = (bf16[3,256,640]{2,1,0:T(8,128)(2,1)}, bf16[3,256,640]{2,1,0:T(8,128)(2,1)}, u32[]{:S(2)}, u32[]{:S(2)}) collective-permute-start(bf16[3,256,640]{2,1,0:T(8,128)(2,1)} %get-tuple-element.64), channel_id=1, source_target_pairs={{0,16},{8,24},{16,0},{24,8},{1,17},{9,25},{17,1},{25,9},{2,18},{10... | collective-permute-start | bytes 2949128 | tf_op jit(solution)/shard_map/ppermute | solution.py:478
  190.2 51.7 %collective-permute-start.13 = (bf16[3,256,640]{2,1,0:T(8,128)(2,1)}, bf16[3,256,640]{2,1,0:T(8,128)(2,1)}, u32[]{:S(2)}, u32[]{:S(2)}) collective-permute-start(bf16[3,256,640]{2,1,0:T(8,128)(2,1)} %get-tuple-element.65), channel_id=1, source_target_pairs={{0,24},{8,16},{16,8},{24,0},{1,25},{9,17},{17,9},{25,1},{2,26},{10... | collective-permute-start | bytes 2949128 | tf_op jit(solution)/shard_map/ppermute | solution.py:478
  212.9 34.8 %collective-permute-start.8 = (bf16[256,1536]{1,0:T(8,128)(2,1)}, bf16[256,1536]{1,0:T(8,128)(2,1)}, u32[]{:S(2)}, u32[]{:S(2)}) collective-permute-start(bf16[256,1536]{1,0:T(8,128)(2,1)} %get-tuple-element.60), channel_id=1, source_target_pairs={{0,8},{8,0},{16,24},{24,16},{1,9},{9,1},{17,25},{25,17},{2,10},{10... | collective-permute-start | bytes 2359304 | tf_op jit(solution)/shard_map/ppermute | solution.py:478
  239.7 13.1 %collective-permute-start.14 = (bf16[80,2560]{1,0:T(8,128)(2,1)}, bf16[80,2560]{1,0:T(8,128)(2,1)}, u32[]{:S(2)}, u32[]{:S(2)}) collective-permute-start(bf16[80,2560]{1,0:T(8,128)(2,1)} %get-tuple-element.74), channel_id=1, source_target_pairs={{0,8},{8,0},{16,24},{24,16},{1,9},{9,1},{17,25},{25,17},{2,10},{10... | collective-permute-start | bytes 1228808 | tf_op jit(solution)/shard_map/ppermute | solution.py:478
Sparse Core Ops, SparseCore 0:
  12.7 42.0 all-gather.2
  73.4 39.8 all-gather.4
  166.0 71.5 reduce-scatter.1

commit v3 on v2

--- a/solution.py
+++ b/solution.py
@@ -49,30 +49,42 @@
         o.wait()
 
 
-def pack_kernel(q_ref, k_ref, v_ref, out_ref, *rest):
-    n, _, _, width = out_ref.shape
-    moves = [
-        (src.at[0, :, pl.ds(g * width, width)], out_ref.at[g, t])
-        for g in range(n)
-        for t, src in enumerate((q_ref, k_ref, v_ref))
-    ]
-    staged(moves, *rest)
-
-
-def pack(q, k, v, n):
+def pack_kernel(n, width, me_ref, q_ref, k_ref, v_ref, *rest):
+    outs = rest[: n - 1]
+    moves = []
+    for r, out in enumerate(outs, 1):
+        col = pl.multiple_of((me_ref[0] ^ r) * width, 128)
+        for t, src in enumerate((q_ref, k_ref, v_ref)):
+            moves.append((src.at[0, :, pl.ds(col, width)], out.at[t]))
+    staged(moves, *rest[n - 1 :])
+
+
+def pack(me, q, k, v, n):
     rows, cols = q.shape[1:]
     width = cols // n
     return pl.pallas_call(
-        pack_kernel,
-        out_shape=sds((n, 3, rows, width)),
-        in_specs=[ANY, ANY, ANY],
-        out_specs=ANY,
-        scratch_shapes=[pltpu.VMEM((rows, width), BF)] * (3 * n)
-        + [pltpu.SemaphoreType.DMA((3 * n,))] * 2,
+        functools.partial(pack_kernel, n, width),
+        out_shape=[sds((3, rows, width))] * (n - 1),
+        in_specs=[SMEM, ANY, ANY, ANY],
+        out_specs=[ANY] * (n - 1),
+        scratch_shapes=[pltpu.VMEM((rows, width), BF)] * (3 * (n - 1))
+        + [pltpu.SemaphoreType.DMA((3 * (n - 1),))] * 2,
         compiler_params=params(64),
         cost_estimate=COST,
         name="pack",
-    )(q, k, v)
+    )(me, q, k, v)
+
+
+def load_copies(me, own, parts, held, sem):
+    width = held.shape[3]
+    col = pl.multiple_of(me * width, 128)
+    copies = [
+        pltpu.make_async_copy(x.at[0, :, pl.ds(col, width)], held.at[me, t], sem.at[t])
+        for t, x in enumerate(own)
+    ]
+    for r, part in enumerate(parts, 1):
+        copies.append(pltpu.make_async_copy(part, held.at[me ^ r], sem.at[2 + r]))
+    return copies
 
 
 def unpack_kernel(n, width, cuts, me_ref, *rest):
@@ -172,8 +184,10 @@
         out[j * BLK : (j + 1) * BLK] = held[e // per, t, rows]
 
 
-def fwd_kernel(heads, slots, scale, me_ref, nbr_ref, cnt_ref, held, attn_ref, swap_ref, t_ref, ks, vs):
+def fwd_kernel(heads, slots, scale, me_ref, nbr_ref, cnt_ref, *rest):
+    own, parts, (attn_ref, swap_ref, t_ref, held, ks, vs, sem) = rest[:3], rest[3:-7], rest[-7:]
     me = me_ref[0]
+    run_copies(load_copies(me, own, parts, held, sem))
     n, per = held.shape[0], held.shape[2] // BLK
 
     def body(b, keys):
@@ -195,27 +209,30 @@
 
 
 def attend(me, nbr, cnt, got, scale):
-    n, _, rows, width = got.shape
+    n = len(got) - 2
+    _, rows, width = got[3].shape
     vm = pl.BlockSpec(memory_space=pltpu.VMEM)
     return pl.pallas_call(
         functools.partial(fwd_kernel, width // HD, nbr.shape[2], scale),
         out_shape=[sds((n * rows, width))] * 2 + [sds((width, n * rows))],
-        in_specs=[SMEM] * 3 + [vm],
+        in_specs=[SMEM] * 3 + [ANY] * len(got),
         out_specs=[vm] * 3,
-        scratch_shapes=[pltpu.VMEM((nbr.shape[2] * BLK, width), BF)] * 2,
+        scratch_shapes=[pltpu.VMEM((n, 3, rows, width), BF)]
+        + [pltpu.VMEM((nbr.shape[2] * BLK, width), BF)] * 2
+        + [pltpu.SemaphoreType.DMA((n + 2,))],
         compiler_params=params(64),
         cost_estimate=COST,
         name="attend",
-    )(me, nbr, cnt, got)
-
-
-def bwd_kernel(begin, slots, scale, me_ref, nbr_ref, cnt_ref, got_ref, *rest):
+    )(me, nbr, cnt, *got)
+
+
+def bwd_kernel(n_got, slots, scale, me_ref, nbr_ref, cnt_ref, *rest):
+    got, rest = rest[:n_got], rest[n_got:]
     d_refs, outs, (held, terms, dq, dk, dv, ks, vs, sem, d_sem) = rest[:4], rest[4:-9], rest[-9:]
     me = me_ref[0]
     n, _, rows, some = held.shape
     per = rows // BLK
-    cols = pl.ds(begin, some)
-    copies = [pltpu.make_async_copy(got_ref.at[:, :, :, cols], held, sem)]
+    copies = load_copies(me, got[:3], got[3:], held, sem)
     own_0, own_1, pair_0, pair_1 = d_refs
     for i, (ref, begin, end, t, start) in enumerate(
         (
@@ -228,7 +245,7 @@
     ):
         part, there = pl.ds(begin * rows, (end - begin) * rows), pl.ds(start * rows, (end - begin) * rows)
         copies.append(
-            pltpu.make_async_copy(ref.at[part, cols], terms.at[t, there], d_sem.at[i])
+            pltpu.make_async_copy(ref.at[part], terms.at[t, there], d_sem.at[i])
         )
     for c in copies:
         c.start()
@@ -272,14 +289,14 @@
         out[2] = dv[rows_g].astype(BF)
 
 
-def attend_back(me, nbr, cnt, got, terms, begin, end, scale):
-    n, _, rows, _ = got.shape
-    some = end - begin
+def attend_back(me, nbr, cnt, got, terms, scale):
+    n = len(got) - 2
+    _, rows, some = got[3].shape
     vm = pl.BlockSpec(memory_space=pltpu.VMEM)
     return pl.pallas_call(
-        functools.partial(bwd_kernel, begin, nbr.shape[2], scale),
+        functools.partial(bwd_kernel, len(got), nbr.shape[2], scale),
         out_shape=[sds((3, rows, some))] * n,
-        in_specs=[SMEM] * 3 + [ANY] * 5,
+        in_specs=[SMEM] * 3 + [ANY] * (len(got) + 4),
         out_specs=[vm] * n,
         scratch_shapes=[
             pltpu.VMEM((n, 3, rows, some), BF),
@@ -289,13 +306,13 @@
             pltpu.VMEM((n * rows, some), F32),
             pltpu.VMEM((nbr.shape[2] * BLK, some), BF),
             pltpu.VMEM((nbr.shape[2] * BLK, some), BF),
-            pltpu.SemaphoreType.DMA,
+            pltpu.SemaphoreType.DMA((n + 2,)),
             pltpu.SemaphoreType.DMA((5,)),
         ],
         compiler_params=params(64),
         cost_estimate=COST,
         name="attend_back",
-    )(me, nbr, cnt, got, *terms)
+    )(me, nbr, cnt, *got, *terms)
 
 
 def project_own_kernel(a_ref, w_ref, o_ref):
@@ -440,7 +457,7 @@
         o_ref[:, i] = out.astype(BF).reshape(o_ref.shape[0], *o_ref.shape[2:])
 
 
-def weight_grad(done, at, b, ds, owners, tile=512):
+def weight_grad(done, at, b, ds, owners, tile=1280):
     n = len(ds)
     tokens, width = b.shape
     rows, cols = ds[0].shape
@@ -486,21 +503,17 @@
     def after(x, *others):
         return lax.optimization_barrier((x, *others))[0]
 
-    def exchange(x):
-        return lax.all_to_all(x, "seq", split_axis=0, concat_axis=0, tiled=True)
-
-    def exchange(x):
-        return lax.all_to_all(x, "seq", split_axis=0, concat_axis=0, tiled=True)
-
-    sent = pack(q_proj, k_proj, v_proj, n)
-    got = exchange(sent)
+    sent = pack(me, q_proj, k_proj, v_proj, n)
+    parts = [to(x, r) for r, x in enumerate(sent, 1)]
+    got = [q_proj, k_proj, v_proj, *parts]
+    sent = sent[0]
 
     w_out = after(w_out, sent)
     w_a = lax.all_gather(mine(w_out), "zero", axis=0, tiled=True)
     d_local = after(d_out, sent)[0]
     d0, d_theirs = mine(d_local), theirs(d_local)
 
-    w_pair = after(to(theirs(after(w_out, d0, d_theirs)), 1), w_a, got)
+    w_pair = after(to(theirs(after(w_out, d0, d_theirs)), 1), w_a, *parts)
     w_b = lax.all_gather(w_pair, "zero", axis=0, tiled=True)
 
     d1 = to(d_theirs, 1)
@@ -530,7 +543,7 @@
     gw = weight_grad(gw_own, attn_t, after(after_far, own_1), [d0, d1, d2, d3], owners)
 
     terms = [own_0, after(own_1, gw), pair_0, pair_1]
-    grads = attend_back(me, neighbours, counts, got, terms, 0, attn.shape[1], scale)
+    grads = attend_back(me, neighbours, counts, got, terms, scale)
     back = [grads[0]] + [to(x, r) for r, x in enumerate(grads[1:], 1)]
 
     ys, y_pair, last = [], [], gw

time: 264 us -> 259 us (0.981)
  waiting for transfers between devices: 108 us -> 101 us
  starting transfers between devices: 23 us -> 25.9 us
    ppermute x15 -> x18, waiting for transfers between devices: 83.4 us -> 74.4 us  [to(): return lax.ppermute(x, 'seq', [(i, i ^ r) for i in range(n)])]
    ppermute x15 -> x18, starting transfers between devices: 17.5 us -> 25.8 us  [to(): return lax.ppermute(x, 'seq', [(i, i ^ r) for i in range(n)])]
    all_to_all x1 -> x0, starting transfers between devices: 5.44 us -> none  [exchange(): return lax.all_to_all(x, 'seq', split_axis=0, concat_axis=0, tiled=True)]
  transfers between devices with their start and end apart: 19 -> 21, of which waited for: 9 -> 8; matrix products, arithmetic and copies ran while one was open for 2% -> 2% of each run, Pallas kernels for 40% -> 40%
where the time goes in v3:
time: 259 us; the launch traced here: 258 us
  Pallas kernels  106 us (41%)
  waiting for transfers between devices  101 us (39%)
  starting transfers between devices  25.9 us (10%)
  between operations  13.9 us (5%)
  local copies, waits for them, and re-layouts  8.71 us (3%)
  other arithmetic  2.73 us (1%)
    ppermute x18, waiting for transfers between devices, to(): return lax.ppermute(x, 'seq', [(i, i ^ r) for i in range(n)])  74.4 us
    reduce_scatter x1, waiting for transfers between devices, on_device(): lax.psum_scatter(after(gw, y_far[0], pair_0, pair_1), 'zero', scatter_dim...  26.1 us
    ppermute x18, starting transfers between devices, to(): return lax.ppermute(x, 'seq', [(i, i ^ r) for i in range(n)])  25.8 us
    pallas_call x4, Pallas kernels, project_back(): pl.pallas_call(functools.partial(project_back_kernel, n, m, order), out_s...  23.3 us
    pallas_call x4, Pallas kernels, project(): pl.pallas_call(project_kernel, grid=(cols // tile,), out_shape=[sds((out,...  18.7 us
    pallas_call x1, Pallas kernels, attend_back(): pl.pallas_call(functools.partial(bwd_kernel, len(got), nbr.shape[2], scal...  16.4 us
    pallas_call x1, Pallas kernels, attend(): pl.pallas_call(functools.partial(fwd_kernel, width // HD, nbr.shape[2], s...  11.3 us
    pallas_call x1, Pallas kernels, weight_grad(): pl.pallas_call(functools.partial(weight_kernel, n), grid=(cols // tile,),...  10.4 us
  transfers between devices with their start and end apart: 21, of which 8 were waited for; matrix products, arithmetic and copies ran while one was open for 2% of the time, Pallas kernels for 40%

profile of v3, /device:TPU:0, one launch (start us, length us, event | category | flops | bytes accessed | tf_op | source)
XLA Modules:
  0.0 257.9 jit_solution(2586275192497273351)
XLA Ops:
  7.2 2.7 %pack.1 = (bf16[3,256,640]{2,1,0:T(8,128)(2,1)}, bf16[3,256,640]{2,1,0:T(8,128)(2,1)}, bf16[3,256,640]{2,1,0:T(8,128)(2,1)}) custom-call(s32[1]{0:T(128)} %bitcast.1.me_ref, bf16[1,256,2560]{2,1,0:T(8,128)(2,1)} %rest_0_.3, bf16[1,256,2560]{2,1,0:T(8,128)(2,1)} %rest_1_.3, bf16[1,256,2560]{2,1,0:T(8,128)(2,1)} %rest_2_.3), custom_call_target="tpu_custom_call" | custom-call | flops 1024 | bytes 1024 | tf_op jit(solution)/shard_map/pack/pallas_call | solution.py:65
  9.9 1.8 constant_dynamic-slice_fusion.1
  11.8 3.0 %collective-permute-start = (bf16[3,256,640]{2,1,0:T(8,128)(2,1)}, bf16[3,256,640]{2,1,0:T(8,128)(2,1)}, u32[]{:S(2)}, u32[]{:S(2)}) collective-permute-start(bf16[3,256,640]{2,1,0:T(8,128)(2,1)} %get-tuple-element.41), channel_id=1, source_target_pairs={{0,8},{8,0},{16,24},{24,16},{1,9},{9,1},{17,25},{25,17},{2,10},{10... | collective-permute-start | bytes 2949128 | tf_op jit(solution)/shard_map/ppermute | solution.py:495
  16.4 3.4 %dynamic-slice_bitcast_fusion = (bf16[256,2560]{1,0:T(8,128)(2,1)}, bf16[256,2560]{1,0:T(8,128)(2,1)}) fusion(bf16[1,256,5120]{2,1,0:T(8,128)(2,1)} %param.13, s32[]{:T(128)S(6)} %select_n.17, s32[]{:T(128)S(6)} %select_n.16), kind=kLoop, calls=%fused_computation | loop fusion | bytes 5242888 | tf_op jit(solution)/shard_map/dynamic_slice | solution.py:501
  19.8 2.0 collective-permute-start.6
  21.9 44.8 %collective-permute-done.6 = bf16[80,2560]{1,0:T(8,128)(2,1)S(1)} collective-permute-done((bf16[80,2560]{1,0:T(8,128)(2,1)S(1)}, bf16[80,2560]{1,0:T(8,128)(2,1)S(1)}, u32[]{:S(2)}, u32[]{:S(2)}) %collective-permute-start.6) | collective-permute-done | bytes 409632 | tf_op jit(solution)/shard_map/ppermute | solution.py:495
  67.5 1.8 collective-permute-start.4
  71.4 11.3 %attend.1 = (bf16[1024,640]{1,0:T(8,128)(2,1)}, bf16[1024,640]{1,0:T(8,128)(2,1)}, bf16[640,1024]{1,0:T(8,128)(2,1)}) custom-call(s32[1]{0:T(128)} %bitcast.1.me_ref, s32[1,8,4]{2,1,0:T(8,128)} %copy.12.nbr_ref, s32[1,8]{1,0:T(1,128)} %cnt_ref.3, bf16[1,256,2560]{2,1,0:T(8,128)(2,1)} %rest_0_.3, bf16[1,256,2560]{2,1,0:T(8,128)(2,1)} %rest_1_.3, ...), custom_call_target="tpu_custom_call" | custom-call | flops 1024 | bytes 1024 | tf_op jit(solution)/shard_map/attend/pallas_call | solution.py:215
  83.4 9.2 %project_own.1.own_ref = f32[1024,2560]{1,0:T(8,128)} custom-call(bf16[1024,640]{1,0:T(8,128)(2,1)} %get-tuple-element.46.a_ref, bf16[640,2560]{1,0:T(8,128)(2,1)} %all-gather.3.cloned.1.call-done.w_ref.refs_3_.refs_1_), custom_call_target="tpu_custom_call" | custom-call | flops 1024 | bytes 1024 | tf_op jit(solution)/shard_map/project_own/pallas_call | solution.py:325
  92.6 7.0 %collective-permute-done.4.refs_1_ = bf16[256,2560]{1,0:T(8,128)(2,1)} collective-permute-done((bf16[256,2560]{1,0:T(8,128)(2,1)}, bf16[256,2560]{1,0:T(8,128)(2,1)}, u32[]{:S(2)}, u32[]{:S(2)}) %collective-permute-start.4) | collective-permute-done | bytes 1310752 | tf_op jit(solution)/shard_map/ppermute | solution.py:495
  99.6 1.8 collective-permute-start.7
  101.4 7.4 %project_back.4.rest_6_ = bf16[768,640]{1,0:T(8,128)(2,1)} custom-call(bf16[256,2560]{1,0:T(8,128)(2,1)} %get-tuple-element.78.refs_0_, bf16[256,2560]{1,0:T(8,128)(2,1)} %collective-permute-done.4.refs_1_, bf16[256,2560]{1,0:T(8,128)(2,1)} %collective-permute-done.5.refs_2_, bf16[640,2560]{1,0:T(8,128)(2,1)} %all-gather.3.cloned.1.call-done.w_ref.refs_3_.refs_1_), custom_call_target="tpu_custom_call" | custom-call | flops 1024 | bytes 1024 | tf_op jit(solution)/shard_map/project_back/pallas_call | solution.py:403
  108.8 7.3 %project_back.5 = bf16[768,640]{1,0:T(8,128)(2,1)} custom-call(bf16[256,2560]{1,0:T(8,128)(2,1)} %get-tuple-element.78.refs_0_, bf16[256,2560]{1,0:T(8,128)(2,1)} %collective-permute-done.4.refs_1_, bf16[256,2560]{1,0:T(8,128)(2,1)} %collective-permute-done.5.refs_2_, bf16[640,2560]{1,0:T(8,128)(2,1)} %all-gather.5.cloned.1.call-done.refs_3_.w_ref.refs_1_), custom_call_target="tpu_custom_call" | custom-call | flops 1024 | bytes 1024 | tf_op jit(solution)/shard_map/project_back/pallas_call | solution.py:403
  116.2 7.9 %weight_own.1.done_ref = f32[640,2560]{1,0:T(8,128)} custom-call(bf16[640,1024]{1,0:T(8,128)(2,1)} %get-tuple-element.53.at, bf16[256,2560]{1,0:T(8,128)(2,1)} %get-tuple-element.78.refs_0_, bf16[256,2560]{1,0:T(8,128)(2,1)} %collective-permute-done.4.refs_1_, bf16[256,2560]{1,0:T(8,128)(2,1)} %collective-permute-done.5.refs_2_), custom_call_target="tpu_custom_call" | custom-call | flops 1024 | bytes 1024 | tf_op jit(solution)/shard_map/weight_own/pallas_call | solution.py:431
  124.1 1.8 collective-permute-done.3.b_ref
  125.9 3.6 %project.4 = bf16[512,1024]{1,0:T(8,128)(2,1)} custom-call(f32[1024,2560]{1,0:T(8,128)} %project_own.1.own_ref, bf16[1024,640]{1,0:T(8,128)(2,1)} %collective-permute-done.3.b_ref, bf16[640,2560]{1,0:T(8,128)(2,1)} %all-gather.5.cloned.1.call-done.refs_3_.w_ref.refs_1_), custom_call_target="tpu_custom_call" | custom-call | flops 1024 | bytes 1024 | tf_op jit(solution)/shard_map/project/pallas_call | solution.py:360
  132.4 4.3 %project_back.6 = bf16[256,640]{1,0:T(8,128)(2,1)} custom-call(bf16[256,2560]{1,0:T(8,128)(2,1)} %collective-permute-done.7.refs_0_.refs_3_, bf16[640,2560]{1,0:T(8,128)(2,1)} %all-gather.5.cloned.1.call-done.refs_3_.w_ref.refs_1_), custom_call_target="tpu_custom_call" | custom-call | flops 1024 | bytes 1024 | tf_op jit(solution)/shard_map/project_back/pallas_call | solution.py:403
  137.3 5.4 %project.5 = bf16[512,1536]{1,0:T(8,128)(2,1)} custom-call(f32[1024,2560]{1,0:T(8,128)} %project_own.1.own_ref, bf16[1024,640]{1,0:T(8,128)(2,1)} %collective-permute-done.3.b_ref, bf16[640,2560]{1,0:T(8,128)(2,1)} %all-gather.5.cloned.1.call-done.refs_3_.w_ref.refs_1_), custom_call_target="tpu_custom_call" | custom-call | flops 1024 | bytes 1024 | tf_op jit(solution)/shard_map/project/pallas_call | solution.py:360
  142.7 4.3 %project_back.7.rest_7_ = bf16[256,640]{1,0:T(8,128)(2,1)} custom-call(bf16[256,2560]{1,0:T(8,128)(2,1)} %collective-permute-done.7.refs_0_.refs_3_, bf16[640,2560]{1,0:T(8,128)(2,1)} %all-gather.3.cloned.1.call-done.w_ref.refs_3_.refs_1_), custom_call_target="tpu_custom_call" | custom-call | flops 1024 | bytes 1024 | tf_op jit(solution)/shard_map/project_back/pallas_call | solution.py:403
  147.0 10.4 %weight_grad.1 = bf16[8,2,80,2560]{3,2,1,0:T(8,128)(2,1)} custom-call(f32[640,2560]{1,0:T(8,128)} %weight_own.1.done_ref, bf16[640,1024]{1,0:T(8,128)(2,1)} %get-tuple-element.53.at, bf16[1024,640]{1,0:T(8,128)(2,1)} %collective-permute-done.3.b_ref, bf16[256,2560]{1,0:T(8,128)(2,1)} %get-tuple-element.78.refs_0_, ...), custom_call_target="tpu_custom_call" | custom-call | flops 1024 | bytes 1024 | tf_op jit(solution)/shard_map/weight_grad/pallas_call | solution.py:466
  157.4 2.3 collective-permute-done.13.rest_9_
  160.7 4.0 %project.6 = (bf16[256,1024]{1,0:T(8,128)(2,1)}, bf16[256,1024]{1,0:T(8,128)(2,1)}) custom-call(f32[1024,2560]{1,0:T(8,128)} %project_own.1.own_ref, bf16[1024,640]{1,0:T(8,128)(2,1)} %collective-permute-done.3.b_ref, bf16[640,2560]{1,0:T(8,128)(2,1)} %all-gather.5.cloned.1.call-done.refs_3_.w_ref.refs_1_, bf16[512,1024]{1,0:T(8,128)(2,1)} %collective-permute-done.8.rest_0_), custom_call_target="tpu_custom_call" | custom-call | flops 1024 | bytes 1024 | tf_op jit(solution)/shard_map/project/pallas_call | solution.py:360
  165.8 16.4 %attend_back.1 = (bf16[3,256,640]{2,1,0:T(8,128)(2,1)}, bf16[3,256,640]{2,1,0:T(8,128)(2,1)}, bf16[3,256,640]{2,1,0:T(8,128)(2,1)}, bf16[3,256,640]{2,1,0:T(8,128)(2,1)}) custom-call(s32[1]{0:T(128)} %bitcast.1.me_ref, s32[1,8,4]{2,1,0:T(8,128)} %copy.12.nbr_ref, s32[1,8]{1,0:T(1,128)} %cnt_ref.3, bf16[1,256,2560]{2,1,0:T(8,128)(2,1)} %rest_0_.3, ...), custom_call_target="tpu_custom_call" | custom-call | flops 1024 | bytes 1024 | tf_op jit(solution)/shard_map/attend_back/pallas_call | solution.py:296
  185.8 11.9 %collective-permute-done.10.rest_0_ = bf16[512,1536]{1,0:T(8,128)(2,1)} collective-permute-done((bf16[512,1536]{1,0:T(8,128)(2,1)}, bf16[512,1536]{1,0:T(8,128)(2,1)}, u32[]{:S(2)}, u32[]{:S(2)}) %collective-permute-start.10) | collective-permute-done | bytes 1572896 | tf_op jit(solution)/shard_map/ppermute | solution.py:495
  197.7 5.8 %project.7 = (bf16[256,1536]{1,0:T(8,128)(2,1)}, bf16[256,1536]{1,0:T(8,128)(2,1)}) custom-call(f32[1024,2560]{1,0:T(8,128)} %project_own.1.own_ref, bf16[1024,640]{1,0:T(8,128)(2,1)} %collective-permute-done.3.b_ref, bf16[640,2560]{1,0:T(8,128)(2,1)} %all-gather.5.cloned.1.call-done.refs_3_.w_ref.refs_1_, bf16[512,1536]{1,0:T(8,128)(2,1)} %collective-permute-done.10.rest_0_), custom_call_target="tpu_custom_call" | custom-call | flops 1024 | bytes 1024 | tf_op jit(solution)/shard_map/project/pallas_call | solution.py:360
  203.5 2.9 %collective-permute-start.11 = (bf16[256,1536]{1,0:T(8,128)(2,1)}, bf16[256,1536]{1,0:T(8,128)(2,1)}, u32[]{:S(2)}, u32[]{:S(2)}) collective-permute-start(bf16[256,1536]{1,0:T(8,128)(2,1)} %get-tuple-element.66), channel_id=1, source_target_pairs={{0,8},{8,0},{16,24},{24,16},{1,9},{9,1},{17,25},{25,17},{2,10},{10... | collective-permute-start | bytes 2359304 | tf_op jit(solution)/shard_map/ppermute | solution.py:495
  206.4 26.1 %reduce-scatter.2.cloned.1.call-done = bf16[160,2560]{1,0:T(8,128)(2,1)} async-done(((bf16[1280,2560]{1,0:T(8,128)(2,1)}), bf16[160,2560]{1,0:T(8,128)(2,1)}) %reduce-scatter.2.cloned.1.call-update) | async-done | bytes 819216 | tf_op jit(solution)/shard_map/reduce_scatter | solution.py:557
  232.4 2.1 fusion.1
  236.0 3.5 %unpack.1 = (bf16[1,256,2560]{2,1,0:T(8,128)(2,1)}, bf16[1,256,2560]{2,1,0:T(8,128)(2,1)}, bf16[1,256,2560]{2,1,0:T(8,128)(2,1)}) custom-call(s32[1]{0:T(128)} %bitcast.1.me_ref, bf16[3,256,640]{2,1,0:T(8,128)(2,1)} %get-tuple-element.68.rest_0_, bf16[3,256,640]{2,1,0:T(8,128)(2,1)} %collective-permute-done.14.rest_1_, ...), custom_call_target="tpu_custom_call" | custom-call | flops 1024 | bytes 1024 | tf_op jit(solution)/shard_map/unpack/pallas_call | solution.py:107
  239.5 4.7 %collective-permute-done.11.rest_3_ = bf16[256,1536]{1,0:T(8,128)(2,1)} collective-permute-done((bf16[256,1536]{1,0:T(8,128)(2,1)}, bf16[256,1536]{1,0:T(8,128)(2,1)}, u32[]{:S(2)}, u32[]{:S(2)}) %collective-permute-start.11) | collective-permute-done | bytes 786464 | tf_op jit(solution)/shard_map/ppermute | solution.py:495
  244.2 2.7 %join.1 = bf16[1,256,5120]{2,1,0:T(8,128)(2,1)} custom-call(s32[1]{0:T(128)} %bitcast.low_ref, bf16[256,1024]{1,0:T(8,128)(2,1)} %get-tuple-element.62.rest_0_, bf16[256,1536]{1,0:T(8,128)(2,1)} %get-tuple-element.65.rest_1_, bf16[256,1024]{1,0:T(8,128)(2,1)} %collective-permute-done.9.rest_2_, bf16[256,1536]{1,0:T(8,128)(2,1)} %collective-permute-done.11.rest_3_), custom_call_target="tpu_custom_call" | custom-call | flops 1024 | bytes 1024 | tf_op jit(solution)/shard_map/join/pallas_call | solution.py:138
  248.6 2.7 %fusion = f32[80,5120]{1,0:T(8,128)} fusion(bf16[80,2560]{1,0:T(8,128)(2,1)} %collective-permute-done.17, bf16[80,2560]{1,0:T(8,128)(2,1)} %get-tuple-element.79, pred[]{:T(512)S(6)} %eq.3), kind=kLoop, calls=%fused_computation.3 | loop fusion | flops 4096000 | bytes 2457601 | tf_op jit(solution)/shard_map/convert_element_type | solution.py:565
  (41 shorter events, 17.7 us)
Async XLA Ops:
  7.2 59.5 %all-gather.3.cloned.1.call-start = ((), (), s32[]{:S(2)}) async-start(), calls=%async_computation.1 | async-start | bytes 3686400 | tf_op jit(solution)/shard_map/all_gather | solution.py:512
  11.8 97.0 %all-gather.5.cloned.1.call-start = ((), (), s32[]{:S(2)}) async-start(), calls=%async_computation.2 | async-start | bytes 3686400 | tf_op jit(solution)/shard_map/all_gather | solution.py:517
  11.8 54.9 %collective-permute-start = (bf16[3,256,640]{2,1,0:T(8,128)(2,1)}, bf16[3,256,640]{2,1,0:T(8,128)(2,1)}, u32[]{:S(2)}, u32[]{:S(2)}) collective-permute-start(bf16[3,256,640]{2,1,0:T(8,128)(2,1)} %get-tuple-element.41), channel_id=1, source_target_pairs={{0,8},{8,0},{16,24},{24,16},{1,9},{9,1},{17,25},{25,17},{2,10},{10... | collective-permute-start | bytes 2949128 | tf_op jit(solution)/shard_map/ppermute | solution.py:495
  14.8 51.9 %collective-permute-start.1 = (bf16[3,256,640]{2,1,0:T(8,128)(2,1)}, bf16[3,256,640]{2,1,0:T(8,128)(2,1)}, u32[]{:S(2)}, u32[]{:S(2)}) collective-permute-start(bf16[3,256,640]{2,1,0:T(8,128)(2,1)} %get-tuple-element.42), channel_id=1, source_target_pairs={{0,16},{8,24},{16,0},{24,8},{1,17},{9,25},{17,1},{25,9},{2,18},{10... | collective-permute-start | bytes 2949128 | tf_op jit(solution)/shard_map/ppermute | solution.py:495
  16.3 50.3 %collective-permute-start.2 = (bf16[3,256,640]{2,1,0:T(8,128)(2,1)}, bf16[3,256,640]{2,1,0:T(8,128)(2,1)}, u32[]{:S(2)}, u32[]{:S(2)}) collective-permute-start(bf16[3,256,640]{2,1,0:T(8,128)(2,1)} %get-tuple-element.43), channel_id=1, source_target_pairs={{0,24},{8,16},{16,8},{24,0},{1,25},{9,17},{17,9},{25,1},{2,26},{10... | collective-permute-start | bytes 2949128 | tf_op jit(solution)/shard_map/ppermute | solution.py:495
  16.4 3.4 %copy-start = (bf16[80,5120]{1,0:T(8,128)(2,1)S(1)}, bf16[80,5120]{1,0:T(8,128)(2,1)}, u32[]{:S(2)}) copy-start(bf16[80,5120]{1,0:T(8,128)(2,1)} %param.12) | copy-start | bytes 2457604
  16.4 54.4 %copy-start.2 = (s32[1,8,4]{1,2,0:T(4,128)S(1)}, s32[1,8,4]{1,2,0:T(4,128)}, u32[]{:S(2)}) copy-start(s32[1,8,4]{1,2,0:T(4,128)} %param.10) | copy-start | bytes 388
  19.8 46.8 %collective-permute-start.6 = (bf16[80,2560]{1,0:T(8,128)(2,1)S(1)}, bf16[80,2560]{1,0:T(8,128)(2,1)S(1)}, u32[]{:S(2)}, u32[]{:S(2)}) collective-permute-start(bf16[80,2560]{1,0:T(8,128)(2,1)S(1)} %constant_dynamic-slice_fusion), channel_id=1, source_target_pairs={{0,8},{8,0},{16,24},{24,16},{1,9},{9,1},{17,25},{25,17},{2,10},{10... | collective-permute-start | bytes 1228808 | tf_op jit(solution)/shard_map/ppermute | solution.py:495
  66.7 0.8 copy-start.1
  67.4 165.0 %reduce-scatter.2.cloned.1.call-start = ((), (), s32[]{:S(2)}) async-start(), calls=%async_computation.3 | async-start | bytes 7372800 | tf_op jit(solution)/shard_map/reduce_scatter | solution.py:557
  67.5 32.1 %collective-permute-start.4 = (bf16[256,2560]{1,0:T(8,128)(2,1)}, bf16[256,2560]{1,0:T(8,128)(2,1)}, u32[]{:S(2)}, u32[]{:S(2)}) collective-permute-start(bf16[256,2560]{1,0:T(8,128)(2,1)} %get-tuple-element.77), channel_id=1, source_target_pairs={{0,8},{8,0},{16,24},{24,16},{1,9},{9,1},{17,25},{25,17},{2,10},{10... | collective-permute-start | bytes 3932168 | tf_op jit(solution)/shard_map/ppermute | solution.py:495
  69.3 32.1 %collective-permute-start.5 = (bf16[256,2560]{1,0:T(8,128)(2,1)}, bf16[256,2560]{1,0:T(8,128)(2,1)}, u32[]{:S(2)}, u32[]{:S(2)}) collective-permute-start(bf16[256,2560]{1,0:T(8,128)(2,1)} %get-tuple-element.78.refs_0_), channel_id=1, source_target_pairs={{0,16},{8,24},{16,0},{24,8},{1,17},{9,25},{17,1},{25,9},{2,18},{10... | collective-permute-start | bytes 3932168 | tf_op jit(solution)/shard_map/ppermute | solution.py:495
  82.7 43.2 %collective-permute-start.3 = (bf16[1024,640]{1,0:T(8,128)(2,1)}, bf16[1024,640]{1,0:T(8,128)(2,1)}, u32[]{:S(2)}, u32[]{:S(2)}) collective-permute-start(bf16[1024,640]{1,0:T(8,128)(2,1)} %get-tuple-element.45), channel_id=1, source_target_pairs={{0,8},{8,0},{16,24},{24,16},{1,9},{9,1},{17,25},{25,17},{2,10},{10... | collective-permute-start | bytes 3932168 | tf_op jit(solution)/shard_map/ppermute | solution.py:495
  99.6 32.8 %collective-permute-start.7 = (bf16[256,2560]{1,0:T(8,128)(2,1)}, bf16[256,2560]{1,0:T(8,128)(2,1)}, u32[]{:S(2)}, u32[]{:S(2)}) collective-permute-start(bf16[256,2560]{1,0:T(8,128)(2,1)} %collective-permute-done.4.refs_1_), channel_id=1, source_target_pairs={{0,16},{8,24},{16,0},{24,8},{1,17},{9,25},{17,1},{25,9},{2,18},{10... | collective-permute-start | bytes 3932168 | tf_op jit(solution)/shard_map/ppermute | solution.py:495
  129.5 30.2 %collective-permute-start.8 = (bf16[512,1024]{1,0:T(8,128)(2,1)}, bf16[512,1024]{1,0:T(8,128)(2,1)}, u32[]{:S(2)}, u32[]{:S(2)}) collective-permute-start(bf16[512,1024]{1,0:T(8,128)(2,1)} %project.4), channel_id=1, source_target_pairs={{0,16},{8,24},{16,0},{24,8},{1,17},{9,25},{17,1},{25,9},{2,18},{10... | collective-permute-start | bytes 3145736 | tf_op jit(solution)/shard_map/ppermute | solution.py:495
  131.0 28.8 %collective-permute-start.12 = (bf16[768,640]{1,0:T(8,128)(2,1)}, bf16[768,640]{1,0:T(8,128)(2,1)}, u32[]{:S(2)}, u32[]{:S(2)}) collective-permute-start(bf16[768,640]{1,0:T(8,128)(2,1)} %project_back.5), channel_id=1, source_target_pairs={{0,8},{8,0},{16,24},{24,16},{1,9},{9,1},{17,25},{25,17},{2,10},{10... | collective-permute-start | bytes 2949128 | tf_op jit(solution)/shard_map/ppermute | solution.py:495
  136.7 23.0 %collective-permute-start.13 = (bf16[256,640]{1,0:T(8,128)(2,1)}, bf16[256,640]{1,0:T(8,128)(2,1)}, u32[]{:S(2)}, u32[]{:S(2)}) collective-permute-start(bf16[256,640]{1,0:T(8,128)(2,1)} %project_back.6), channel_id=1, source_target_pairs={{0,8},{8,0},{16,24},{24,16},{1,9},{9,1},{17,25},{25,17},{2,10},{10... | collective-permute-start | bytes 983048 | tf_op jit(solution)/shard_map/ppermute | solution.py:495
  159.8 37.9 %collective-permute-start.10 = (bf16[512,1536]{1,0:T(8,128)(2,1)}, bf16[512,1536]{1,0:T(8,128)(2,1)}, u32[]{:S(2)}, u32[]{:S(2)}) collective-permute-start(bf16[512,1536]{1,0:T(8,128)(2,1)} %project.5), channel_id=1, source_target_pairs={{0,16},{8,24},{16,0},{24,8},{1,17},{9,25},{17,1},{25,9},{2,18},{10... | collective-permute-start | bytes 4718600 | tf_op jit(solution)/shard_map/ppermute | solution.py:495
  164.7 21.1 %collective-permute-start.9 = (bf16[256,1024]{1,0:T(8,128)(2,1)}, bf16[256,1024]{1,0:T(8,128)(2,1)}, u32[]{:S(2)}, u32[]{:S(2)}) collective-permute-start(bf16[256,1024]{1,0:T(8,128)(2,1)} %get-tuple-element.63), channel_id=1, source_target_pairs={{0,8},{8,0},{16,24},{24,16},{1,9},{9,1},{17,25},{25,17},{2,10},{10... | collective-permute-start | bytes 1572872 | tf_op jit(solution)/shard_map/ppermute | solution.py:495
  182.2 53.8 %collective-permute-start.14 = (bf16[3,256,640]{2,1,0:T(8,128)(2,1)}, bf16[3,256,640]{2,1,0:T(8,128)(2,1)}, u32[]{:S(2)}, u32[]{:S(2)}) collective-permute-start(bf16[3,256,640]{2,1,0:T(8,128)(2,1)} %get-tuple-element.69), channel_id=1, source_target_pairs={{0,8},{8,0},{16,24},{24,16},{1,9},{9,1},{17,25},{25,17},{2,10},{10... | collective-permute-start | bytes 2949128 | tf_op jit(solution)/shard_map/ppermute | solution.py:495
  183.5 52.5 %collective-permute-start.15 = (bf16[3,256,640]{2,1,0:T(8,128)(2,1)}, bf16[3,256,640]{2,1,0:T(8,128)(2,1)}, u32[]{:S(2)}, u32[]{:S(2)}) collective-permute-start(bf16[3,256,640]{2,1,0:T(8,128)(2,1)} %get-tuple-element.70), channel_id=1, source_target_pairs={{0,16},{8,24},{16,0},{24,8},{1,17},{9,25},{17,1},{25,9},{2,18},{10... | collective-permute-start | bytes 2949128 | tf_op jit(solution)/shard_map/ppermute | solution.py:495
  184.8 51.2 %collective-permute-start.16 = (bf16[3,256,640]{2,1,0:T(8,128)(2,1)}, bf16[3,256,640]{2,1,0:T(8,128)(2,1)}, u32[]{:S(2)}, u32[]{:S(2)}) collective-permute-start(bf16[3,256,640]{2,1,0:T(8,128)(2,1)} %get-tuple-element.71), channel_id=1, source_target_pairs={{0,24},{8,16},{16,8},{24,0},{1,25},{9,17},{17,9},{25,1},{2,26},{10... | collective-permute-start | bytes 2949128 | tf_op jit(solution)/shard_map/ppermute | solution.py:495
  203.5 40.7 %collective-permute-start.11 = (bf16[256,1536]{1,0:T(8,128)(2,1)}, bf16[256,1536]{1,0:T(8,128)(2,1)}, u32[]{:S(2)}, u32[]{:S(2)}) collective-permute-start(bf16[256,1536]{1,0:T(8,128)(2,1)} %get-tuple-element.66), channel_id=1, source_target_pairs={{0,8},{8,0},{16,24},{24,16},{1,9},{9,1},{17,25},{25,17},{2,10},{10... | collective-permute-start | bytes 2359304 | tf_op jit(solution)/shard_map/ppermute | solution.py:495
  234.5 14.1 %collective-permute-start.17 = (bf16[80,2560]{1,0:T(8,128)(2,1)}, bf16[80,2560]{1,0:T(8,128)(2,1)}, u32[]{:S(2)}, u32[]{:S(2)}) collective-permute-start(bf16[80,2560]{1,0:T(8,128)(2,1)} %get-tuple-element.80), channel_id=1, source_target_pairs={{0,8},{8,0},{16,24},{24,16},{1,9},{9,1},{17,25},{25,17},{2,10},{10... | collective-permute-start | bytes 1228808 | tf_op jit(solution)/shard_map/ppermute | solution.py:495
Sparse Core Ops, SparseCore 0:
  11.9 42.0 all-gather.2
  67.6 40.8 all-gather.4
  159.9 72.5 reduce-scatter.1

commit v4 on v3

--- a/solution.py
+++ b/solution.py
@@ -49,30 +49,36 @@
         o.wait()
 
 
-def pack_kernel(n, width, me_ref, q_ref, k_ref, v_ref, *rest):
-    outs = rest[: n - 1]
+def pack_kernel(n, width, me_ref, q_ref, k_ref, v_ref, w_ref, *rest):
+    outs = rest[: n + 1]
+    half = w_ref.shape[1] // 2
     moves = []
-    for r, out in enumerate(outs, 1):
+    for r, out in enumerate(outs[: n - 1], 1):
         col = pl.multiple_of((me_ref[0] ^ r) * width, 128)
         for t, src in enumerate((q_ref, k_ref, v_ref)):
             moves.append((src.at[0, :, pl.ds(col, width)], out.at[t]))
-    staged(moves, *rest[n - 1 :])
-
-
-def pack(me, q, k, v, n):
+    for i, out in enumerate(outs[n - 1 :]):
+        col = pl.multiple_of(((me_ref[0] & 1) ^ i) * half, 128)
+        moves.append((w_ref.at[:, pl.ds(col, half)], out))
+    staged(moves, *rest[n + 1 :])
+
+
+def pack(me, q, k, v, w, n):
     rows, cols = q.shape[1:]
     width = cols // n
+    w_half = (w.shape[0], w.shape[1] // 2)
     return pl.pallas_call(
         functools.partial(pack_kernel, n, width),
-        out_shape=[sds((3, rows, width))] * (n - 1),
-        in_specs=[SMEM, ANY, ANY, ANY],
-        out_specs=[ANY] * (n - 1),
+        out_shape=[sds((3, rows, width))] * (n - 1) + [sds(w_half)] * 2,
+        in_specs=[SMEM, ANY, ANY, ANY, ANY],
+        out_specs=[ANY] * (n + 1),
         scratch_shapes=[pltpu.VMEM((rows, width), BF)] * (3 * (n - 1))
-        + [pltpu.SemaphoreType.DMA((3 * (n - 1),))] * 2,
+        + [pltpu.VMEM(w_half, BF)] * 2
+        + [pltpu.SemaphoreType.DMA((3 * n - 1,))] * 2,
         compiler_params=params(64),
         cost_estimate=COST,
         name="pack",
-    )(me, q, k, v)
+    )(me, q, k, v, w)
 
 
 def load_copies(me, own, parts, held, sem):
@@ -503,17 +509,16 @@
     def after(x, *others):
         return lax.optimization_barrier((x, *others))[0]
 
-    sent = pack(me, q_proj, k_proj, v_proj, n)
+    *sent, w_mine, w_theirs = pack(me, q_proj, k_proj, v_proj, w_out, n)
     parts = [to(x, r) for r, x in enumerate(sent, 1)]
     got = [q_proj, k_proj, v_proj, *parts]
     sent = sent[0]
 
-    w_out = after(w_out, sent)
-    w_a = lax.all_gather(mine(w_out), "zero", axis=0, tiled=True)
+    w_a = lax.all_gather(w_mine, "zero", axis=0, tiled=True)
     d_local = after(d_out, sent)[0]
     d0, d_theirs = mine(d_local), theirs(d_local)
 
-    w_pair = after(to(theirs(after(w_out, d0, d_theirs)), 1), w_a, *parts)
+    w_pair = after(to(after(w_theirs, d0, d_theirs), 1), w_a, *parts)
     w_b = lax.all_gather(w_pair, "zero", axis=0, tiled=True)
 
     d1 = to(d_theirs, 1)

time: 259 us -> 257 us (level)
  waiting for transfers between devices: 101 us -> 105 us
    ppermute x18, waiting for transfers between devices: 74.4 us -> 77 us  [to(): return lax.ppermute(x, 'seq', [(i, i ^ r) for i in range(n)])]
  transfers between devices with their start and end apart: 21 -> 21, of which waited for: 8 -> 8; matrix products, arithmetic and copies ran while one was open for 2% -> 2% of each run, Pallas kernels for 40% -> 39%
where the time goes in v4:
time: 257 us
  waiting for transfers between devices  105 us (41%)
  Pallas kernels  104 us (40%)
  starting transfers between devices  24.4 us (9%)
  between operations  13.9 us (5%)
  local copies, waits for them, and re-layouts  6.87 us (3%)
  other arithmetic  2.73 us (1%)
    ppermute x18, waiting for transfers between devices, to(): return lax.ppermute(x, 'seq', [(i, i ^ r) for i in range(n)])  77 us
    reduce_scatter x1, waiting for transfers between devices, on_device(): lax.psum_scatter(after(gw, y_far[0], pair_0, pair_1), 'zero', scatter_dim...  27.7 us
    ppermute x18, starting transfers between devices, to(): return lax.ppermute(x, 'seq', [(i, i ^ r) for i in range(n)])  24.3 us
    pallas_call x4, Pallas kernels, project_back(): pl.pallas_call(functools.partial(project_back_kernel, n, m, order), out_s...  23.3 us
    pallas_call x4, Pallas kernels, project(): pl.pallas_call(project_kernel, grid=(cols // tile,), out_shape=[sds((out,...  18.7 us
    pallas_call x1, Pallas kernels, attend_back(): pl.pallas_call(functools.partial(bwd_kernel, len(got), nbr.shape[2], scal...  14.3 us
    pallas_call x1, Pallas kernels, attend(): pl.pallas_call(functools.partial(fwd_kernel, width // HD, nbr.shape[2], s...  10.5 us
    pallas_call x1, Pallas kernels, weight_grad(): pl.pallas_call(functools.partial(weight_kernel, n), grid=(cols // tile,),...  10.4 us
  transfers between devices with their start and end apart: 21, of which 8 were waited for; matrix products, arithmetic and copies ran while one was open for 2% of the time, Pallas kernels for 39%

profile of v4, /device:TPU:0, one launch (start us, length us, event | category | flops | bytes accessed | tf_op | source)
XLA Modules:
  0.0 256.6 jit_solution(8195775165438447405)
XLA Ops:
  7.2 3.4 %pack.1 = (bf16[3,256,640]{2,1,0:T(8,128)(2,1)}, bf16[3,256,640]{2,1,0:T(8,128)(2,1)}, bf16[3,256,640]{2,1,0:T(8,128)(2,1)}, bf16[80,2560]{1,0:T(8,128)(2,1)}, bf16[80,2560]{1,0:T(8,128)(2,1)}) custom-call(s32[1]{0:T(128)} %bitcast.1.me_ref, bf16[1,256,2560]{2,1,0:T(8,128)(2,1)} %rest_0_.3, bf16[1,256,2560]{2,1,0:T(8,128)(2,1)} %rest_1_.3, ...), custom_call_target="tpu_custom_call" | custom-call | flops 1024 | bytes 1024 | tf_op jit(solution)/shard_map/pack/pallas_call | solution.py:70
  10.7 3.0 %collective-permute-start = (bf16[3,256,640]{2,1,0:T(8,128)(2,1)}, bf16[3,256,640]{2,1,0:T(8,128)(2,1)}, u32[]{:S(2)}, u32[]{:S(2)}) collective-permute-start(bf16[3,256,640]{2,1,0:T(8,128)(2,1)} %get-tuple-element.42), channel_id=1, source_target_pairs={{0,8},{8,0},{16,24},{24,16},{1,9},{9,1},{17,25},{25,17},{2,10},{10... | collective-permute-start | bytes 2949128 | tf_op jit(solution)/shard_map/ppermute | solution.py:501
  13.7 1.5 collective-permute-start.1
  15.2 3.4 %dynamic-slice_bitcast_fusion = (bf16[256,2560]{1,0:T(8,128)(2,1)}, bf16[256,2560]{1,0:T(8,128)(2,1)}) fusion(bf16[1,256,5120]{2,1,0:T(8,128)(2,1)} %param.13, s32[]{:T(128)S(6)} %select_n.15, s32[]{:T(128)S(6)} %select_n.14), kind=kLoop, calls=%fused_computation | loop fusion | bytes 5242888 | tf_op jit(solution)/shard_map/dynamic_slice | solution.py:507
  18.7 1.9 collective-permute-start.6
  20.6 44.9 %collective-permute-done.6 = bf16[80,2560]{1,0:T(8,128)(2,1)S(1)} collective-permute-done((bf16[80,2560]{1,0:T(8,128)(2,1)S(1)}, bf16[80,2560]{1,0:T(8,128)(2,1)S(1)}, u32[]{:S(2)}, u32[]{:S(2)}) %collective-permute-start.6) | collective-permute-done | bytes 409632 | tf_op jit(solution)/shard_map/ppermute | solution.py:501
  66.4 1.8 collective-permute-start.4
  70.3 10.5 %attend.1 = (bf16[1024,640]{1,0:T(8,128)(2,1)}, bf16[1024,640]{1,0:T(8,128)(2,1)}, bf16[640,1024]{1,0:T(8,128)(2,1)}) custom-call(s32[1]{0:T(128)} %bitcast.1.me_ref, s32[1,8,4]{2,1,0:T(8,128)} %copy.12.nbr_ref, s32[1,8]{1,0:T(1,128)} %cnt_ref.3, bf16[1,256,2560]{2,1,0:T(8,128)(2,1)} %rest_0_.3, bf16[1,256,2560]{2,1,0:T(8,128)(2,1)} %rest_1_.3, ...), custom_call_target="tpu_custom_call" | custom-call | flops 1024 | bytes 1024 | tf_op jit(solution)/shard_map/attend/pallas_call | solution.py:221
  81.5 9.2 %project_own.1.own_ref = f32[1024,2560]{1,0:T(8,128)} custom-call(bf16[1024,640]{1,0:T(8,128)(2,1)} %get-tuple-element.47.a_ref, bf16[640,2560]{1,0:T(8,128)(2,1)} %all-gather.3.cloned.1.call-done.w_ref.refs_3_.refs_1_), custom_call_target="tpu_custom_call" | custom-call | flops 1024 | bytes 1024 | tf_op jit(solution)/shard_map/project_own/pallas_call | solution.py:331
  90.7 7.8 %collective-permute-done.4.refs_1_ = bf16[256,2560]{1,0:T(8,128)(2,1)} collective-permute-done((bf16[256,2560]{1,0:T(8,128)(2,1)}, bf16[256,2560]{1,0:T(8,128)(2,1)}, u32[]{:S(2)}, u32[]{:S(2)}) %collective-permute-start.4) | collective-permute-done | bytes 1310752 | tf_op jit(solution)/shard_map/ppermute | solution.py:501
  98.5 1.8 collective-permute-start.7
  100.2 7.4 %project_back.4.rest_6_ = bf16[768,640]{1,0:T(8,128)(2,1)} custom-call(bf16[256,2560]{1,0:T(8,128)(2,1)} %get-tuple-element.80.refs_0_, bf16[256,2560]{1,0:T(8,128)(2,1)} %collective-permute-done.4.refs_1_, bf16[256,2560]{1,0:T(8,128)(2,1)} %collective-permute-done.5.refs_2_, bf16[640,2560]{1,0:T(8,128)(2,1)} %all-gather.3.cloned.1.call-done.w_ref.refs_3_.refs_1_), custom_call_target="tpu_custom_call" | custom-call | flops 1024 | bytes 1024 | tf_op jit(solution)/shard_map/project_back/pallas_call | solution.py:409
  107.7 7.3 %project_back.5 = bf16[768,640]{1,0:T(8,128)(2,1)} custom-call(bf16[256,2560]{1,0:T(8,128)(2,1)} %get-tuple-element.80.refs_0_, bf16[256,2560]{1,0:T(8,128)(2,1)} %collective-permute-done.4.refs_1_, bf16[256,2560]{1,0:T(8,128)(2,1)} %collective-permute-done.5.refs_2_, bf16[640,2560]{1,0:T(8,128)(2,1)} %all-gather.5.cloned.1.call-done.refs_3_.w_ref.refs_1_), custom_call_target="tpu_custom_call" | custom-call | flops 1024 | bytes 1024 | tf_op jit(solution)/shard_map/project_back/pallas_call | solution.py:409
  115.0 7.9 %weight_own.1.done_ref = f32[640,2560]{1,0:T(8,128)} custom-call(bf16[640,1024]{1,0:T(8,128)(2,1)} %get-tuple-element.55.at, bf16[256,2560]{1,0:T(8,128)(2,1)} %get-tuple-element.80.refs_0_, bf16[256,2560]{1,0:T(8,128)(2,1)} %collective-permute-done.4.refs_1_, bf16[256,2560]{1,0:T(8,128)(2,1)} %collective-permute-done.5.refs_2_), custom_call_target="tpu_custom_call" | custom-call | flops 1024 | bytes 1024 | tf_op jit(solution)/shard_map/weight_own/pallas_call | solution.py:437
  123.0 1.8 collective-permute-done.3.b_ref
  124.8 3.6 %project.4 = bf16[512,1024]{1,0:T(8,128)(2,1)} custom-call(f32[1024,2560]{1,0:T(8,128)} %project_own.1.own_ref, bf16[1024,640]{1,0:T(8,128)(2,1)} %collective-permute-done.3.b_ref, bf16[640,2560]{1,0:T(8,128)(2,1)} %all-gather.5.cloned.1.call-done.refs_3_.w_ref.refs_1_), custom_call_target="tpu_custom_call" | custom-call | flops 1024 | bytes 1024 | tf_op jit(solution)/shard_map/project/pallas_call | solution.py:366
  131.3 4.3 %project_back.6 = bf16[256,640]{1,0:T(8,128)(2,1)} custom-call(bf16[256,2560]{1,0:T(8,128)(2,1)} %collective-permute-done.7.refs_0_.refs_3_, bf16[640,2560]{1,0:T(8,128)(2,1)} %all-gather.5.cloned.1.call-done.refs_3_.w_ref.refs_1_), custom_call_target="tpu_custom_call" | custom-call | flops 1024 | bytes 1024 | tf_op jit(solution)/shard_map/project_back/pallas_call | solution.py:409
  136.2 5.4 %project.5 = bf16[512,1536]{1,0:T(8,128)(2,1)} custom-call(f32[1024,2560]{1,0:T(8,128)} %project_own.1.own_ref, bf16[1024,640]{1,0:T(8,128)(2,1)} %collective-permute-done.3.b_ref, bf16[640,2560]{1,0:T(8,128)(2,1)} %all-gather.5.cloned.1.call-done.refs_3_.w_ref.refs_1_), custom_call_target="tpu_custom_call" | custom-call | flops 1024 | bytes 1024 | tf_op jit(solution)/shard_map/project/pallas_call | solution.py:366
  141.6 4.3 %project_back.7.rest_7_ = bf16[256,640]{1,0:T(8,128)(2,1)} custom-call(bf16[256,2560]{1,0:T(8,128)(2,1)} %collective-permute-done.7.refs_0_.refs_3_, bf16[640,2560]{1,0:T(8,128)(2,1)} %all-gather.3.cloned.1.call-done.w_ref.refs_3_.refs_1_), custom_call_target="tpu_custom_call" | custom-call | flops 1024 | bytes 1024 | tf_op jit(solution)/shard_map/project_back/pallas_call | solution.py:409
  145.8 10.4 %weight_grad.1 = bf16[8,2,80,2560]{3,2,1,0:T(8,128)(2,1)} custom-call(f32[640,2560]{1,0:T(8,128)} %weight_own.1.done_ref, bf16[640,1024]{1,0:T(8,128)(2,1)} %get-tuple-element.55.at, bf16[1024,640]{1,0:T(8,128)(2,1)} %collective-permute-done.3.b_ref, bf16[256,2560]{1,0:T(8,128)(2,1)} %get-tuple-element.80.refs_0_, ...), custom_call_target="tpu_custom_call" | custom-call | flops 1024 | bytes 1024 | tf_op jit(solution)/shard_map/weight_grad/pallas_call | solution.py:472
  156.2 2.4 collective-permute-done.13.rest_9_
  159.6 4.0 %project.6 = (bf16[256,1024]{1,0:T(8,128)(2,1)}, bf16[256,1024]{1,0:T(8,128)(2,1)}) custom-call(f32[1024,2560]{1,0:T(8,128)} %project_own.1.own_ref, bf16[1024,640]{1,0:T(8,128)(2,1)} %collective-permute-done.3.b_ref, bf16[640,2560]{1,0:T(8,128)(2,1)} %all-gather.5.cloned.1.call-done.refs_3_.w_ref.refs_1_, bf16[512,1024]{1,0:T(8,128)(2,1)} %collective-permute-done.8.rest_0_), custom_call_target="tpu_custom_call" | custom-call | flops 1024 | bytes 1024 | tf_op jit(solution)/shard_map/project/pallas_call | solution.py:366
  164.7 14.3 %attend_back.1 = (bf16[3,256,640]{2,1,0:T(8,128)(2,1)}, bf16[3,256,640]{2,1,0:T(8,128)(2,1)}, bf16[3,256,640]{2,1,0:T(8,128)(2,1)}, bf16[3,256,640]{2,1,0:T(8,128)(2,1)}) custom-call(s32[1]{0:T(128)} %bitcast.1.me_ref, s32[1,8,4]{2,1,0:T(8,128)} %copy.12.nbr_ref, s32[1,8]{1,0:T(1,128)} %cnt_ref.3, bf16[1,256,2560]{2,1,0:T(8,128)(2,1)} %rest_0_.3, ...), custom_call_target="tpu_custom_call" | custom-call | flops 1024 | bytes 1024 | tf_op jit(solution)/shard_map/attend_back/pallas_call | solution.py:302
  182.5 13.8 %collective-permute-done.10.rest_0_ = bf16[512,1536]{1,0:T(8,128)(2,1)} collective-permute-done((bf16[512,1536]{1,0:T(8,128)(2,1)}, bf16[512,1536]{1,0:T(8,128)(2,1)}, u32[]{:S(2)}, u32[]{:S(2)}) %collective-permute-start.10) | collective-permute-done | bytes 1572896 | tf_op jit(solution)/shard_map/ppermute | solution.py:501
  196.3 5.8 %project.7 = (bf16[256,1536]{1,0:T(8,128)(2,1)}, bf16[256,1536]{1,0:T(8,128)(2,1)}) custom-call(f32[1024,2560]{1,0:T(8,128)} %project_own.1.own_ref, bf16[1024,640]{1,0:T(8,128)(2,1)} %collective-permute-done.3.b_ref, bf16[640,2560]{1,0:T(8,128)(2,1)} %all-gather.5.cloned.1.call-done.refs_3_.w_ref.refs_1_, bf16[512,1536]{1,0:T(8,128)(2,1)} %collective-permute-done.10.rest_0_), custom_call_target="tpu_custom_call" | custom-call | flops 1024 | bytes 1024 | tf_op jit(solution)/shard_map/project/pallas_call | solution.py:366
  203.6 27.7 %reduce-scatter.2.cloned.1.call-done = bf16[160,2560]{1,0:T(8,128)(2,1)} async-done(((bf16[1280,2560]{1,0:T(8,128)(2,1)}), bf16[160,2560]{1,0:T(8,128)(2,1)}) %reduce-scatter.2.cloned.1.call-update) | async-done | bytes 819216 | tf_op jit(solution)/shard_map/reduce_scatter | solution.py:562
  231.3 2.1 fusion.1
  234.9 3.5 %unpack.1 = (bf16[1,256,2560]{2,1,0:T(8,128)(2,1)}, bf16[1,256,2560]{2,1,0:T(8,128)(2,1)}, bf16[1,256,2560]{2,1,0:T(8,128)(2,1)}) custom-call(s32[1]{0:T(128)} %bitcast.1.me_ref, bf16[3,256,640]{2,1,0:T(8,128)(2,1)} %get-tuple-element.70.rest_0_, bf16[3,256,640]{2,1,0:T(8,128)(2,1)} %collective-permute-done.14.rest_1_, ...), custom_call_target="tpu_custom_call" | custom-call | flops 1024 | bytes 1024 | tf_op jit(solution)/shard_map/unpack/pallas_call | solution.py:113
  238.4 3.6 %collective-permute-done.11.rest_3_ = bf16[256,1536]{1,0:T(8,128)(2,1)} collective-permute-done((bf16[256,1536]{1,0:T(8,128)(2,1)}, bf16[256,1536]{1,0:T(8,128)(2,1)}, u32[]{:S(2)}, u32[]{:S(2)}) %collective-permute-start.11) | collective-permute-done | bytes 786464 | tf_op jit(solution)/shard_map/ppermute | solution.py:501
  242.0 2.7 %join.1 = bf16[1,256,5120]{2,1,0:T(8,128)(2,1)} custom-call(s32[1]{0:T(128)} %bitcast.low_ref, bf16[256,1024]{1,0:T(8,128)(2,1)} %get-tuple-element.64.rest_0_, bf16[256,1536]{1,0:T(8,128)(2,1)} %get-tuple-element.67.rest_1_, bf16[256,1024]{1,0:T(8,128)(2,1)} %collective-permute-done.9.rest_2_, bf16[256,1536]{1,0:T(8,128)(2,1)} %collective-permute-done.11.rest_3_), custom_call_target="tpu_custom_call" | custom-call | flops 1024 | bytes 1024 | tf_op jit(solution)/shard_map/join/pallas_call | solution.py:144
  244.7 2.6 %collective-permute-done.17 = bf16[80,2560]{1,0:T(8,128)(2,1)} collective-permute-done((bf16[80,2560]{1,0:T(8,128)(2,1)}, bf16[80,2560]{1,0:T(8,128)(2,1)}, u32[]{:S(2)}, u32[]{:S(2)}) %collective-permute-start.17) | collective-permute-done | bytes 409632 | tf_op jit(solution)/shard_map/ppermute | solution.py:501
  247.3 2.7 %fusion = f32[80,5120]{1,0:T(8,128)} fusion(bf16[80,2560]{1,0:T(8,128)(2,1)} %collective-permute-done.17, bf16[80,2560]{1,0:T(8,128)(2,1)} %get-tuple-element.81, pred[]{:T(512)S(6)} %eq.3), kind=kLoop, calls=%fused_computation.3 | loop fusion | flops 4096000 | bytes 2457601 | tf_op jit(solution)/shard_map/convert_element_type | solution.py:570
  (39 shorter events, 15.9 us)
Async XLA Ops:
  7.2 58.4 %all-gather.3.cloned.1.call-start = ((), (), s32[]{:S(2)}) async-start(), calls=%async_computation.1 | async-start | bytes 3686400 | tf_op jit(solution)/shard_map/all_gather | solution.py:517
  10.6 97.0 %all-gather.5.cloned.1.call-start = ((), (), s32[]{:S(2)}) async-start(), calls=%async_computation.2 | async-start | bytes 3686400 | tf_op jit(solution)/shard_map/all_gather | solution.py:522
  10.7 54.9 %collective-permute-start = (bf16[3,256,640]{2,1,0:T(8,128)(2,1)}, bf16[3,256,640]{2,1,0:T(8,128)(2,1)}, u32[]{:S(2)}, u32[]{:S(2)}) collective-permute-start(bf16[3,256,640]{2,1,0:T(8,128)(2,1)} %get-tuple-element.42), channel_id=1, source_target_pairs={{0,8},{8,0},{16,24},{24,16},{1,9},{9,1},{17,25},{25,17},{2,10},{10... | collective-permute-start | bytes 2949128 | tf_op jit(solution)/shard_map/ppermute | solution.py:501
  13.7 51.9 %collective-permute-start.1 = (bf16[3,256,640]{2,1,0:T(8,128)(2,1)}, bf16[3,256,640]{2,1,0:T(8,128)(2,1)}, u32[]{:S(2)}, u32[]{:S(2)}) collective-permute-start(bf16[3,256,640]{2,1,0:T(8,128)(2,1)} %get-tuple-element.43), channel_id=1, source_target_pairs={{0,16},{8,24},{16,0},{24,8},{1,17},{9,25},{17,1},{25,9},{2,18},{10... | collective-permute-start | bytes 2949128 | tf_op jit(solution)/shard_map/ppermute | solution.py:501
  15.2 50.3 %collective-permute-start.2 = (bf16[3,256,640]{2,1,0:T(8,128)(2,1)}, bf16[3,256,640]{2,1,0:T(8,128)(2,1)}, u32[]{:S(2)}, u32[]{:S(2)}) collective-permute-start(bf16[3,256,640]{2,1,0:T(8,128)(2,1)} %get-tuple-element.44), channel_id=1, source_target_pairs={{0,24},{8,16},{16,8},{24,0},{1,25},{9,17},{17,9},{25,1},{2,26},{10... | collective-permute-start | bytes 2949128 | tf_op jit(solution)/shard_map/ppermute | solution.py:501
  15.2 3.4 %copy-start.2 = (bf16[80,2560]{1,0:T(8,128)(2,1)S(1)}, bf16[80,2560]{1,0:T(8,128)(2,1)}, u32[]{:S(2)}) copy-start(bf16[80,2560]{1,0:T(8,128)(2,1)} %get-tuple-element.53) | copy-start | bytes 1228804
  15.2 54.4 %copy-start.1 = (s32[1,8,4]{1,2,0:T(4,128)S(1)}, s32[1,8,4]{1,2,0:T(4,128)}, u32[]{:S(2)}) copy-start(s32[1,8,4]{1,2,0:T(4,128)} %param.10) | copy-start | bytes 388
  18.7 46.9 %collective-permute-start.6 = (bf16[80,2560]{1,0:T(8,128)(2,1)S(1)}, bf16[80,2560]{1,0:T(8,128)(2,1)S(1)}, u32[]{:S(2)}, u32[]{:S(2)}) collective-permute-start(bf16[80,2560]{1,0:T(8,128)(2,1)S(1)} %copy-done.2), channel_id=1, source_target_pairs={{0,8},{8,0},{16,24},{24,16},{1,9},{9,1},{17,25},{25,17},{2,10},{10... | collective-permute-start | bytes 1228808 | tf_op jit(solution)/shard_map/ppermute | solution.py:501
  65.5 0.8 copy-start
  66.3 165.0 %reduce-scatter.2.cloned.1.call-start = ((), (), s32[]{:S(2)}) async-start(), calls=%async_computation.3 | async-start | bytes 7372800 | tf_op jit(solution)/shard_map/reduce_scatter | solution.py:562
  66.4 32.1 %collective-permute-start.4 = (bf16[256,2560]{1,0:T(8,128)(2,1)}, bf16[256,2560]{1,0:T(8,128)(2,1)}, u32[]{:S(2)}, u32[]{:S(2)}) collective-permute-start(bf16[256,2560]{1,0:T(8,128)(2,1)} %get-tuple-element.79), channel_id=1, source_target_pairs={{0,8},{8,0},{16,24},{24,16},{1,9},{9,1},{17,25},{25,17},{2,10},{10... | collective-permute-start | bytes 3932168 | tf_op jit(solution)/shard_map/ppermute | solution.py:501
  68.2 32.1 %collective-permute-start.5 = (bf16[256,2560]{1,0:T(8,128)(2,1)}, bf16[256,2560]{1,0:T(8,128)(2,1)}, u32[]{:S(2)}, u32[]{:S(2)}) collective-permute-start(bf16[256,2560]{1,0:T(8,128)(2,1)} %get-tuple-element.80.refs_0_), channel_id=1, source_target_pairs={{0,16},{8,24},{16,0},{24,8},{1,17},{9,25},{17,1},{25,9},{2,18},{10... | collective-permute-start | bytes 3932168 | tf_op jit(solution)/shard_map/ppermute | solution.py:501
  80.9 43.9 %collective-permute-start.3 = (bf16[1024,640]{1,0:T(8,128)(2,1)}, bf16[1024,640]{1,0:T(8,128)(2,1)}, u32[]{:S(2)}, u32[]{:S(2)}) collective-permute-start(bf16[1024,640]{1,0:T(8,128)(2,1)} %get-tuple-element.46), channel_id=1, source_target_pairs={{0,8},{8,0},{16,24},{24,16},{1,9},{9,1},{17,25},{25,17},{2,10},{10... | collective-permute-start | bytes 3932168 | tf_op jit(solution)/shard_map/ppermute | solution.py:501
  98.5 32.8 %collective-permute-start.7 = (bf16[256,2560]{1,0:T(8,128)(2,1)}, bf16[256,2560]{1,0:T(8,128)(2,1)}, u32[]{:S(2)}, u32[]{:S(2)}) collective-permute-start(bf16[256,2560]{1,0:T(8,128)(2,1)} %collective-permute-done.4.refs_1_), channel_id=1, source_target_pairs={{0,16},{8,24},{16,0},{24,8},{1,17},{9,25},{17,1},{25,9},{2,18},{10... | collective-permute-start | bytes 3932168 | tf_op jit(solution)/shard_map/ppermute | solution.py:501
  128.4 30.2 %collective-permute-start.8 = (bf16[512,1024]{1,0:T(8,128)(2,1)}, bf16[512,1024]{1,0:T(8,128)(2,1)}, u32[]{:S(2)}, u32[]{:S(2)}) collective-permute-start(bf16[512,1024]{1,0:T(8,128)(2,1)} %project.4), channel_id=1, source_target_pairs={{0,16},{8,24},{16,0},{24,8},{1,17},{9,25},{17,1},{25,9},{2,18},{10... | collective-permute-start | bytes 3145736 | tf_op jit(solution)/shard_map/ppermute | solution.py:501
  129.8 28.8 %collective-permute-start.12 = (bf16[768,640]{1,0:T(8,128)(2,1)}, bf16[768,640]{1,0:T(8,128)(2,1)}, u32[]{:S(2)}, u32[]{:S(2)}) collective-permute-start(bf16[768,640]{1,0:T(8,128)(2,1)} %project_back.5), channel_id=1, source_target_pairs={{0,8},{8,0},{16,24},{24,16},{1,9},{9,1},{17,25},{25,17},{2,10},{10... | collective-permute-start | bytes 2949128 | tf_op jit(solution)/shard_map/ppermute | solution.py:501
  135.6 23.0 %collective-permute-start.13 = (bf16[256,640]{1,0:T(8,128)(2,1)}, bf16[256,640]{1,0:T(8,128)(2,1)}, u32[]{:S(2)}, u32[]{:S(2)}) collective-permute-start(bf16[256,640]{1,0:T(8,128)(2,1)} %project_back.6), channel_id=1, source_target_pairs={{0,8},{8,0},{16,24},{24,16},{1,9},{9,1},{17,25},{25,17},{2,10},{10... | collective-permute-start | bytes 983048 | tf_op jit(solution)/shard_map/ppermute | solution.py:501
  158.6 37.7 %collective-permute-start.10 = (bf16[512,1536]{1,0:T(8,128)(2,1)}, bf16[512,1536]{1,0:T(8,128)(2,1)}, u32[]{:S(2)}, u32[]{:S(2)}) collective-permute-start(bf16[512,1536]{1,0:T(8,128)(2,1)} %project.5), channel_id=1, source_target_pairs={{0,16},{8,24},{16,0},{24,8},{1,17},{9,25},{17,1},{25,9},{2,18},{10... | collective-permute-start | bytes 4718600 | tf_op jit(solution)/shard_map/ppermute | solution.py:501
  163.5 19.0 %collective-permute-start.9 = (bf16[256,1024]{1,0:T(8,128)(2,1)}, bf16[256,1024]{1,0:T(8,128)(2,1)}, u32[]{:S(2)}, u32[]{:S(2)}) collective-permute-start(bf16[256,1024]{1,0:T(8,128)(2,1)} %get-tuple-element.65), channel_id=1, source_target_pairs={{0,8},{8,0},{16,24},{24,16},{1,9},{9,1},{17,25},{25,17},{2,10},{10... | collective-permute-start | bytes 1572872 | tf_op jit(solution)/shard_map/ppermute | solution.py:501
  179.0 55.9 %collective-permute-start.14 = (bf16[3,256,640]{2,1,0:T(8,128)(2,1)}, bf16[3,256,640]{2,1,0:T(8,128)(2,1)}, u32[]{:S(2)}, u32[]{:S(2)}) collective-permute-start(bf16[3,256,640]{2,1,0:T(8,128)(2,1)} %get-tuple-element.71), channel_id=1, source_target_pairs={{0,8},{8,0},{16,24},{24,16},{1,9},{9,1},{17,25},{25,17},{2,10},{10... | collective-permute-start | bytes 2949128 | tf_op jit(solution)/shard_map/ppermute | solution.py:501
  180.2 54.7 %collective-permute-start.15 = (bf16[3,256,640]{2,1,0:T(8,128)(2,1)}, bf16[3,256,640]{2,1,0:T(8,128)(2,1)}, u32[]{:S(2)}, u32[]{:S(2)}) collective-permute-start(bf16[3,256,640]{2,1,0:T(8,128)(2,1)} %get-tuple-element.72), channel_id=1, source_target_pairs={{0,16},{8,24},{16,0},{24,8},{1,17},{9,25},{17,1},{25,9},{2,18},{10... | collective-permute-start | bytes 2949128 | tf_op jit(solution)/shard_map/ppermute | solution.py:501
  181.6 53.3 %collective-permute-start.16 = (bf16[3,256,640]{2,1,0:T(8,128)(2,1)}, bf16[3,256,640]{2,1,0:T(8,128)(2,1)}, u32[]{:S(2)}, u32[]{:S(2)}) collective-permute-start(bf16[3,256,640]{2,1,0:T(8,128)(2,1)} %get-tuple-element.73), channel_id=1, source_target_pairs={{0,24},{8,16},{16,8},{24,0},{1,25},{9,17},{17,9},{25,1},{2,26},{10... | collective-permute-start | bytes 2949128 | tf_op jit(solution)/shard_map/ppermute | solution.py:501
  202.1 39.9 %collective-permute-start.11 = (bf16[256,1536]{1,0:T(8,128)(2,1)}, bf16[256,1536]{1,0:T(8,128)(2,1)}, u32[]{:S(2)}, u32[]{:S(2)}) collective-permute-start(bf16[256,1536]{1,0:T(8,128)(2,1)} %get-tuple-element.68), channel_id=1, source_target_pairs={{0,8},{8,0},{16,24},{24,16},{1,9},{9,1},{17,25},{25,17},{2,10},{10... | collective-permute-start | bytes 2359304 | tf_op jit(solution)/shard_map/ppermute | solution.py:501
  233.4 13.9 %collective-permute-start.17 = (bf16[80,2560]{1,0:T(8,128)(2,1)}, bf16[80,2560]{1,0:T(8,128)(2,1)}, u32[]{:S(2)}, u32[]{:S(2)}) collective-permute-start(bf16[80,2560]{1,0:T(8,128)(2,1)} %get-tuple-element.82), channel_id=1, source_target_pairs={{0,8},{8,0},{16,24},{24,16},{1,9},{9,1},{17,25},{25,17},{2,10},{10... | collective-permute-start | bytes 1228808 | tf_op jit(solution)/shard_map/ppermute | solution.py:501
Sparse Core Ops, SparseCore 0:
  10.8 42.0 all-gather.2
  66.4 40.8 all-gather.4
  158.7 72.5 reduce-scatter.1
